TPU v7x, 32 devices: a whole 2x2x4 slice. The times are simulated.
32 devices in a mesh: slot: 8 (over z, y), pb: 4 (over x, core).
Axes of the slice: x: 2, y: 2, z: 4, core: 2. Of those that a mesh axis runs over, the one named last changes fastest.
Arguments:
- enc_input: bfloat16 [4, 8, 384, 1024], P('pb', 'slot'), may hold values from -6 to 6
- dec_input: bfloat16 [4, 8, 128, 1024], P('pb', 'slot'), may hold values from -6 to 6
- doc_scores: float32 [4, 8], P('pb', 'slot'), may hold values from -5 to 5
- owner: int32 [4, 8], P('pb', 'slot'), may hold values from 0 to 1, as said below
- targets: int32 [4, 2, 128], P('pb'), may hold values from 0 to 49151
- enc_attn: bfloat16 [4, 1024, 1024], P(None, 'pb'), may hold values from -0.1875 to 0.1875
- enc_up: bfloat16 [1024, 4096], P('pb'), may hold values from -0.1875 to 0.1875
- enc_down: bfloat16 [4096, 1024], P('pb'), may hold values from -0.09375 to 0.09375
- enc_up_bias: bfloat16 [4096], P('pb'), may hold values from -1.5 to 1.5
- enc_bias: bfloat16 [6, 1024], P(None, 'pb'), may hold values from -1.5 to 1.5
- enc_gain: bfloat16 [2, 1024], P(None, 'pb'), may hold values from 0.5 to 1.5
- dec_self: bfloat16 [4, 1024, 1024], P(None, 'pb'), may hold values from -0.1875 to 0.1875
- dec_cross: bfloat16 [4, 1024, 1024], P(None, 'pb'), may hold values from -0.1875 to 0.1875
- dec_up: bfloat16 [1024, 4096], P('pb'), may hold values from -0.1875 to 0.1875
- dec_down: bfloat16 [4096, 1024], P('pb'), may hold values from -0.09375 to 0.09375
- dec_up_bias: bfloat16 [4096], P('pb'), may hold values from -1.5 to 1.5
- dec_bias: bfloat16 [10, 1024], P(None, 'pb'), may hold values from -1.5 to 1.5
- dec_gain: bfloat16 [3, 1024], P(None, 'pb'), may hold values from 0.5 to 1.5
- embed: bfloat16 [49152, 1024], P(('slot', 'pb')), may hold values from -0.375 to 0.375
Outputs:
- loss: float32 [4], P('pb')
- enc_input_grad: float32 [4, 8, 384, 1024], P('pb', 'slot')
- dec_input_grad: float32 [4, 8, 128, 1024], P('pb', 'slot')
- doc_scores_grad: float32 [4, 8], P('pb', 'slot')
- enc_attn_grad: float32 [4, 1024, 1024], P(None, 'pb')
- enc_up_grad: float32 [1024, 4096], P('pb')
- enc_down_grad: float32 [4096, 1024], P('pb')
- enc_up_bias_grad: float32 [4096], P('pb')
- enc_bias_grad: float32 [6, 1024], P(None, 'pb')
- enc_gain_grad: float32 [2, 1024], P(None, 'pb')
- dec_self_grad: float32 [4, 1024, 1024], P(None, 'pb')
- dec_cross_grad: float32 [4, 1024, 1024], P(None, 'pb')
- dec_up_grad: float32 [1024, 4096], P('pb')
- dec_down_grad: float32 [4096, 1024], P('pb')
- dec_up_bias_grad: float32 [4096], P('pb')
- dec_bias_grad: float32 [10, 1024], P(None, 'pb')
- dec_gain_grad: float32 [3, 1024], P(None, 'pb')
- embed_grad: float32 [49152, 1024], P(('slot', 'pb'))
Inputs may be any that keep to these rules, and one draw needn't show every extreme that they name: `owner`: in each group every question is served by between 2 and 6 slots, and one question by exactly 6; the slots of a question may lie anywhere along the group.
All inputs are finite; a program needn't handle non-finite values.
Results may differ from a plain program's by a relative error of at most 0.019.
Values may be sent and summed in bfloat16 or wider, within the bound.
A program may use at most 576 MiB of HBM per device.

v0:
```python
import jax
import jax.numpy as jnp
from jax import lax
from jax.sharding import PartitionSpec as P

D = 1024
HEADS = 16
HEAD_DIM = 64
SRC_LEN = 384
TGT_LEN = 128


BIG_NEGATIVE = -1e30
MASK_FILL = -1000000000.0


def shortened(x):
    return jax.tree.map(lambda a: a.astype(jnp.bfloat16) if a.dtype == jnp.float32 else a, x)


def matmul(left, right):
    return jnp.dot(left, right, preferred_element_type=jnp.float32)


def matmul_nt(left, right):
    return lax.dot_general(
        left, right, (((1,), (1,)), ((), ())), preferred_element_type=jnp.float32
    )


def matmul_tn(left, right):
    return lax.dot_general(
        left, right, (((0,), (0,)), ((), ())), preferred_element_type=jnp.float32
    )


def to_low(value):
    return value.astype(jnp.bfloat16)


def norm_forward(total, gain, shift):
    centered = total - jnp.mean(total, axis=-1, keepdims=True)
    inverse = lax.rsqrt(jnp.mean(centered * centered, axis=-1, keepdims=True) + 1e-05)
    normed = centered * inverse
    return (normed * gain + shift, (normed, inverse))


def norm_backward(upstream, saved, gain):
    normed, inverse = saved
    scaled = upstream * gain
    inner = (
        scaled
        - jnp.mean(scaled, axis=-1, keepdims=True)
        - normed * jnp.mean(scaled * normed, axis=-1, keepdims=True)
    )
    return (inverse * inner, jnp.sum(upstream * normed, axis=0), jnp.sum(upstream, axis=0))


def attend_forward(query_low, memory_low, matrices, bias_query, bias_value, bias_out, causal):
    rows = query_low.shape[0]
    columns = memory_low.shape[0]
    queries = to_low(matmul(query_low, matrices[0]) + bias_query).reshape(rows, HEADS, HEAD_DIM)
    keys = to_low(matmul(memory_low, matrices[1])).reshape(columns, HEADS, HEAD_DIM)
    values = to_low(matmul(memory_low, matrices[2]) + bias_value).reshape(columns, HEADS, HEAD_DIM)
    scores = jnp.einsum(
        "qhd,khd->hqk", queries, keys, preferred_element_type=jnp.float32
    ) * HEAD_DIM ** (-0.5)
    if causal:
        visible = jnp.arange(rows)[:, None] >= jnp.arange(columns)[None, :]
        scores = jnp.where(visible[None], scores, MASK_FILL)
    shifted = jnp.exp(scores - jnp.max(scores, axis=-1, keepdims=True))
    probs = shifted / jnp.sum(shifted, axis=-1, keepdims=True)
    context = to_low(
        jnp.einsum(
            "hqk,khd->qhd", to_low(probs), values, preferred_element_type=jnp.float32
        ).reshape(rows, D)
    )
    output = matmul(context, matrices[3]) + bias_out
    return (output, (queries, keys, values, probs, context))


def attend_backward(upstream, query_low, memory_low, matrices, saved):
    queries, keys, values, probs, context = saved
    rows = query_low.shape[0]
    columns = memory_low.shape[0]
    scale = HEAD_DIM ** (-0.5)
    upstream_low = to_low(upstream)
    grad_out = matmul_tn(context, upstream_low)
    grad_context = to_low(matmul_nt(upstream_low, matrices[3])).reshape(rows, HEADS, HEAD_DIM)
    grad_probs = jnp.einsum(
        "qhd,khd->hqk", grad_context, values, preferred_element_type=jnp.float32
    )
    grad_values = jnp.einsum(
        "hqk,qhd->khd", to_low(probs), grad_context, preferred_element_type=jnp.float32
    ).reshape(columns, D)
    grad_scores = to_low(probs * (grad_probs - jnp.sum(grad_probs * probs, axis=-1, keepdims=True)))
    grad_queries = (
        jnp.einsum("hqk,khd->qhd", grad_scores, keys, preferred_element_type=jnp.float32) * scale
    ).reshape(rows, D)
    grad_keys = (
        jnp.einsum("hqk,qhd->khd", grad_scores, queries, preferred_element_type=jnp.float32) * scale
    ).reshape(columns, D)
    queries_low = to_low(grad_queries)
    keys_low = to_low(grad_keys)
    values_low = to_low(grad_values)
    grad_query_input = matmul_nt(queries_low, matrices[0])
    grad_memory_input = matmul_nt(keys_low, matrices[1]) + matmul_nt(values_low, matrices[2])
    grad_matrices = jnp.stack(
        [
            matmul_tn(query_low, queries_low),
            matmul_tn(memory_low, keys_low),
            matmul_tn(memory_low, values_low),
            grad_out,
        ]
    )
    bias_grads = (
        jnp.sum(grad_queries, axis=0),
        jnp.sum(grad_values, axis=0),
        jnp.sum(upstream, axis=0),
    )
    return (grad_query_input, grad_memory_input, grad_matrices, bias_grads)


def gelu_exact(value):
    return jax.nn.gelu(value, approximate=False)


def feed_forward(input_low, weight_up, bias_up, weight_down, bias_down):
    before = matmul(input_low, weight_up) + bias_up
    hidden_low = to_low(gelu_exact(before))
    return (matmul(hidden_low, weight_down) + bias_down, (before, hidden_low))


def feed_backward(upstream, input_low, weight_up, weight_down, saved):
    before, hidden_low = saved
    upstream_low = to_low(upstream)
    grad_down = matmul_tn(hidden_low, upstream_low)
    grad_hidden = matmul_nt(upstream_low, weight_down)
    unused, pullback = jax.vjp(gelu_exact, before)
    grad_before = pullback(grad_hidden)[0]
    before_low = to_low(grad_before)
    return (
        matmul_nt(before_low, weight_up),
        matmul_tn(input_low, before_low),
        grad_down,
        jnp.sum(grad_before, axis=0),
        jnp.sum(upstream, axis=0),
    )


def local(
    enc_input,
    dec_input,
    doc_scores,
    owner,
    targets,
    enc_attn,
    enc_up,
    enc_down,
    enc_up_bias,
    enc_bias,
    enc_gain,
    dec_self,
    dec_cross,
    dec_up,
    dec_down,
    dec_up_bias,
    dec_bias,
    dec_gain,
    embed,
):
    gathered = (
        lax.all_gather(enc_attn, "pb", axis=1, tiled=True),
        lax.all_gather(enc_up, "pb", axis=0, tiled=True),
        lax.all_gather(enc_down, "pb", axis=0, tiled=True),
        lax.all_gather(enc_up_bias, "pb", axis=0, tiled=True),
        lax.all_gather(enc_bias, "pb", axis=1, tiled=True),
        lax.all_gather(enc_gain, "pb", axis=1, tiled=True),
        lax.all_gather(dec_self, "pb", axis=1, tiled=True),
        lax.all_gather(dec_cross, "pb", axis=1, tiled=True),
        lax.all_gather(dec_up, "pb", axis=0, tiled=True),
        lax.all_gather(dec_down, "pb", axis=0, tiled=True),
        lax.all_gather(dec_up_bias, "pb", axis=0, tiled=True),
        lax.all_gather(dec_bias, "pb", axis=1, tiled=True),
        lax.all_gather(dec_gain, "pb", axis=1, tiled=True),
    )
    encoder_attn, encoder_up, encoder_down = (gathered[0], gathered[1], gathered[2])
    encoder_upbias = gathered[3].astype(jnp.float32)
    encoder_bias = gathered[4].astype(jnp.float32)
    encoder_gain = gathered[5].astype(jnp.float32)
    decoder_self, decoder_cross, decoder_up, decoder_down = (
        gathered[6],
        gathered[7],
        gathered[8],
        gathered[9],
    )
    decoder_upbias = gathered[10].astype(jnp.float32)
    decoder_bias = gathered[11].astype(jnp.float32)
    decoder_gain = gathered[12].astype(jnp.float32)
    passage_low = enc_input[0, 0]
    passage = passage_low.astype(jnp.float32)
    attn_out, enc_saved = attend_forward(
        passage_low,
        passage_low,
        encoder_attn,
        encoder_bias[0],
        encoder_bias[1],
        encoder_bias[2],
        False,
    )
    enc_first, enc_norm_one = norm_forward(passage + attn_out, encoder_gain[0], encoder_bias[3])
    enc_first_low = to_low(enc_first)
    ffn_out, enc_ffn_saved = feed_forward(
        enc_first_low, encoder_up, encoder_upbias, encoder_down, encoder_bias[4]
    )
    encoded, enc_norm_two = norm_forward(enc_first + ffn_out, encoder_gain[1], encoder_bias[5])
    memory_low = to_low(encoded)
    question_low = dec_input[0, 0]
    question = question_low.astype(jnp.float32)
    self_out, self_saved = attend_forward(
        question_low,
        question_low,
        decoder_self,
        decoder_bias[0],
        decoder_bias[1],
        decoder_bias[2],
        True,
    )
    dec_first, dec_norm_one = norm_forward(question + self_out, decoder_gain[0], decoder_bias[3])
    dec_first_low = to_low(dec_first)
    cross_out, cross_saved = attend_forward(
        dec_first_low,
        memory_low,
        decoder_cross,
        decoder_bias[4],
        decoder_bias[5],
        decoder_bias[6],
        False,
    )
    dec_second, dec_norm_two = norm_forward(dec_first + cross_out, decoder_gain[1], decoder_bias[7])
    dec_second_low = to_low(dec_second)
    dec_ffn_out, dec_ffn_saved = feed_forward(
        dec_second_low, decoder_up, decoder_upbias, decoder_down, decoder_bias[8]
    )
    state, dec_norm_three = norm_forward(dec_second + dec_ffn_out, decoder_gain[2], decoder_bias[9])
    state_low = to_low(state)
    serving = jnp.arange(targets.shape[1]) == owner[0, 0]
    target_ids = jnp.sum(jnp.where(serving[:, None], targets[0], 0), axis=0)
    piece = lax.all_gather(embed, ("slot", "pb"), axis=0, tiled=True)
    running_max = jnp.full((TGT_LEN,), BIG_NEGATIVE, jnp.float32)
    logits = matmul_nt(state_low, piece)
    block_max = jnp.maximum(running_max, jnp.max(logits, axis=1))
    running_sum = jnp.sum(jnp.exp(logits - block_max[:, None]), axis=1)
    vocab_ids = jnp.arange(piece.shape[0])
    running_pick = jnp.sum(
        jnp.where(vocab_ids[None, :] == target_ids[:, None], logits, 0.0), axis=1
    )
    log_total = block_max + jnp.log(running_sum)
    own_score = doc_scores[0, 0]
    picked = running_pick - log_total
    score_terms = jnp.where(serving, own_score, BIG_NEGATIVE)
    token_terms = jnp.where(serving[:, None], own_score + picked[None, :], BIG_NEGATIVE)
    score_top, token_top = lax.pmax((score_terms, token_terms), "slot")
    score_sum, token_sum = lax.psum(
        (jnp.exp(score_terms - score_top), jnp.exp(token_terms - token_top)), "slot"
    )
    score_norm = score_top + jnp.log(score_sum)
    token_mix = token_top + jnp.log(token_sum)
    group_tokens = targets.shape[1] * TGT_LEN
    tokens_total = lax.axis_size("pb") * group_tokens
    group_loss = -jnp.sum(token_mix - score_norm[:, None])
    loss = (group_loss / group_tokens).reshape(1)
    own_mix = jnp.sum(jnp.where(serving[:, None], token_mix, 0.0), axis=0)
    own_norm = jnp.sum(jnp.where(serving, score_norm, 0.0))
    posterior = jnp.exp(own_score + picked - own_mix)
    prior = jnp.exp(own_score - own_norm)
    token_grad = -posterior / tokens_total
    score_grad = (-jnp.sum(posterior - prior) / tokens_total).reshape(1, 1)
    piece = lax.all_gather(embed, ("slot", "pb"), axis=0, tiled=True)
    logits = matmul_nt(state_low, piece)
    vocab_ids = jnp.arange(piece.shape[0])
    probs = jnp.exp(logits - log_total[:, None])
    onehot = jnp.where(vocab_ids[None, :] == target_ids[:, None], 1.0, 0.0)
    delta = to_low(token_grad[:, None] * (onehot - probs))
    grad_state_sum = matmul(delta, piece)
    embed_grad = lax.psum_scatter(
        matmul_tn(delta, state_low), ("slot", "pb"), scatter_dimension=0, tiled=True
    )
    grad_third, gain_third, shift_third = norm_backward(
        grad_state_sum, dec_norm_three, decoder_gain[2]
    )
    dec_ffn_input, dec_up_grad, dec_down_grad, dec_upbias_grad, dec_downbias_grad = feed_backward(
        grad_third, dec_second_low, decoder_up, decoder_down, dec_ffn_saved
    )
    grad_second, gain_second, shift_second = norm_backward(
        grad_third + dec_ffn_input, dec_norm_two, decoder_gain[1]
    )
    cross_query, grad_memory, dec_cross_grad, cross_biases = attend_backward(
        grad_second, dec_first_low, memory_low, decoder_cross, cross_saved
    )
    grad_first, gain_first, shift_first = norm_backward(
        grad_second + cross_query, dec_norm_one, decoder_gain[0]
    )
    self_query, self_memory, dec_self_grad, self_biases = attend_backward(
        grad_first, question_low, question_low, decoder_self, self_saved
    )
    question_grad = grad_first + self_query + self_memory
    enc_grad_two, enc_gain_two, enc_shift_two = norm_backward(
        grad_memory, enc_norm_two, encoder_gain[1]
    )
    enc_ffn_input, enc_up_grad, enc_down_grad, enc_upbias_grad, enc_downbias_grad = feed_backward(
        enc_grad_two, enc_first_low, encoder_up, encoder_down, enc_ffn_saved
    )
    enc_grad_one, enc_gain_one, enc_shift_one = norm_backward(
        enc_grad_two + enc_ffn_input, enc_norm_one, encoder_gain[0]
    )
    enc_query, enc_memory, enc_attn_grad, enc_biases = attend_backward(
        enc_grad_one, passage_low, passage_low, encoder_attn, enc_saved
    )
    passage_grad = enc_grad_one + enc_query + enc_memory
    enc_bias_grad = jnp.stack(
        [
            enc_biases[0],
            enc_biases[1],
            enc_biases[2],
            enc_shift_one,
            enc_downbias_grad,
            enc_shift_two,
        ]
    )
    enc_gain_grad = jnp.stack([enc_gain_one, enc_gain_two])
    dec_bias_grad = jnp.stack(
        [
            self_biases[0],
            self_biases[1],
            self_biases[2],
            shift_first,
            cross_biases[0],
            cross_biases[1],
            cross_biases[2],
            shift_second,
            dec_downbias_grad,
            shift_third,
        ]
    )
    dec_gain_grad = jnp.stack([gain_first, gain_second, gain_third])
    shares = (
        lax.psum_scatter(
            enc_attn_grad.astype(jnp.bfloat16), "pb", scatter_dimension=1, tiled=True
        ).astype(jnp.float32),
        lax.psum_scatter(
            enc_up_grad.astype(jnp.bfloat16), "pb", scatter_dimension=0, tiled=True
        ).astype(jnp.float32),
        lax.psum_scatter(
            enc_down_grad.astype(jnp.bfloat16), "pb", scatter_dimension=0, tiled=True
        ).astype(jnp.float32),
        lax.psum_scatter(
            enc_upbias_grad.astype(jnp.bfloat16), "pb", scatter_dimension=0, tiled=True
        ).astype(jnp.float32),
        lax.psum_scatter(
            enc_bias_grad.astype(jnp.bfloat16), "pb", scatter_dimension=1, tiled=True
        ).astype(jnp.float32),
        lax.psum_scatter(
            enc_gain_grad.astype(jnp.bfloat16), "pb", scatter_dimension=1, tiled=True
        ).astype(jnp.float32),
        lax.psum_scatter(
            dec_self_grad.astype(jnp.bfloat16), "pb", scatter_dimension=1, tiled=True
        ).astype(jnp.float32),
        lax.psum_scatter(
            dec_cross_grad.astype(jnp.bfloat16), "pb", scatter_dimension=1, tiled=True
        ).astype(jnp.float32),
        lax.psum_scatter(
            dec_up_grad.astype(jnp.bfloat16), "pb", scatter_dimension=0, tiled=True
        ).astype(jnp.float32),
        lax.psum_scatter(
            dec_down_grad.astype(jnp.bfloat16), "pb", scatter_dimension=0, tiled=True
        ).astype(jnp.float32),
        lax.psum_scatter(
            dec_upbias_grad.astype(jnp.bfloat16), "pb", scatter_dimension=0, tiled=True
        ).astype(jnp.float32),
        lax.psum_scatter(
            dec_bias_grad.astype(jnp.bfloat16), "pb", scatter_dimension=1, tiled=True
        ).astype(jnp.float32),
        lax.psum_scatter(
            dec_gain_grad.astype(jnp.bfloat16), "pb", scatter_dimension=1, tiled=True
        ).astype(jnp.float32),
    )
    summed = jax.tree.map(
        lambda part: part.astype(jnp.float32), lax.psum(shortened(tuple(shares)), "slot")
    )
    return (
        (
            loss,
            passage_grad.reshape(1, 1, SRC_LEN, D),
            question_grad.reshape(1, 1, TGT_LEN, D),
            score_grad,
        )
        + tuple(summed)
        + (embed_grad,)
    )


def solution(mesh):
    placed = (
        P("pb", "slot", None, None),
        P("pb", "slot", None, None),
        P("pb", "slot"),
        P("pb", "slot"),
        P("pb", None, None),
        P(None, "pb", None),
        P("pb", None),
        P("pb", None),
        P("pb"),
        P(None, "pb"),
        P(None, "pb"),
        P(None, "pb", None),
        P(None, "pb", None),
        P("pb", None),
        P("pb", None),
        P("pb"),
        P(None, "pb"),
        P(None, "pb"),
        P(("slot", "pb"), None),
    )
    return jax.shard_map(
        local,
        mesh=mesh,
        in_specs=placed,
        out_specs=(
            P("pb"),
            P("pb", "slot", None, None),
            P("pb", "slot", None, None),
            P("pb", "slot"),
            P(None, "pb", None),
            P("pb", None),
            P("pb", None),
            P("pb"),
            P(None, "pb"),
            P(None, "pb"),
            P(None, "pb", None),
            P(None, "pb", None),
            P("pb", None),
            P("pb", None),
            P("pb"),
            P(None, "pb"),
            P(None, "pb"),
            P(("slot", "pb"), None),
        ),
        check_vma=False,
    )
```

profile of v0, /device:TPU:0, one launch (start us, length us, event | category | flops | bytes accessed | tf_op | source)
XLA Modules:
  0.0 3815.3 jit_solution(12197246419202198882)
XLA Ops:
  14.1 6.1 all_gather.50
  20.2 5.4 all_gather.54
  25.6 5.1 all_gather.48
  30.7 5.2 all_gather.45
  35.9 5.2 all_gather.47
  41.1 5.3 all_gather.44
  47.8 23.2 all-gather.9.cloned.1.call-done
  77.9 52.9 %all-gather.11.cloned.1.call-done = bf16[4,1024,1024]{2,1,0:T(8,128)(2,1)} async-done(((bf16[4,256,1024]{2,1,0:T(8,128)(2,1)}), bf16[4,1024,1024]{2,1,0:T(8,128)(2,1)}) %all-gather.11.cloned.1.call-update) | async-done | bytes 8388624 | tf_op jit(solution)/shard_map/all_gather | solution.py:173
  137.8 3.2 fusion.64
  146.3 44.5 %all-gather.17.cloned.1.call-done = bf16[4,1024,1024]{2,1,0:T(8,128)(2,1)} async-done(((bf16[4,256,1024]{2,1,0:T(8,128)(2,1)}), bf16[4,1024,1024]{2,1,0:T(8,128)(2,1)}) %all-gather.17.cloned.1.call-update) | async-done | bytes 8388624 | tf_op jit(solution)/shard_map/all_gather | solution.py:180
  193.1 5.4 fusion.159
  198.5 5.9 fusion.59
  204.5 3.0 fusion.160
  207.8 42.7 %all-gather.13.cloned.1.call-done = bf16[1024,4096]{1,0:T(8,128)(2,1)} async-done(((bf16[256,4096]{1,0:T(8,128)(2,1)}), bf16[1024,4096]{1,0:T(8,128)(2,1)}) %all-gather.13.cloned.1.call-update) | async-done | bytes 8388624 | tf_op jit(solution)/shard_map/all_gather | solution.py:174
  250.5 20.4 multiply_convert_fusion.2
  271.0 39.3 %all-gather.15.cloned.1.call-done = bf16[4096,1024]{1,0:T(8,128)(2,1)} async-done(((bf16[1024,1024]{1,0:T(8,128)(2,1)}), bf16[4096,1024]{1,0:T(8,128)(2,1)}) %all-gather.15.cloned.1.call-update) | async-done | bytes 8388624 | tf_op jit(solution)/shard_map/all_gather | solution.py:175
  310.3 7.2 fusion.161
  319.0 3.2 add_convert_fusion
  334.9 35.1 all-gather.19.cloned.1.call-done
  370.0 9.1 multiply_convert_fusion.4
  379.1 50.8 %all-gather.21.cloned.1.call-done = bf16[4096,1024]{1,0:T(8,128)(2,1)} async-done(((bf16[1024,1024]{1,0:T(8,128)(2,1)}), bf16[4096,1024]{1,0:T(8,128)(2,1)}) %all-gather.21.cloned.1.call-update) | async-done | bytes 8388624 | tf_op jit(solution)/shard_map/all_gather | solution.py:182
  429.9 4.8 fusion.166
  434.9 514.9 %all-gather.23.cloned.1.call-done = bf16[49152,1024]{1,0:T(8,128)(2,1)} async-done(((bf16[1536,1024]{1,0:T(8,128)(2,1)}), bf16[49152,1024]{1,0:T(8,128)(2,1)}) %all-gather.23.cloned.1.call-update) | async-done | bytes 100663312 | tf_op jit(solution)/shard_map/all_gather | solution.py:249
  949.8 47.5 %fusion.167 = (f32[128]{0:T(128)S(1)}, f32[128,49152]{1,0:T(8,128)}) fusion(bf16[49152,1024]{1,0:T(8,128)(2,1)} %all-gather.23.cloned.1.call-done, f32[128,1024]{1,0:T(8,128)S(1)} %get-tuple-element.178, f32[1024]{0:T(1024)S(1)} %bitcast.425, f32[1024]{0:T(1024)S(1)} %bitcast.418, f32[128]{0:T(128)S(1)} %add_rsqrt_fusion.2, ...), kind=kOutput, calls=%fused_computation.317 | convolution fusion | flops 12891848704 | bytes 126363136 | tf_op jit(solution)/shard_map/dot_general | solution.py:26
  997.4 12.0 exponential_reduce_fusion
  1009.5 19.4 all-reduce.3
  1028.9 17.6 all-reduce.2
  1049.1 41.9 %multiply_reduce_fusion.13 = (bf16[1024]{0:T(1024)(128)(2,1)}, f32[128]{0:T(128)S(1)}, f32[128]{0:T(128)S(1)}, bf16[1024]{0:T(1024)(128)(2,1)}, f32[128,1024]{1,0:T(8,128)S(1)}) fusion(f32[128,1024]{1,0:T(8,128)S(1)} %get-tuple-element.178, f32[128]{0:T(128)S(1)} %add_rsqrt_fusion.2, f32[128]{0:T(128)S(1)} %broadcast_multiply_fusion.12, ...), kind=kOutput, calls=%fused_computation.201 | convolution fusion | flops 12923828224 | bytes 126889472 | tf_op jit(solution)/shard_map/dot_general | solution.py:22
  1091.9 10.6 fusion.169
  1102.5 6.9 multiply_reduce_fusion.14
  1110.3 3.1 fusion.84
  1115.3 3.8 bitcast_convert_fusion.2
  1126.1 3.9 pad_maximum_fusion.2
  1150.8 3.9 pad_maximum_fusion.1
  1155.1 3.0 fusion.42
  1158.2 3.3 multiply_reduce_fusion.4
  1162.1 9.5 fusion.168
  1173.3 7.0 convolution_convert_fusion.1
  1180.6 10.3 convolution_convert_fusion
  1192.1 5.7 convolution_convert_fusion.3
  1199.2 5.7 convolution_convert_fusion.2
  1206.3 8.2 multiply_reduce_fusion.5
  1215.1 3.1 fusion.63
  1218.6 6.8 bitcast_convert_fusion
  1228.9 4.6 multiply_reduce_fusion
  1233.5 10.8 multiply_convert_fusion.1
  1244.3 4.5 multiply_convert_fusion.5
  1254.8 3.8 pad_maximum_fusion
  1267.6 6.4 reduce-scatter.25.cloned.1.call-done
  1274.0 74.4 %reduce-scatter.19.cloned.1.call-done = bf16[256,4096]{1,0:T(8,128)(2,1)} async-done(((bf16[1024,4096]{1,0:T(8,128)(2,1)}), bf16[256,4096]{1,0:T(8,128)(2,1)}) %reduce-scatter.19.cloned.1.call-update) | async-done | bytes 2097168 | tf_op jit(solution)/shard_map/reduce_scatter | solution.py:351
  1348.4 74.4 %reduce-scatter.21.cloned.1.call-done = bf16[1024,1024]{1,0:T(8,128)(2,1)} async-done(((bf16[4096,1024]{1,0:T(8,128)(2,1)}), bf16[1024,1024]{1,0:T(8,128)(2,1)}) %reduce-scatter.21.cloned.1.call-update) | async-done | bytes 2097168 | tf_op jit(solution)/shard_map/reduce_scatter | solution.py:354
  1422.8 74.4 %reduce-scatter.29.cloned.1.call-done = bf16[256,4096]{1,0:T(8,128)(2,1)} async-done(((bf16[1024,4096]{1,0:T(8,128)(2,1)}), bf16[256,4096]{1,0:T(8,128)(2,1)}) %reduce-scatter.29.cloned.1.call-update) | async-done | bytes 2097168 | tf_op jit(solution)/shard_map/reduce_scatter | solution.py:372
  1497.1 74.4 %reduce-scatter.31.cloned.1.call-done = bf16[1024,1024]{1,0:T(8,128)(2,1)} async-done(((bf16[4096,1024]{1,0:T(8,128)(2,1)}), bf16[1024,1024]{1,0:T(8,128)(2,1)}) %reduce-scatter.31.cloned.1.call-update) | async-done | bytes 2097168 | tf_op jit(solution)/shard_map/reduce_scatter | solution.py:375
  1571.5 74.2 %reduce-scatter.17.cloned.1.call-done = bf16[4,256,1024]{1,2,0:T(8,128)(2,1)} async-done(((bf16[4,1024,1024]{1,2,0:T(8,128)(2,1)}), bf16[4,256,1024]{1,2,0:T(8,128)(2,1)}) %reduce-scatter.17.cloned.1.call-update) | async-done | bytes 2097168 | tf_op jit(solution)/shard_map/reduce_scatter | solution.py:348
  1646.8 77.5 %fusion.141 = f32[49152,1024]{1,0:T(8,128)} fusion(f32[128,1024]{1,0:T(8,128)S(1)} %copy-done.6, f32[1024]{0:T(1024)S(1)} %bitcast.426, f32[1024]{0:T(1024)S(1)} %bitcast.421, f32[128]{0:T(128)S(1)} %copy-done.112, f32[128]{0:T(128)S(1)} %copy-done.110, f32[128,49152]{1,0:T(8,128)} %get-tuple-element.180, f32[128]{0:T(128)S(1)} %copy-done.81, ...), kind=kOutput, calls=%fused_computation.294 | convolution fusion | flops 12923305984 | bytes 227027456 | tf_op jit(solution)/shard_map/dot_general | solution.py:32
  1727.4 10.2 all-reduce.6
  1742.6 3.3 fusion.76
  1748.6 3.0 fusion.36
  1751.6 3.9 add_bitcast_fusion
  1757.4 39.7 %all-reduce.4 = (bf16[1024]{0:T(1024)(128)(2,1)S(1)}, bf16[6,256]{1,0:T(8,128)(2,1)S(1)}, bf16[2,256]{1,0:T(2,128)(2,1)S(1)}, bf16[1024]{0:T(1024)(128)(2,1)S(1)...) all-reduce(bf16[1024]{0:T(1024)(128)(2,1)S(1)} %dynamic-slice.1, ...), channel_id=1, replica_groups=mesh['slot'=8,'pb'=4] {'slot'}, use_global_device_ids=true, to_apply=%region_49.50 | all-reduce | flops 7424 | bytes 29696 | tf_op jit(solution)/shard_map/psum | solution.py:389
  1800.7 401.4 %all-reduce.9.cloned.1.call-done = (bf16[4,256,1024]{1,2,0:T(8,128)(2,1)}, bf16[4,256,1024]{1,2,0:T(8,128)(2,1)}, bf16[256,4096]{1,0:T(8,128)(2,1)}, bf16[1024,1...) async-done(((bf16[4,256,1024]{1,2,0:T(8,128)(2,1)}, bf16[4,256,1024]{1,2,0:T(8,128)(2,1)}, ...) | async-done | bytes 14680080 | tf_op jit(solution)/shard_map/psum | solution.py:389
  2202.1 4.1 copy.119
  2206.3 4.3 copy.120
  2224.5 1581.5 %reduce-scatter.35.cloned.1.call-done = f32[1536,1024]{1,0:T(8,128)} async-done(((f32[49152,1024]{1,0:T(8,128)}), f32[1536,1024]{1,0:T(8,128)}) %reduce-scatter.35.cloned.1.call-update) | async-done | bytes 6291472 | tf_op jit(solution)/shard_map/reduce_scatter | solution.py:286
  (463 shorter events, 130.8 us)
Async XLA Ops:
  7.2 63.8 %all-gather.9.cloned.1.call-start = ((), (), s32[]{:S(2)}) async-start(), calls=%async_computation.12 | async-start | bytes 10485760 | tf_op jit(solution)/shard_map/all_gather | solution.py:179
  7.9 122.9 %all-gather.11.cloned.1.call-start = ((), (), s32[]{:S(2)}) async-start(), calls=%async_computation.13 | async-start | bytes 10485760 | tf_op jit(solution)/shard_map/all_gather | solution.py:173
  8.7 182.1 %all-gather.17.cloned.1.call-start = ((), (), s32[]{:S(2)}) async-start(), calls=%async_computation.16 | async-start | bytes 10485760 | tf_op jit(solution)/shard_map/all_gather | solution.py:180
  9.4 241.1 %all-gather.13.cloned.1.call-start = ((), (), s32[]{:S(2)}) async-start(), calls=%async_computation.14 | async-start | bytes 10485760 | tf_op jit(solution)/shard_map/all_gather | solution.py:174
  10.0 300.3 %all-gather.15.cloned.1.call-start = ((), (), s32[]{:S(2)}) async-start(), calls=%async_computation.15 | async-start | bytes 10485760 | tf_op jit(solution)/shard_map/all_gather | solution.py:175
  10.6 359.4 %all-gather.19.cloned.1.call-start = ((), (), s32[]{:S(2)}) async-start(), calls=%async_computation.17 | async-start | bytes 10485760 | tf_op jit(solution)/shard_map/all_gather | solution.py:181
  11.2 418.7 %all-gather.21.cloned.1.call-start = ((), (), s32[]{:S(2)}) async-start(), calls=%async_computation.18 | async-start | bytes 10485760 | tf_op jit(solution)/shard_map/all_gather | solution.py:182
  11.9 13.7 copy-start.121
  11.9 18.8 copy-start.118
  11.9 23.9 copy-start.113
  12.0 29.1 copy-start.104
  12.0 35.0 copy-start.122
  12.0 59.0 %copy-start.20 = (bf16[1,1,128,1024]{3,2,1,0:T(8,128)(2,1)S(1)}, bf16[1,1,128,1024]{3,2,1,0:T(8,128)(2,1)}, u32[]{:S(2)}) copy-start(bf16[1,1,128,1024]{3,2,1,0:T(8,128)(2,1)} %param.20) | copy-start | bytes 786436
  12.0 937.8 %all-gather.23.cloned.1.call-start = ((), (), s32[]{:S(2)}) async-start(), calls=%async_computation.19 | async-start | bytes 103809024 | tf_op jit(solution)/shard_map/all_gather | solution.py:249
  12.7 1254.9 %reduce-scatter.27.cloned.1.call-start = ((), (), s32[]{:S(2)}) async-start(), calls=%async_computation.25 | async-start | bytes 10485760 | tf_op jit(solution)/shard_map/reduce_scatter | solution.py:369
  46.4 29.0 copy-start.107
  46.9 95.9 %copy-start.98 = (pred[128,128]{0,1:T(8,128)(4,1)}, pred[128,128]{0,1:T(8,128)(4,1)S(1)}, u32[]{:S(2)}) copy-start(pred[128,128]{0,1:T(8,128)(4,1)S(1)} %iota_compare_fusion.1) | copy-start | bytes 49156
  47.6 262.6 %copy-start.96 = (f32[1,1024]{1,0:T(1,128)}, f32[1,1024]{1,0:T(1,128)S(1)}, u32[]{:S(2)}) copy-start(f32[1,1024]{1,0:T(1,128)S(1)} %get-tuple-element.157) | copy-start | bytes 12292
  47.6 270.2 %copy-start.86 = (f32[1,1024]{1,0:T(1,128)}, f32[1,1024]{1,0:T(1,128)S(1)}, u32[]{:S(2)}) copy-start(f32[1,1024]{1,0:T(1,128)S(1)} %get-tuple-element.156) | copy-start | bytes 12292
  47.7 1043.4 %copy-start.78 = (f32[1,1024]{1,0:T(1,128)}, f32[1,1024]{1,0:T(1,128)S(1)}, u32[]{:S(2)}) copy-start(f32[1,1024]{1,0:T(1,128)S(1)} %get-tuple-element.153) | copy-start | bytes 12292
  47.7 262.5 %copy-start.114 = (f32[1,1024]{1,0:T(1,128)}, f32[1,1024]{1,0:T(1,128)S(1)}, u32[]{:S(2)}) copy-start(f32[1,1024]{1,0:T(1,128)S(1)} %get-tuple-element.149) | copy-start | bytes 12292
  47.8 382.1 %copy-start.74 = (f32[1,1024]{1,0:T(1,128)}, f32[1,1024]{1,0:T(1,128)S(1)}, u32[]{:S(2)}) copy-start(f32[1,1024]{1,0:T(1,128)S(1)} %get-tuple-element.139) | copy-start | bytes 12292
  47.8 902.1 %copy-start.84 = (f32[1,1024]{1,0:T(1,128)}, f32[1,1024]{1,0:T(1,128)S(1)}, u32[]{:S(2)}) copy-start(f32[1,1024]{1,0:T(1,128)S(1)} %get-tuple-element.137) | copy-start | bytes 12292
  73.2 69.7 %copy-start.47 = (bf16[128,1024]{0,1:T(8,128)(2,1)}, bf16[128,1024]{0,1:T(8,128)(2,1)S(1)}, u32[]{:S(2)}) copy-start(bf16[128,1024]{0,1:T(8,128)(2,1)S(1)} %copy.98) | copy-start | bytes 786436
  75.4 55.5 %copy-start.62 = (bf16[1,1,384,1024]{3,2,1,0:T(8,128)(2,1)S(1)}, bf16[1,1,384,1024]{3,2,1,0:T(8,128)(2,1)}, u32[]{:S(2)}) copy-start(bf16[1,1,384,1024]{3,2,1,0:T(8,128)(2,1)} %param.19) | copy-start | bytes 2359300
  75.5 67.3 %copy-start.69 = (bf16[128,1024]{0,1:T(8,128)(2,1)}, bf16[128,1024]{0,1:T(8,128)(2,1)S(1)}, u32[]{:S(2)}) copy-start(bf16[128,1024]{0,1:T(8,128)(2,1)S(1)} %copy.97) | copy-start | bytes 786436
  77.9 65.0 %copy-start.49 = (bf16[128,1024]{0,1:T(8,128)(2,1)}, bf16[128,1024]{0,1:T(8,128)(2,1)S(1)}, u32[]{:S(2)}) copy-start(bf16[128,1024]{0,1:T(8,128)(2,1)S(1)} %copy.99) | copy-start | bytes 786436
  133.8 59.3 %copy-start.26 = (bf16[384,1024]{0,1:T(8,128)(2,1)}, bf16[384,1024]{0,1:T(8,128)(2,1)S(1)}, u32[]{:S(2)}) copy-start(bf16[384,1024]{0,1:T(8,128)(2,1)S(1)} %copy.102) | copy-start | bytes 2359300
  141.4 51.7 %copy-start.30 = (bf16[384,1024]{0,1:T(8,128)(2,1)}, bf16[384,1024]{0,1:T(8,128)(2,1)S(1)}, u32[]{:S(2)}) copy-start(bf16[384,1024]{0,1:T(8,128)(2,1)S(1)} %copy.103) | copy-start | bytes 2359300
  143.6 49.3 %copy-start.53 = (bf16[16,64,128]{2,1,0:T(8,128)(2,1)}, bf16[16,64,128]{2,1,0:T(8,128)(2,1)S(1)}, u32[]{:S(2)}) copy-start(bf16[16,64,128]{2,1,0:T(8,128)(2,1)S(1)} %convolution_convert_fusion.5) | copy-start | bytes 786436
  146.0 47.0 %copy-start.11 = (f32[128,1024]{1,0:T(8,128)}, f32[128,1024]{1,0:T(8,128)S(1)}, u32[]{:S(2)}) copy-start(f32[128,1024]{1,0:T(8,128)S(1)} %get-tuple-element.170) | copy-start | bytes 1572868
  207.5 102.8 %copy-start.3 = (f32[384,1024]{1,0:T(8,128)}, f32[384,1024]{1,0:T(8,128)S(1)}, u32[]{:S(2)}) copy-start(f32[384,1024]{1,0:T(8,128)S(1)} %get-tuple-element.163) | copy-start | bytes 4718596
  207.5 102.8 %copy-start.92 = (f32[384]{0:T(512)}, f32[384]{0:T(512)S(1)}, u32[]{:S(2)}) copy-start(f32[384]{0:T(512)S(1)} %broadcast_multiply_fusion.5) | copy-start | bytes 4612
  207.8 102.4 %copy-start.99 = (f32[384]{0:T(512)}, f32[384]{0:T(512)S(1)}, u32[]{:S(2)}) copy-start(f32[384]{0:T(512)S(1)} %add_rsqrt_fusion.1) | copy-start | bytes 4612
  379.1 55.6 %copy-start.9 = (bf16[128,4096]{1,0:T(8,128)(2,1)}, bf16[128,4096]{1,0:T(8,128)(2,1)S(1)}, u32[]{:S(2)}) copy-start(bf16[128,4096]{1,0:T(8,128)(2,1)S(1)} %get-tuple-element.175) | copy-start | bytes 3145732
  434.7 656.4 %copy-start.5 = (f32[128,1024]{1,0:T(8,128)}, f32[128,1024]{1,0:T(8,128)S(1)}, u32[]{:S(2)}) copy-start(f32[128,1024]{1,0:T(8,128)S(1)} %get-tuple-element.178) | copy-start | bytes 1572868
  434.7 656.4 %copy-start.109 = (f32[128]{0:T(128)}, f32[128]{0:T(128)S(1)}, u32[]{:S(2)}) copy-start(f32[128]{0:T(128)S(1)} %broadcast_multiply_fusion.12) | copy-start | bytes 1540
  434.9 656.2 %copy-start.111 = (f32[128]{0:T(128)}, f32[128]{0:T(128)S(1)}, u32[]{:S(2)}) copy-start(f32[128]{0:T(128)S(1)} %add_rsqrt_fusion.2) | copy-start | bytes 1540
  949.8 47.5 %copy-start.76 = (s32[128]{0:T(128)S(1)}, s32[128]{0:T(128)}, u32[]{:S(2)}) copy-start(s32[128]{0:T(128)} %fusion.131) | copy-start | bytes 1540
  997.3 12.1 copy-start.108
  997.3 12.1 copy-start.127
  1009.4 81.7 %copy-start.80 = (f32[128]{0:T(128)}, f32[128]{0:T(128)S(1)}, u32[]{:S(2)}) copy-start(f32[128]{0:T(128)S(1)} %get-tuple-element.128) | copy-start | bytes 1540
  1049.1 41.9 %copy-start.82 = (f32[128]{0:T(128)}, f32[128]{0:T(128)S(1)}, u32[]{:S(2)}) copy-start(f32[128]{0:T(128)S(1)} %get-tuple-element.159) | copy-start | bytes 1540
  1130.1 144.0 %reduce-scatter.25.cloned.1.call-start = ((), (), s32[]{:S(2)}) async-start(), calls=%async_computation.24 | async-start | bytes 10485760 | tf_op jit(solution)/shard_map/reduce_scatter | solution.py:366
  1134.0 15.2 copy-start.16
  1154.8 193.6 %reduce-scatter.19.cloned.1.call-start = ((), (), s32[]{:S(2)}) async-start(), calls=%async_computation.21 | async-start | bytes 10485760 | tf_op jit(solution)/shard_map/reduce_scatter | solution.py:351
  1162.0 11.2 copy-start.4
  1162.1 11.2 copy-start.93
  1162.1 11.2 copy-start.97
  1162.1 11.2 copy-start.100
  1162.1 11.2 copy-start.115
  1180.3 242.4 %reduce-scatter.21.cloned.1.call-start = ((), (), s32[]{:S(2)}) async-start(), calls=%async_computation.22 | async-start | bytes 10485760 | tf_op jit(solution)/shard_map/reduce_scatter | solution.py:354
  1190.9 306.2 %reduce-scatter.29.cloned.1.call-start = ((), (), s32[]{:S(2)}) async-start(), calls=%async_computation.26 | async-start | bytes 10485760 | tf_op jit(solution)/shard_map/reduce_scatter | solution.py:372
  1197.9 373.6 %reduce-scatter.31.cloned.1.call-start = ((), (), s32[]{:S(2)}) async-start(), calls=%async_computation.27 | async-start | bytes 10485760 | tf_op jit(solution)/shard_map/reduce_scatter | solution.py:375
  1204.9 440.8 %reduce-scatter.17.cloned.1.call-start = ((), (), s32[]{:S(2)}) async-start(), calls=%async_computation.20 | async-start | bytes 10485760 | tf_op jit(solution)/shard_map/reduce_scatter | solution.py:348
  1258.7 496.9 %reduce-scatter.37.cloned.1.call-start = ((), (), s32[]{:S(2)}) async-start(), calls=%async_computation.30 | async-start | bytes 327680
  1262.0 494.5 %reduce-scatter.39.cloned.1.call-start = ((), (), s32[]{:S(2)}) async-start(), calls=%async_computation.31 | async-start | bytes 327680
  1262.9 494.5 %reduce-scatter.23.cloned.1.call-start = ((), (), s32[]{:S(2)}) async-start(), calls=%async_computation.23 | async-start | bytes 20480 | tf_op jit(solution)/shard_map/reduce_scatter | solution.py:360
  1264.1 493.3 %reduce-scatter.33.cloned.1.call-start = ((), (), s32[]{:S(2)}) async-start(), calls=%async_computation.28 | async-start | bytes 40960 | tf_op jit(solution)/shard_map/reduce_scatter | solution.py:381
  1267.5 934.6 %all-reduce.9.cloned.1.call-start = ((), (), s32[]{:S(2)}) async-start(), calls=%async_computation.32 | async-start | bytes 29360128 | tf_op jit(solution)/shard_map/psum | solution.py:389
  1645.8 2160.3 %reduce-scatter.35.cloned.1.call-start = ((), (), s32[]{:S(2)}) async-start(), calls=%async_computation.29 | async-start | bytes 207618048 | tf_op jit(solution)/shard_map/reduce_scatter | solution.py:286
  1724.2 13.4 copy-start.68
  1724.3 15.8 copy-start.17
  1724.3 15.8 copy-start.33
  (91 other events, 298.4 us)
Sparse Core Ops, SparseCore 0:
  9.6 61.3 all-gather.8
  72.5 58.2 all-gather.10
  132.4 58.2 all-gather.16
  192.2 58.2 all-gather.12
  251.9 58.2 all-gather.14
  311.7 58.2 all-gather.18
  371.5 58.2 all-gather.20
  432.8 517.0 all-gather.22
  1130.2 69.4 reduce-scatter.26
  1202.3 71.6 reduce-scatter.24
  1276.6 71.7 reduce-scatter.18
  1351.0 71.6 reduce-scatter.20
  1425.3 71.7 reduce-scatter.28
  1499.7 71.6 reduce-scatter.30
  1573.9 71.7 reduce-scatter.16
  1648.7 19.9 reduce-scatter.36
  1671.6 20.0 reduce-scatter.38
  1694.7 19.2 reduce-scatter.22
  1717.0 19.3 reduce-scatter.32
  1742.9 459.1 all-reduce.8
  2209.1 1596.8 reduce-scatter.34
where the time goes:
time: 3820 us
  waiting for transfers between devices  3170 us (83%)
  matrix products  400 us (10%)
  blocking collectives  119 us (3%)
  other arithmetic  63.4 us (2%)
  local copies, waits for them, and re-layouts  38.2 us (1%)
    reduce_scatter x1, waiting for transfers between devices, local(): lax.psum_scatter(matmul_tn(delta, state_low), ('slot', 'pb'), scatter_dim...  1580 us
    all_gather x1, waiting for transfers between devices, local(): piece = lax.all_gather(embed, ('slot', 'pb'), axis=0, tiled=True)  515 us
    psum x1, waiting for transfers between devices, local(): lax.psum(shortened(tuple(shares)), 'slot')  401 us
    dot_general x17, matrix products, matmul_tn(): lax.dot_general(left, right, (((0,), (0,)), ((), ())), preferred_element_...  122 us
    dot_general x17, matrix products, matmul_nt(): lax.dot_general(left, right, (((1,), (1,)), ((), ())), preferred_element_...  118 us
    dot_general x17, matrix products, matmul(): return jnp.dot(left, right, preferred_element_type=jnp.float32)  114 us
  transfers between devices with their start and end apart: 21, of which 16 were waited for; matrix products, arithmetic and copies ran while one was open for 9% of the time, Pallas kernels for 0%

commit v1 on v0

v1 whole, which is shorter than its diff:
```python
import functools

import jax
import jax.numpy as jnp
from jax import lax
from jax.experimental import pallas as pl
from jax.experimental.pallas import tpu as pltpu
from jax.sharding import PartitionSpec as P

D = 1024
HEADS = 16
HEAD_DIM = 64
SRC_LEN = 384
TGT_LEN = 128
MESH = pl.DeviceIdType.MESH
UNIT = 256
UNITS = 28
RING = 8


BIG_NEGATIVE = -1e30
MASK_FILL = -1000000000.0


def matmul(left, right):
    return jnp.dot(left, right, preferred_element_type=jnp.float32)


def matmul_nt(left, right):
    return lax.dot_general(
        left, right, (((1,), (1,)), ((), ())), preferred_element_type=jnp.float32
    )


def matmul_tn(left, right):
    return lax.dot_general(
        left, right, (((0,), (0,)), ((), ())), preferred_element_type=jnp.float32
    )


def to_low(value):
    return value.astype(jnp.bfloat16)


def norm_forward(total, gain, shift):
    centered = total - jnp.mean(total, axis=-1, keepdims=True)
    inverse = lax.rsqrt(jnp.mean(centered * centered, axis=-1, keepdims=True) + 1e-05)
    normed = centered * inverse
    return (normed * gain + shift, (normed, inverse))


def norm_backward(upstream, saved, gain):
    normed, inverse = saved
    scaled = upstream * gain
    inner = (
        scaled
        - jnp.mean(scaled, axis=-1, keepdims=True)
        - normed * jnp.mean(scaled * normed, axis=-1, keepdims=True)
    )
    return (inverse * inner, jnp.sum(upstream * normed, axis=0), jnp.sum(upstream, axis=0))


def attend_forward(query_low, memory_low, matrices, bias_query, bias_value, bias_out, causal):
    rows = query_low.shape[0]
    columns = memory_low.shape[0]
    queries = to_low(matmul(query_low, matrices[0]) + bias_query).reshape(rows, HEADS, HEAD_DIM)
    keys = to_low(matmul(memory_low, matrices[1])).reshape(columns, HEADS, HEAD_DIM)
    values = to_low(matmul(memory_low, matrices[2]) + bias_value).reshape(columns, HEADS, HEAD_DIM)
    scores = jnp.einsum(
        "qhd,khd->hqk", queries, keys, preferred_element_type=jnp.float32
    ) * HEAD_DIM ** (-0.5)
    if causal:
        visible = jnp.arange(rows)[:, None] >= jnp.arange(columns)[None, :]
        scores = jnp.where(visible[None], scores, MASK_FILL)
    shifted = jnp.exp(scores - jnp.max(scores, axis=-1, keepdims=True))
    probs = shifted / jnp.sum(shifted, axis=-1, keepdims=True)
    context = to_low(
        jnp.einsum(
            "hqk,khd->qhd", to_low(probs), values, preferred_element_type=jnp.float32
        ).reshape(rows, D)
    )
    output = matmul(context, matrices[3]) + bias_out
    return (output, (queries, keys, values, probs, context))


def attend_backward(upstream, query_low, memory_low, matrices, saved):
    queries, keys, values, probs, context = saved
    rows = query_low.shape[0]
    columns = memory_low.shape[0]
    scale = HEAD_DIM ** (-0.5)
    upstream_low = to_low(upstream)
    grad_context = to_low(matmul_nt(upstream_low, matrices[3])).reshape(rows, HEADS, HEAD_DIM)
    grad_probs = jnp.einsum(
        "qhd,khd->hqk", grad_context, values, preferred_element_type=jnp.float32
    )
    grad_values = jnp.einsum(
        "hqk,qhd->khd", to_low(probs), grad_context, preferred_element_type=jnp.float32
    ).reshape(columns, D)
    grad_scores = to_low(probs * (grad_probs - jnp.sum(grad_probs * probs, axis=-1, keepdims=True)))
    grad_queries = (
        jnp.einsum("hqk,khd->qhd", grad_scores, keys, preferred_element_type=jnp.float32) * scale
    ).reshape(rows, D)
    grad_keys = (
        jnp.einsum("hqk,qhd->khd", grad_scores, queries, preferred_element_type=jnp.float32) * scale
    ).reshape(columns, D)
    queries_low = to_low(grad_queries)
    keys_low = to_low(grad_keys)
    values_low = to_low(grad_values)
    grad_query_input = matmul_nt(queries_low, matrices[0])
    grad_memory_input = matmul_nt(keys_low, matrices[1]) + matmul_nt(values_low, matrices[2])
    grad_pairs = [
        (query_low, queries_low),
        (memory_low, keys_low),
        (memory_low, values_low),
        (context, upstream_low),
    ]
    bias_grads = (
        jnp.sum(grad_queries, axis=0),
        jnp.sum(grad_values, axis=0),
        jnp.sum(upstream, axis=0),
    )
    return (grad_query_input, grad_memory_input, grad_pairs, bias_grads)


def gelu_exact(value):
    return jax.nn.gelu(value, approximate=False)


def feed_forward(input_low, weight_up, bias_up, weight_down, bias_down):
    before = matmul(input_low, weight_up) + bias_up
    hidden_low = to_low(gelu_exact(before))
    return (matmul(hidden_low, weight_down) + bias_down, (before, hidden_low))


def hidden_backward(upstream_low, weight_down, before):
    grad_hidden = matmul_nt(upstream_low, weight_down)
    unused, pullback = jax.vjp(gelu_exact, before)
    return pullback(grad_hidden)[0]


def bit_of(name, mask):
    return (lax.axis_index(name) // mask) % 2


def swap(value, name, mask):
    size = lax.axis_size(name)
    return lax.ppermute(value, name, [(i, i ^ mask) for i in range(size)])


def take(value, index, count, axis):
    size = value.shape[axis] // count
    return lax.dynamic_slice_in_dim(value, index * size, size, axis)


def masks_of(name):
    return masks_below(lax.axis_size(name))


class Ticker:
    def __init__(self):
        self.active = []

    def add(self, steps):
        self.active.append((steps, next(steps)))

    def tick(self, *values):
        held, tree = jax.tree.flatten((values, [arrays for _, arrays in self.active]))
        values, arrays = jax.tree.unflatten(tree, lax.optimization_barrier(held))
        going = []
        for (steps, _), mine in zip(self.active, arrays):
            try:
                going.append((steps, steps.send(mine)))
            except StopIteration:
                pass
        self.active = going
        return values if len(values) != 1 else values[0]

    def drain(self):
        while self.active:
            self.tick()


def gather_rows(shard, axis, box):
    size = lax.axis_size("pb")
    me = lax.axis_index("pb")
    side = bit_of("slot", 1)
    rows = shard.shape[axis]
    far = size // 2
    half = rows // 2

    def spread(pieces):
        mask = 1
        while mask < far:
            pieces = pieces + [
                ((start // rows ^ mask) * rows + start % rows, swap(piece, "pb", mask))
                for start, piece in pieces
            ]
            mask *= 2
        return pieces

    first = swap(take(shard, side, 2, axis), "pb", far)
    near = spread([(me * rows, shard)])
    starts = [start for start, _ in near]
    arrays = yield ([piece for _, piece in near], first)
    near = list(zip(starts, arrays[0]))
    first = arrays[1]
    second = swap(first, "slot", 1)
    pieces = near + spread([((me ^ far) * rows + side * half, first)])
    pieces = pieces + spread([((me ^ far) * rows + (1 - side) * half, second)])
    starts = [start for start, _ in pieces]
    arrays = yield [piece for _, piece in pieces]
    shape = list(shard.shape)
    shape[axis] = rows * size
    full = jnp.zeros(tuple(shape), shard.dtype)
    for start, piece in zip(starts, arrays):
        full = lax.dynamic_update_slice_in_dim(full, piece, start, axis)
    box.append(full)


def gather_small(value, names, box):
    held = value[None]
    for name in names:
        for mask in masks_of(name):
            side = bit_of(name, mask)
            came = swap(held, name, mask)
            held = jnp.concatenate(
                [jnp.where(side == 0, held, came), jnp.where(side == 0, came, held)], axis=0
            )
    held = yield held
    box.append(held)


def masks_below(size):
    return [1 << i for i in range(size.bit_length() - 1)]


def xor(value, mask):
    return jnp.where((value // mask) % 2 == 0, value + mask, value - mask)


def sync_kernel(
    slots,
    count,
    parts,
    small,
    out,
    small_out,
    keep,
    core_in,
    far_out,
    far_keep,
    far_in,
    half_out,
    half_keep,
    half_in,
    full,
    small_core,
    small_far,
    small_in,
    small_out_far,
    small_out_slot,
    load_sem,
    store_sem,
    send_sem,
    recv_sem,
    small_send,
    small_recv,
):
    masks = masks_below(slots)
    levels = len(masks)
    rows = full.shape[1]
    slot, pb = lax.axis_index("slot"), lax.axis_index("pb")
    core, far = xor(pb, 1), xor(pb, 2)
    far_core = xor(core, 2)
    partners = [(slot, core), (slot, far)] + [(xor(slot, mask), pb) for mask in masks]
    bits = [(slot // mask) % 2 for mask in masks]

    barrier = pltpu.get_barrier_semaphore()
    for partner in partners:
        pl.semaphore_signal(barrier, inc=1, device_id=partner, device_id_type=MESH)
    pl.semaphore_wait(barrier, len(partners))

    def remote(source, target, stage, at, partner):
        return pltpu.make_async_remote_copy(
            src_ref=source,
            dst_ref=target,
            send_sem=send_sem.at[stage, at],
            recv_sem=recv_sem.at[stage, at],
            device_id=partner,
            device_id_type=MESH,
        )

    def core_copies(c):
        at = lax.rem(c, RING)
        ring = lax.rem(c, 4)
        return (
            remote(parts.at[c, core], core_in.at[ring, 0], 0, at, partners[0]),
            remote(parts.at[c, far_core], core_in.at[ring, 1], 1, at, partners[0]),
        )

    def loads(c):
        ring = lax.rem(c, 4)
        return (
            pltpu.make_async_copy(parts.at[c, pb], keep.at[ring, 0], load_sem.at[0, ring]),
            pltpu.make_async_copy(parts.at[c, far], keep.at[ring, 1], load_sem.at[1, ring]),
        )

    def far_copy(c):
        ring = lax.rem(c, 4)
        return remote(far_out.at[ring], far_in.at[ring], 2, lax.rem(c, RING), partners[1])

    def halve_copy(level, c):
        ring = lax.rem(c, 4)
        return remote(
            half_out[level].at[ring],
            half_in[level].at[ring],
            3 + level,
            lax.rem(c, RING),
            partners[2 + level],
        )

    def join_copy(level, c):
        at = lax.rem(c, RING)
        size = rows >> (level + 1)
        offset = sum(bits[i] * (rows >> (i + 1)) for i in range(level + 1))
        where = pl.ds(pl.multiple_of(offset, size), size)
        return remote(
            full.at[at, where], full.at[at, where], 3 + levels + level, at, partners[2 + level]
        )

    def store(c):
        at = lax.rem(c, RING)
        return pltpu.make_async_copy(full.at[at], out.at[c], store_sem.at[at])

    def add(target, left, right, size):
        tile = min(size, 32)

        @pl.loop(0, size // tile)
        def _(i):
            at = pl.ds(pl.multiple_of(i * tile, tile), tile)
            total = left[at, :].astype(jnp.float32) + right[at, :].astype(jnp.float32)
            target[at, :] = total.astype(target.dtype)

    def small_core_copies():
        return [
            pltpu.make_async_remote_copy(
                src_ref=small.at[source],
                dst_ref=small_core.at[i],
                send_sem=small_send.at[i],
                recv_sem=small_recv.at[i],
                device_id=partners[0],
                device_id_type=MESH,
            )
            for i, source in ((0, core), (1, far_core))
        ]

    def small_far_copy():
        return pltpu.make_async_remote_copy(
            src_ref=small_out_far,
            dst_ref=small_far,
            send_sem=small_send.at[2],
            recv_sem=small_recv.at[2],
            device_id=partners[1],
            device_id_type=MESH,
        )

    def small_slot_copy(level):
        return pltpu.make_async_remote_copy(
            src_ref=small_out_slot.at[level],
            dst_ref=small_in.at[level],
            send_sem=small_send.at[3 + level],
            recv_sem=small_recv.at[3 + level],
            device_id=partners[2 + level],
            device_id_type=MESH,
        )

    def small_stage(step):
        if step == 0:
            for copy in small_core_copies():
                copy.start()
        elif step == 1:
            for copy in small_core_copies():
                copy.wait()
            small_out_far[...] = small[far] + small_core[1]
            small_out[...] = small[pb] + small_core[0]
            small_far_copy().start()
        elif step == 2:
            small_far_copy().wait()
            small_out[...] = small_out[...] + small_far[...]
            small_out_slot[0] = small_out[...]
            small_slot_copy(0).start()
        else:
            level = step - 3
            small_slot_copy(level).wait()
            small_out[...] = small_out[...] + small_in[level]
            if level + 1 < levels:
                small_out_slot[level + 1] = small_out[...]
                small_slot_copy(level + 1).start()

    def stage(step, c):
        ring = lax.rem(c, 4)
        at = lax.rem(c, RING)
        if step == 0:
            for copy in core_copies(c) + loads(c):
                copy.start()
        elif step == 1:
            for copy in core_copies(c) + loads(c):
                copy.wait()
            add(far_out.at[ring], keep.at[ring, 1], core_in.at[ring, 1], rows)
            far_copy(c).start()
            add(far_keep.at[ring], keep.at[ring, 0], core_in.at[ring, 0], rows)
        elif step < 2 + levels:
            level = step - 2
            size = rows >> (level + 1)
            if level == 0:
                far_copy(c).wait()
                left, right = far_keep.at[ring], far_in.at[ring]
            else:
                halve_copy(level - 1, c).wait()
                left, right = half_keep[level - 1].at[ring], half_in[level - 1].at[ring]
            mine = pl.ds(pl.multiple_of(bits[level] * size, size), size)
            other = pl.ds(pl.multiple_of((1 - bits[level]) * size, size), size)
            add(half_out[level].at[ring], left.at[other], right.at[other], size)
            halve_copy(level, c).start()
            add(half_keep[level].at[ring], left.at[mine], right.at[mine], size)
        elif step == 2 + levels:
            level = levels - 1
            size = rows >> levels
            halve_copy(level, c).wait()
            offset = sum(bits[i] * (rows >> (i + 1)) for i in range(levels))
            where = pl.ds(pl.multiple_of(offset, size), size)
            add(full.at[at, where], half_keep[level].at[ring], half_in[level].at[ring], size)
            join_copy(level, c).start()
        elif step < 2 + 2 * levels:
            level = levels - 1 - (step - 3 - levels)
            join_copy(level, c).wait()
            join_copy(level - 1, c).start()
        elif step == 2 + 2 * levels:
            join_copy(0, c).wait()
            store(c).start()
        else:
            store(c).wait()

    stages = 4 + 2 * levels

    @pl.loop(0, count + stages - 1)
    def _(it):
        for step in range(3 + levels):

            @pl.when(it == step)
            def _():
                small_stage(step)

        for step in range(stages):
            c = it - step

            @pl.when(jnp.logical_and(c >= 0, c < count))
            def _():
                stage(step, c)


def sync_gradients(parts, small):
    slots = lax.axis_size("slot")
    count, size, rows, columns = parts.shape
    levels = slots.bit_length() - 1
    small_rows = small.shape[1:]
    low = jnp.bfloat16
    block = lambda *lead: pltpu.VMEM(lead + (columns,), low)
    halves = [block(4, rows >> (i + 1)) for i in range(levels)]
    return pl.pallas_call(
        functools.partial(sync_kernel, slots, count),
        out_shape=(
            jax.ShapeDtypeStruct((count, rows, columns), low),
            jax.ShapeDtypeStruct(small_rows, jnp.float32),
        ),
        in_specs=[
            pl.BlockSpec(memory_space=pl.ANY),
            pl.BlockSpec(memory_space=pltpu.VMEM),
        ],
        out_specs=(
            pl.BlockSpec(memory_space=pl.ANY),
            pl.BlockSpec(memory_space=pltpu.VMEM),
        ),
        scratch_shapes=[
            block(4, 2, rows),
            block(4, 2, rows),
            block(4, rows),
            block(4, rows),
            block(4, rows),
            halves,
            halves,
            halves,
            block(RING, rows),
            pltpu.VMEM((2,) + small_rows, jnp.float32),
            pltpu.VMEM(small_rows, jnp.float32),
            pltpu.VMEM((levels,) + small_rows, jnp.float32),
            pltpu.VMEM(small_rows, jnp.float32),
            pltpu.VMEM((levels,) + small_rows, jnp.float32),
            pltpu.SemaphoreType.DMA((2, 4)),
            pltpu.SemaphoreType.DMA((RING,)),
            pltpu.SemaphoreType.DMA((3 + 2 * levels, RING)),
            pltpu.SemaphoreType.DMA((3 + 2 * levels, RING)),
            pltpu.SemaphoreType.DMA((3 + levels,)),
            pltpu.SemaphoreType.DMA((3 + levels,)),
        ],
        compiler_params=pltpu.CompilerParams(
            collective_id=1, has_side_effects=True, vmem_limit_bytes=54 << 20
        ),
    )(parts, small)


def weight_grad_kernel(left, right, *rest):
    out = rest[-1]
    product = lax.dot_general(
        left[...], right[...], (((0,), (0,)), ((), ())), preferred_element_type=jnp.float32
    )
    out[0, 0] = product.astype(out.dtype)


def weight_grad(stack, left, right, first, tall=False):
    slots, parts = lax.axis_size("slot"), lax.axis_size("pb")
    rows = max(UNIT, 16 * slots)
    per = rows // UNIT
    tokens = left.shape[0]
    units = left.shape[1] * right.shape[1] // (D * D)
    left_map = (lambda k, p: (0, p * units + k)) if tall else (lambda k, p: (0, p))
    right_map = (lambda k, p: (0, 0)) if tall else (lambda k, p: (0, k))
    specs = [pl.BlockSpec((tokens, UNIT), left_map), pl.BlockSpec((tokens, D), right_map)]
    operands = [left, right]
    if stack is not None:
        specs.append(pl.BlockSpec(memory_space=pl.ANY))
        operands.append(stack)
    return pl.pallas_call(
        weight_grad_kernel,
        grid=(units, parts),
        out_shape=jax.ShapeDtypeStruct((UNITS // per, parts, rows, D), jnp.bfloat16),
        in_specs=specs,
        out_specs=pl.BlockSpec(
            (1, 1, UNIT, D),
            lambda k, p: ((first + k) // per, p, (first + k) % per, 0),
        ),
        input_output_aliases={2: 0} if stack is not None else {},
    )(*operands)


EVERY = ("slot", "pb")


def own_targets(targets, owner):
    serving = jnp.arange(targets.shape[1]) == owner[0, 0]
    own = jnp.sum(jnp.where(serving[:, None], targets[0], 0), axis=0)
    return jnp.concatenate([own, jnp.broadcast_to(owner[0, 0], (TGT_LEN,))])


def vocabulary_head(state_low, target_slots, owner_slots, questions, doc_scores, embed):
    slots, groups = lax.axis_size("slot"), lax.axis_size("pb")
    me = lax.axis_index("slot") * groups + lax.axis_index("pb")
    entries = embed.shape[0]
    tokens = slots * groups * TGT_LEN
    states = lax.all_gather(state_low, EVERY, axis=0, tiled=True)
    logits = matmul_nt(states, embed)
    hit = (
        target_slots.reshape(tokens, 1) - me * entries
        == lax.broadcasted_iota(jnp.int32, (tokens, entries), 1)
    )
    top = jnp.max(logits, axis=1)
    total = jnp.sum(jnp.exp(logits - top[:, None]), axis=1)
    pick = jnp.sum(jnp.where(hit, logits, 0.0), axis=1)
    own_score = jnp.broadcast_to(doc_scores.reshape(1), (TGT_LEN,))
    stats = lax.all_gather(jnp.concatenate([top, total, pick, own_score]), EVERY, axis=0)
    tops, totals = stats[:, :tokens], stats[:, tokens : 2 * tokens]
    scores = stats[:, 3 * tokens].reshape(slots, groups)
    best = jnp.max(tops, axis=0)
    log_total = best + jnp.log(jnp.sum(totals * jnp.exp(tops - best[None]), axis=0))
    picked = jnp.sum(stats[:, 2 * tokens : 3 * tokens], axis=0) - log_total
    picked = picked.reshape(slots, groups, TGT_LEN)
    owners = owner_slots.reshape(slots, groups)
    serving = owners[:, :, None] == jnp.arange(questions)
    score_terms = jnp.where(serving, scores[:, :, None], BIG_NEGATIVE)
    token_terms = jnp.where(
        serving[..., None], (scores[:, :, None] + picked)[:, :, None, :], BIG_NEGATIVE
    )
    score_top, token_top = jnp.max(score_terms, axis=0), jnp.max(token_terms, axis=0)
    score_norm = score_top + jnp.log(jnp.sum(jnp.exp(score_terms - score_top), axis=0))
    token_mix = token_top + jnp.log(jnp.sum(jnp.exp(token_terms - token_top), axis=0))
    group_tokens = questions * TGT_LEN
    count = groups * group_tokens
    losses = -jnp.sum(token_mix - score_norm[:, :, None], axis=(1, 2)) / group_tokens
    own_mix = jnp.sum(jnp.where(serving[..., None], token_mix[None], 0.0), axis=2)
    own_norm = jnp.sum(jnp.where(serving, score_norm[None], 0.0), axis=2)
    posterior = jnp.exp(scores[:, :, None] + picked - own_mix)
    prior = jnp.exp(scores - own_norm)
    token_grad = (-posterior / count).reshape(tokens, 1)
    score_grads = -jnp.sum(posterior - prior[:, :, None], axis=2) / count
    delta = to_low(
        token_grad * (jnp.where(hit, 1.0, 0.0) - jnp.exp(logits - log_total[:, None]))
    )
    grad_state = lax.psum_scatter(
        to_low(matmul(delta, embed)), EVERY, scatter_dimension=0, tiled=True
    ).astype(jnp.float32)
    slot, group = lax.axis_index("slot"), lax.axis_index("pb")
    loss = lax.dynamic_slice(losses, (group,), (1,))
    score_grad = lax.dynamic_slice(score_grads, (slot, group), (1, 1))
    return (loss, score_grad, grad_state, delta, states)


def local(
    enc_input,
    dec_input,
    doc_scores,
    owner,
    targets,
    enc_attn,
    enc_up,
    enc_down,
    enc_up_bias,
    enc_bias,
    enc_gain,
    dec_self,
    dec_cross,
    dec_up,
    dec_down,
    dec_up_bias,
    dec_bias,
    dec_gain,
    embed,
):
    pb_size = lax.axis_size("pb")
    width = D // pb_size
    vectors = (enc_up_bias, enc_bias, enc_gain, dec_up_bias, dec_bias, dec_gain)
    rows = [v.size // width for v in vectors]
    starts = [sum(rows[:i]) for i in range(len(rows) + 1)]
    passage_low = enc_input[0, 0]
    passage = passage_low.astype(jnp.float32)
    question_low = dec_input[0, 0]
    question = question_low.astype(jnp.float32)

    full = []
    ticker = Ticker()
    ticker.add(
        gather_small(jnp.concatenate([v.reshape(-1, width) for v in vectors]), ("pb",), full)
    )
    ticker.add(gather_rows(enc_attn, 1, full))
    ticker.tick()
    packed = full[0].astype(jnp.float32)
    unpacked = [packed[:, starts[i] : starts[i + 1], :] for i in range(len(rows))]
    encoder_upbias = unpacked[0].reshape(-1)
    encoder_bias = unpacked[1].transpose(1, 0, 2).reshape(-1, D)
    encoder_gain = unpacked[2].transpose(1, 0, 2).reshape(-1, D)
    decoder_upbias = unpacked[3].reshape(-1)
    decoder_bias = unpacked[4].transpose(1, 0, 2).reshape(-1, D)
    decoder_gain = unpacked[5].transpose(1, 0, 2).reshape(-1, D)
    ticker.add(gather_rows(enc_up, 0, full))
    ticker.tick()
    encoder_attn = full[1]
    ticker.add(gather_rows(enc_down, 0, full))
    attn_out, enc_saved = attend_forward(
        passage_low,
        passage_low,
        encoder_attn,
        encoder_bias[0],
        encoder_bias[1],
        encoder_bias[2],
        False,
    )
    attn_out = ticker.tick(attn_out)
    encoder_up = full[2]
    ticker.add(gather_rows(dec_self, 1, full))
    enc_first, enc_norm_one = norm_forward(passage + attn_out, encoder_gain[0], encoder_bias[3])
    enc_first_low = to_low(enc_first)
    enc_before = matmul(enc_first_low, encoder_up) + encoder_upbias
    enc_hidden_low = to_low(gelu_exact(enc_before))
    enc_hidden_low, enc_before = ticker.tick(enc_hidden_low, enc_before)
    encoder_down = full[3]
    ticker.add(gather_rows(dec_cross, 1, full))
    ticker.add(gather_small(own_targets(targets, owner), EVERY[::-1], full))
    ffn_out = matmul(enc_hidden_low, encoder_down) + encoder_bias[4]
    encoded, enc_norm_two = norm_forward(enc_first + ffn_out, encoder_gain[1], encoder_bias[5])
    memory_low = to_low(encoded)
    memory_low = ticker.tick(memory_low)
    decoder_self = full[4]
    targets_all = full[5]
    target_slots, owner_slots = targets_all[:, :TGT_LEN], targets_all[:, TGT_LEN]
    ticker.add(gather_rows(dec_up, 0, full))
    self_out, self_saved = attend_forward(
        question_low,
        question_low,
        decoder_self,
        decoder_bias[0],
        decoder_bias[1],
        decoder_bias[2],
        True,
    )
    dec_first, dec_norm_one = norm_forward(question + self_out, decoder_gain[0], decoder_bias[3])
    dec_first = ticker.tick(dec_first)
    dec_first_low = to_low(dec_first)
    decoder_cross = full[6]
    ticker.add(gather_rows(dec_down, 0, full))
    cross_out, cross_saved = attend_forward(
        dec_first_low,
        memory_low,
        decoder_cross,
        decoder_bias[4],
        decoder_bias[5],
        decoder_bias[6],
        False,
    )
    dec_second, dec_norm_two = norm_forward(dec_first + cross_out, decoder_gain[1], decoder_bias[7])
    dec_second = ticker.tick(dec_second)
    dec_second_low = to_low(dec_second)
    decoder_up = full[7]
    dec_before = matmul(dec_second_low, decoder_up) + decoder_upbias
    dec_hidden_low = to_low(gelu_exact(dec_before))
    dec_hidden_low, dec_before = ticker.tick(dec_hidden_low, dec_before)
    decoder_down = full[8]
    dec_ffn_out = matmul(dec_hidden_low, decoder_down) + decoder_bias[8]
    state, dec_norm_three = norm_forward(dec_second + dec_ffn_out, decoder_gain[2], decoder_bias[9])
    state_low = to_low(state)

    loss, score_grad, grad_state_sum, delta, states = vocabulary_head(
        state_low, target_slots, owner_slots, targets.shape[1], doc_scores, embed
    )

    embed_grad = matmul_tn(delta, states)
    grad_third, gain_third, shift_third = norm_backward(
        grad_state_sum, dec_norm_three, decoder_gain[2]
    )
    dec_downbias_grad = jnp.sum(grad_third, axis=0)
    third_low = to_low(grad_third)
    grad_before = hidden_backward(third_low, decoder_down, dec_before)
    dec_upbias_grad = jnp.sum(grad_before, axis=0)
    before_low = to_low(grad_before)
    grad_second, gain_second, shift_second = norm_backward(
        grad_third + matmul_nt(before_low, decoder_up), dec_norm_two, decoder_gain[1]
    )
    cross_query, grad_memory, dec_cross_pairs, cross_biases = attend_backward(
        grad_second, dec_first_low, memory_low, decoder_cross, cross_saved
    )
    grad_first, gain_first, shift_first = norm_backward(
        grad_second + cross_query, dec_norm_one, decoder_gain[0]
    )
    self_query, self_memory, dec_self_pairs, self_biases = attend_backward(
        grad_first, question_low, question_low, decoder_self, self_saved
    )
    question_grad = grad_first + self_query + self_memory
    enc_grad_two, enc_gain_two, enc_shift_two = norm_backward(
        grad_memory, enc_norm_two, encoder_gain[1]
    )
    enc_downbias_grad = jnp.sum(enc_grad_two, axis=0)
    enc_two_low = to_low(enc_grad_two)
    enc_grad_before = hidden_backward(enc_two_low, encoder_down, enc_before)
    enc_upbias_grad = jnp.sum(enc_grad_before, axis=0)
    enc_before_low = to_low(enc_grad_before)
    enc_grad_one, enc_gain_one, enc_shift_one = norm_backward(
        enc_grad_two + matmul_nt(enc_before_low, encoder_up), enc_norm_one, encoder_gain[0]
    )
    enc_query, enc_memory, enc_attn_pairs, enc_biases = attend_backward(
        enc_grad_one, passage_low, passage_low, encoder_attn, enc_saved
    )
    passage_grad = enc_grad_one + enc_query + enc_memory
    stack = weight_grad(None, dec_hidden_low, third_low, 24, tall=True)
    stack = weight_grad(stack, dec_second_low, before_low, 20)
    for i, (left, right) in enumerate(dec_cross_pairs):
        stack = weight_grad(stack, left, right, 16 + i)
    for i, (left, right) in enumerate(dec_self_pairs):
        stack = weight_grad(stack, left, right, 12 + i)
    stack = weight_grad(stack, enc_hidden_low, enc_two_low, 8, tall=True)
    stack = weight_grad(stack, enc_first_low, enc_before_low, 4)
    for i, (left, right) in enumerate(enc_attn_pairs):
        stack = weight_grad(stack, left, right, i)
    enc_bias_grad = jnp.stack(
        [
            enc_biases[0],
            enc_biases[1],
            enc_biases[2],
            enc_shift_one,
            enc_downbias_grad,
            enc_shift_two,
        ]
    )
    enc_gain_grad = jnp.stack([enc_gain_one, enc_gain_two])
    dec_bias_grad = jnp.stack(
        [
            self_biases[0],
            self_biases[1],
            self_biases[2],
            shift_first,
            cross_biases[0],
            cross_biases[1],
            cross_biases[2],
            shift_second,
            dec_downbias_grad,
            shift_third,
        ]
    )
    dec_gain_grad = jnp.stack([gain_first, gain_second, gain_third])
    vector_grads = jnp.concatenate(
        [
            enc_upbias_grad.reshape(pb_size, -1, width),
            enc_bias_grad.reshape(-1, pb_size, width).transpose(1, 0, 2),
            enc_gain_grad.reshape(-1, pb_size, width).transpose(1, 0, 2),
            dec_upbias_grad.reshape(pb_size, -1, width),
            dec_bias_grad.reshape(-1, pb_size, width).transpose(1, 0, 2),
            dec_gain_grad.reshape(-1, pb_size, width).transpose(1, 0, 2),
        ],
        axis=1,
    )
    spare = -starts[-1] % 32
    small = jnp.pad(vector_grads, ((0, 0), (0, spare), (0, 0))).reshape(pb_size, -1, D)
    summed_parts, small_sum = sync_gradients(stack, small)
    units = summed_parts.reshape(UNITS, width, D)
    square = lambda at: units[at : at + 4].astype(jnp.float32)
    wide = lambda at: jnp.concatenate([units[at + i].astype(jnp.float32) for i in range(4)], axis=1)
    tall = lambda at: square(at).reshape(-1, D)
    vector_sum = small_sum.reshape(-1, width)
    vector_out = [
        vector_sum[starts[i] : starts[i + 1]].reshape(v.shape) for i, v in enumerate(vectors)
    ]
    summed = (
        (square(0), wide(4), tall(8))
        + tuple(vector_out[:3])
        + (square(12), square(16), wide(20), tall(24))
        + tuple(vector_out[3:])
    )
    return (
        (
            loss,
            passage_grad.reshape(1, 1, SRC_LEN, D),
            question_grad.reshape(1, 1, TGT_LEN, D),
            score_grad,
        )
        + tuple(summed)
        + (embed_grad,)
    )


def solution(mesh):
    placed = (
        P("pb", "slot", None, None),
        P("pb", "slot", None, None),
        P("pb", "slot"),
        P("pb", "slot"),
        P("pb", None, None),
        P(None, "pb", None),
        P("pb", None),
        P("pb", None),
        P("pb"),
        P(None, "pb"),
        P(None, "pb"),
        P(None, "pb", None),
        P(None, "pb", None),
        P("pb", None),
        P("pb", None),
        P("pb"),
        P(None, "pb"),
        P(None, "pb"),
        P(("slot", "pb"), None),
    )
    return jax.shard_map(
        local,
        mesh=mesh,
        in_specs=placed,
        out_specs=(
            P("pb"),
            P("pb", "slot", None, None),
            P("pb", "slot", None, None),
            P("pb", "slot"),
            P(None, "pb", None),
            P("pb", None),
            P("pb", None),
            P("pb"),
            P(None, "pb"),
            P(None, "pb"),
            P(None, "pb", None),
            P(None, "pb", None),
            P("pb", None),
            P("pb", None),
            P("pb"),
            P(None, "pb"),
            P(None, "pb"),
            P(("slot", "pb"), None),
        ),
        check_vma=False,
    )
```

time: 3820 us -> 1320 us (0.35)
  waiting for transfers between devices: 3170 us -> 348 us
  Pallas kernels: 0 us -> 473 us
  matrix products: 400 us -> 259 us
  blocking collectives: 119 us -> 0 us
  local copies, waits for them, and re-layouts: 38.2 us -> 119 us
    reduce_scatter x10 -> x1, waiting for transfers between devices: 1960 us -> 121 us  [vocabulary_head(): lax.psum_scatter(to_low(matmul(delta, embed)), EVERY, scatter_dimension=0...]
    all_gather x8 -> x2, waiting for transfers between devices: 803 us -> 130 us  [the longest x1 76.3 us: vocabulary_head(): states = lax.all_gather(state_low, EVERY, axis=0, tiled=True)]
    pallas_call x0 -> x17, Pallas kernels: none -> 473 us  [the longest x1 366 us: sync_gradients(): pl.pallas_call(functools.partial(sync_kernel, slots, count), out_shape=(j...]
    psum x1 -> x0, waiting for transfers between devices: 401 us -> none  [local(): lax.psum(shortened(tuple(shares)), 'slot')]
    dot_general x17 -> x1, matrix products: 122 us -> 21.6 us  [matmul_tn(): lax.dot_general(left, right, (((0,), (0,)), ((), ())), preferred_element_...]
    ppermute x0 -> x42, waiting for transfers between devices: none -> 97.3 us  [swap(): return lax.ppermute(value, name, [(i, i ^ mask) for i in range(size)])]
    psum x2 -> x0, blocking collectives: 57.3 us -> none  [the longest x1 39.7 us: local(): lax.psum(shortened(tuple(shares)), 'slot')]
    dynamic_update_slice x0 -> x42, local copies, waits for them, and re-layouts: none -> 42.4 us  [gather_rows(): full = lax.dynamic_update_slice_in_dim(full, piece, start, axis)]
  transfers between devices with their start and end apart: 21 -> 45, of which waited for: 16 -> 12; matrix products, arithmetic and copies ran while one was open for 9% -> 14% of each run, Pallas kernels for 0% -> 0%
where the time goes in v1:
time: 1320 us; the launch traced here: 1300 us
  Pallas kernels  473 us (36%)
  waiting for transfers between devices  348 us (26%)
  matrix products  259 us (20%)
  local copies, waits for them, and re-layouts  119 us (9%)
  other arithmetic  59.3 us (4%)
  starting transfers between devices  25.5 us (2%)
  between operations  17.9 us (1%)
    pallas_call x1, Pallas kernels, sync_gradients(): pl.pallas_call(functools.partial(sync_kernel, slots, count), out_shape=(j...  366 us
    reduce_scatter x1, waiting for transfers between devices, vocabulary_head(): lax.psum_scatter(to_low(matmul(delta, embed)), EVERY, scatter_dimension=0...  121 us
    pallas_call x16, Pallas kernels, weight_grad(): pl.pallas_call(weight_grad_kernel, grid=(units, parts), out_shape=jax.Sha...  107 us
    dot_general x17, matrix products, matmul_nt(): lax.dot_general(left, right, (((1,), (1,)), ((), ())), preferred_element_...  104 us
    ppermute x42, waiting for transfers between devices, swap(): return lax.ppermute(value, name, [(i, i ^ mask) for i in range(size)])  97.3 us
    dot_general x17, matrix products, matmul(): return jnp.dot(left, right, preferred_element_type=jnp.float32)  80.1 us
    all_gather x1, waiting for transfers between devices, vocabulary_head(): states = lax.all_gather(state_low, EVERY, axis=0, tiled=True)  76.3 us
    all_gather x1, waiting for transfers between devices, vocabulary_head(): lax.all_gather(jnp.concatenate([top, total, pick, own_score]), EVERY, axi...  53.4 us
  transfers between devices with their start and end apart: 45, of which 12 were waited for; matrix products, arithmetic and copies ran while one was open for 14% of the time, Pallas kernels for 0%

profile of v1, /device:TPU:0, one launch (start us, length us, event | category | flops | bytes accessed | tf_op | source)
XLA Modules:
  0.0 1301.9 jit_solution(6900938329838547772)
XLA Ops:
  10.8 2.9 concatenate.49
  40.6 20.1 %collective-permute-done.1 = bf16[2,29,256]{2,1,0:T(8,128)(2,1)S(1)} collective-permute-done((bf16[2,29,256]{2,1,0:T(8,128)(2,1)S(1)}, bf16[2,29,256]{2,1,0:T(8,128)(2,1)S(1)}, u32[]{:S(2)}, u32[]{:S(2)}) %collective-permute-start.1) | collective-permute-done | bytes 29728 | tf_op jit(solution)/shard_map/ppermute | solution.py:147
  67.9 19.8 %collective-permute-done.5 = bf16[4,128,1024]{2,1,0:T(8,128)(2,1)} collective-permute-done((bf16[4,128,1024]{2,1,0:T(8,128)(2,1)}, bf16[4,128,1024]{2,1,0:T(8,128)(2,1)}, u32[]{:S(2)}, u32[]{:S(2)}) %collective-permute-start.5) | collective-permute-done | bytes 1048608 | tf_op jit(solution)/shard_map/ppermute | solution.py:147
  97.9 2.8 add_convert_fusion.2
  105.1 7.8 fusion.170
  112.9 3.7 collective-permute-done.10
  116.5 4.8 fusion.84
  121.4 3.4 fusion.82
  136.3 15.5 %collective-permute-done.15 = bf16[512,1024]{1,0:T(8,128)(2,1)} collective-permute-done((bf16[512,1024]{1,0:T(8,128)(2,1)}, bf16[512,1024]{1,0:T(8,128)(2,1)}, u32[]{:S(2)}, u32[]{:S(2)}) %collective-permute-start.15) | collective-permute-done | bytes 1048608 | tf_op jit(solution)/shard_map/ppermute | solution.py:147
  151.8 18.4 %fusion.6 = (bf16[384,4096]{1,0:T(8,128)(2,1)S(1)}, f32[384,4096]{1,0:T(8,128)}) fusion(f32[4096]{0:T(1024)S(1)} %bitcast.474, bf16[384,1024]{1,0:T(8,128)(2,1)S(1)} %fusion.90.left, bf16[1024,4096]{1,0:T(8,128)(2,1)S(1)} %constant_dynamic-update-slice_fusion.30), kind=kOutput, calls=%fused_computation.17 | convolution fusion | flops 3325034496 | bytes 18628608 | tf_op jit(solution)/shard_map/dot_general | solution.py:26
  180.6 16.2 %collective-permute-done.20 = bf16[4,128,1024]{2,1,0:T(8,128)(2,1)} collective-permute-done((bf16[4,128,1024]{2,1,0:T(8,128)(2,1)}, bf16[4,128,1024]{2,1,0:T(8,128)(2,1)}, u32[]{:S(2)}, u32[]{:S(2)}) %collective-permute-start.20) | collective-permute-done | bytes 1048608 | tf_op jit(solution)/shard_map/ppermute | solution.py:147
  196.9 3.7 fusion.171
  219.1 3.1 fusion.112
  224.7 4.5 collective-permute-done.30
  252.2 3.9 fusion.174
  256.1 3.1 convolution_convert_fusion.1
  273.3 14.6 %collective-permute-done.40 = bf16[512,1024]{1,0:T(8,128)(2,1)S(1)} collective-permute-done((bf16[512,1024]{1,0:T(8,128)(2,1)}, bf16[512,1024]{1,0:T(8,128)(2,1)S(1)}, u32[]{:S(2)}, u32[]{:S(2)}) %collective-permute-start.40) | collective-permute-done | bytes 1048608 | tf_op jit(solution)/shard_map/ppermute | solution.py:147
  287.9 7.0 fusion.37
  307.2 76.3 %all-gather.5.cloned.1.call-done = bf16[4096,1024]{1,0:T(8,128)(2,1)} async-done(((bf16[128,1024]{1,0:T(8,128)(2,1)}), bf16[4096,1024]{1,0:T(8,128)(2,1)}) %all-gather.5.cloned.1.call-update) | async-done | bytes 8388624 | tf_op jit(solution)/shard_map/all_gather | solution.py:560
  383.5 20.3 %fusion.177 = (f32[4096]{0:T(1024)S(1)}, f32[4096,1536]{0,1:T(8,128)}) fusion(bf16[4096,1024]{1,0:T(8,128)(2,1)} %all-gather.5.cloned.1.call-done, bf16[1536,1024]{1,0:T(8,128)(2,1)S(1)} %copy-done), kind=kOutput, calls=%fused_computation.434 | convolution fusion | flops 12891189248 | bytes 36716544 | tf_op jit(solution)/shard_map/dot_general | solution.py:30
  403.8 11.6 exponential_reduce_fusion
  416.5 53.4 %all-gather.7.cloned.1.call-done = f32[32,1,12416]{2,1,0:T(1,128)} async-done(((f32[1,1,12416]{2,1,0:T(1,128)}), f32[32,1,12416]{2,1,0:T(1,128)}) %all-gather.7.cloned.1.call-update) | async-done | bytes 1589264 | tf_op jit(solution)/shard_map/all_gather | solution.py:570
  475.3 22.9 %convolution_convert_fusion = bf16[4096,1024]{1,0:T(8,128)(2,1)} fusion(bf16[1536,1024]{1,0:T(8,128)(2,1)S(1)} %copy-done, f32[4096,1536]{0,1:T(8,128)} %get-tuple-element.327, f32[4096]{0:T(1024)S(1)} %get-tuple-element.247, f32[4096]{0:T(1024)S(1)} %negate_multiply_fusion.4, s32[4096]{0:T(1024)S(1)} %subtract_bitcast_fusion), kind=kOutput, calls=%fused_computation.14 | convolution fusion | flops 12926844928 | bytes 36749312 | tf_op jit(solution)/shard_map/dot_general | solution.py:26
  503.7 21.6 %fusion.148 = f32[1536,1024]{1,0:T(8,128)} fusion(bf16[4096,1024]{1,0:T(8,128)(2,1)} %all-gather.5.cloned.1.call-done, f32[4096,1536]{0,1:T(8,128)} %get-tuple-element.327, f32[4096]{0:T(1024)S(1)} %get-tuple-element.247, f32[4096]{0:T(1024)S(1)} %negate_multiply_fusion.4, s32[4096]{0:T(1024)S(1)} %subtract_bitcast_fusion), kind=kOutput, calls=%fused_computation.408 | convolution fusion | flops 12922650624 | bytes 39895040 | tf_op jit(solution)/shard_map/dot_general | solution.py:36
  525.3 120.9 %reduce-scatter.2.cloned.1.call-done = bf16[128,1024]{1,0:T(8,128)(2,1)} async-done(((bf16[4096,1024]{1,0:T(8,128)(2,1)}), bf16[128,1024]{1,0:T(8,128)(2,1)}) %reduce-scatter.2.cloned.1.call-update) | async-done | bytes 262160 | tf_op jit(solution)/shard_map/reduce_scatter | solution.py:598
  649.8 10.5 fusion.153
  660.3 6.8 multiply_reduce_fusion.13
  667.4 2.7 fusion.109
  670.3 3.8 bitcast_convert_fusion.4
  676.6 4.1 fusion.72
  694.8 3.2 fusion.64
  699.9 3.2 fusion.103
  706.3 3.8 multiply_reduce_fusion.4
  710.8 21.1 %fusion.157 = (f32[4096]{0:T(1024)S(1)}, bf16[384,4096]{1,0:T(8,128)(2,1)S(1)}) fusion(f32[384,4096]{1,0:T(8,128)} %get-tuple-element.165, bf16[384,1024]{1,0:T(8,128)(2,1)S(1)} %convert_element_type.302.right, bf16[4096,1024]{1,0:T(8,128)(2,1)} %copy-done.24), kind=kOutput, calls=%fused_computation.415 | convolution fusion | flops 3336040448 | bytes 18628608 | tf_op jit(solution)/shard_map/dot_general | solution.py:30
  732.0 3.9 multiply_reduce_fusion.5
  736.6 4.2 fusion.88
  742.3 6.6 bitcast_convert_fusion.2
  750.1 3.8 fusion.56
  753.8 7.0 multiply_reduce_fusion
  760.9 10.5 multiply_convert_fusion.1
  771.3 4.3 multiply_convert_fusion.3
  777.7 3.9 fusion.58
  781.6 12.1 shard_map.322.rest_0_
  800.8 12.4 shard_map.323.rest_0_
  813.3 4.1 shard_map.324.rest_0_
  817.4 4.7 shard_map.325.rest_0_
  822.1 4.7 shard_map.326.rest_0_
  826.8 4.1 shard_map.327.rest_0_
  830.9 4.2 shard_map.328.rest_0_
  835.1 4.1 shard_map.329.rest_0_
  839.1 4.1 shard_map.330.rest_0_
  843.3 4.1 shard_map.331.rest_0_
  847.3 14.4 %shard_map.332.rest_0_ = bf16[28,4,256,1024]{3,2,1,0:T(8,128)(2,1)} custom-call(bf16[384,4096]{1,0:T(8,128)(2,1)} %copy-done.45, bf16[384,1024]{1,0:T(8,128)(2,1)} %copy-done.48, bf16[28,4,256,1024]{3,2,1,0:T(8,128)(2,1)} %shard_map.331.rest_0_), custom_call_target="tpu_custom_call", output_to_operand_aliasing={{}: (2, {})} | custom-call | tf_op jit(solution)/shard_map/pallas_call | solution.py:533
  861.8 15.2 %shard_map.333.rest_0_ = bf16[28,4,256,1024]{3,2,1,0:T(8,128)(2,1)} custom-call(bf16[384,1024]{1,0:T(8,128)(2,1)} %copy-done.47, bf16[384,4096]{1,0:T(8,128)(2,1)} %copy-done.46, bf16[28,4,256,1024]{3,2,1,0:T(8,128)(2,1)} %shard_map.332.rest_0_), custom_call_target="tpu_custom_call", output_to_operand_aliasing={{}: (2, {})} | custom-call | tf_op jit(solution)/shard_map/pallas_call | solution.py:533
  877.0 4.7 shard_map.334.rest_0_
  881.7 4.7 shard_map.335.rest_0_
  886.4 4.7 shard_map.336.rest_0_
  891.2 4.8 shard_map.337.parts
  895.9 365.9 %shard_map.338 = (bf16[28,256,1024]{2,1,0:T(8,128)(2,1)}, f32[8,1024]{1,0:T(8,128)}) custom-call(bf16[28,4,256,1024]{3,2,1,0:T(8,128)(2,1)} %shard_map.337.parts, f32[4,8,1024]{2,1,0:T(8,128)} %reshape.518.small), custom_call_target="tpu_custom_call" | custom-call | tf_op jit(solution)/shard_map/pallas_call | solution.py:470
  1266.5 2.7 slice_bitcast_fusion.93
  1269.1 7.7 fusion.161
  1279.5 2.7 bitcast_convert_fusion.1
  1282.3 4.0 fusion.101
  1286.2 3.9 add_bitcast_fusion
  (584 shorter events, 204.8 us)
Async XLA Ops:
  7.2 376.3 %copy-start = (bf16[1536,1024]{1,0:T(8,128)(2,1)S(1)}, bf16[1536,1024]{1,0:T(8,128)(2,1)}, u32[]{:S(2)}) copy-start(bf16[1536,1024]{1,0:T(8,128)(2,1)} %param.37) | copy-start | bytes 9437188
  7.2 376.3 %all-gather.5.cloned.1.call-start = ((), (), s32[]{:S(2)}) async-start(), calls=%async_computation.1 | async-start | bytes 8650752 | tf_op jit(solution)/shard_map/all_gather | solution.py:560
  8.9 17.2 %collective-permute-start.24 = (s32[1,256]{1,0:T(1,128)S(1)}, s32[1,256]{1,0:T(1,128)S(1)}, u32[]{:S(2)}, u32[]{:S(2)}) collective-permute-start(s32[1,256]{1,0:T(1,128)S(1)} %bitcast.485), channel_id=1, source_target_pairs={{0,1},{1,0},{2,3},{3,2},{4,5},{5,4},{6,7},{7,6},{8,9},{9,8},{10,11... | collective-permute-start | bytes 3080 | tf_op jit(solution)/shard_map/ppermute | solution.py:147
  13.7 22.5 %collective-permute-start = (bf16[1,29,256]{2,1,0:T(8,128)(2,1)S(1)}, bf16[1,29,256]{2,1,0:T(8,128)(2,1)S(1)}, u32[]{:S(2)}, u32[]{:S(2)}) collective-permute-start(bf16[1,29,256]{2,1,0:T(8,128)(2,1)S(1)} %bitcast.443), channel_id=1, source_target_pairs={{0,1},{1,0},{2,3},{3,2},{4,5},{5,4},{6,7},{7,6},{8,9},{9,8},{10,11... | collective-permute-start | bytes 44552 | tf_op jit(solution)/shard_map/ppermute | solution.py:147
  13.8 50.2 %collective-permute-start.2 = (bf16[4,256,1024]{2,1,0:T(8,128)(2,1)}, bf16[4,256,1024]{2,1,0:T(8,128)(2,1)}, u32[]{:S(2)}, u32[]{:S(2)}) collective-permute-start(bf16[4,256,1024]{2,1,0:T(8,128)(2,1)} %param.24), channel_id=1, source_target_pairs={{0,1},{1,0},{2,3},{3,2},{4,5},{5,4},{6,7},{7,6},{8,9},{9,8},{10,11... | collective-permute-start | bytes 6291464 | tf_op jit(solution)/shard_map/ppermute | solution.py:147
  14.2 75.3 %collective-permute-start.7 = (bf16[256,4096]{1,0:T(8,128)(2,1)}, bf16[256,4096]{1,0:T(8,128)(2,1)}, u32[]{:S(2)}, u32[]{:S(2)}) collective-permute-start(bf16[256,4096]{1,0:T(8,128)(2,1)} %param.25), channel_id=1, source_target_pairs={{0,1},{1,0},{2,3},{3,2},{4,5},{5,4},{6,7},{7,6},{8,9},{9,8},{10,11... | collective-permute-start | bytes 6291464 | tf_op jit(solution)/shard_map/ppermute | solution.py:147
  14.3 111.1 %collective-permute-start.12 = (bf16[1024,1024]{1,0:T(8,128)(2,1)}, bf16[1024,1024]{1,0:T(8,128)(2,1)}, u32[]{:S(2)}, u32[]{:S(2)}) collective-permute-start(bf16[1024,1024]{1,0:T(8,128)(2,1)} %param.26), channel_id=1, source_target_pairs={{0,1},{1,0},{2,3},{3,2},{4,5},{5,4},{6,7},{7,6},{8,9},{9,8},{10,11... | collective-permute-start | bytes 6291464 | tf_op jit(solution)/shard_map/ppermute | solution.py:147
  26.1 4.9 collective-permute-start.25
  31.0 3.9 collective-permute-start.26
  34.9 26.4 %collective-permute-start.3 = (bf16[4,128,1024]{2,1,0:T(8,128)(2,1)}, bf16[4,128,1024]{2,1,0:T(8,128)(2,1)}, u32[]{:S(2)}, u32[]{:S(2)}) collective-permute-start(bf16[4,128,1024]{2,1,0:T(8,128)(2,1)} %constant_dynamic-slice_fusion.6), channel_id=1, source_target_pairs={{0,2},{1,3},{2,0},{3,1},{4,6},{5,7},{6,4},{7,5},{8,10},{9,11},{10,... | collective-permute-start | bytes 3145736 | tf_op jit(solution)/shard_map/ppermute | solution.py:147
  36.2 3.7 collective-permute-start.27
  39.9 20.8 %collective-permute-start.1 = (bf16[2,29,256]{2,1,0:T(8,128)(2,1)S(1)}, bf16[2,29,256]{2,1,0:T(8,128)(2,1)S(1)}, u32[]{:S(2)}, u32[]{:S(2)}) collective-permute-start(bf16[2,29,256]{2,1,0:T(8,128)(2,1)S(1)} %pad_maximum_fusion.2), channel_id=1, source_target_pairs={{0,2},{1,3},{2,0},{3,1},{4,6},{5,7},{6,4},{7,5},{8,10},{9,11},{10,... | collective-permute-start | bytes 89096 | tf_op jit(solution)/shard_map/ppermute | solution.py:147
  60.7 28.3 %collective-permute-start.8 = (bf16[128,4096]{1,0:T(8,128)(2,1)}, bf16[128,4096]{1,0:T(8,128)(2,1)}, u32[]{:S(2)}, u32[]{:S(2)}) collective-permute-start(bf16[128,4096]{1,0:T(8,128)(2,1)} %constant_dynamic-slice_fusion.5), channel_id=1, source_target_pairs={{0,2},{1,3},{2,0},{3,1},{4,6},{5,7},{6,4},{7,5},{8,10},{9,11},{10,... | collective-permute-start | bytes 3145736 | tf_op jit(solution)/shard_map/ppermute | solution.py:147
  61.3 4.7 collective-permute-start.28
  64.0 23.7 %collective-permute-start.5 = (bf16[4,128,1024]{2,1,0:T(8,128)(2,1)}, bf16[4,128,1024]{2,1,0:T(8,128)(2,1)}, u32[]{:S(2)}, u32[]{:S(2)}) collective-permute-start(bf16[4,128,1024]{2,1,0:T(8,128)(2,1)} %collective-permute-done.3), channel_id=1, source_target_pairs={{0,4},{4,0},{8,12},{12,8},{16,20},{20,16},{24,28},{28,24},{1,5},{5... | collective-permute-start | bytes 3145736 | tf_op jit(solution)/shard_map/ppermute | solution.py:147
  66.6 24.7 %collective-permute-start.4 = (bf16[4,128,1024]{2,1,0:T(8,128)(2,1)}, bf16[4,128,1024]{2,1,0:T(8,128)(2,1)S(1)}, u32[]{:S(2)}, u32[]{:S(2)}) collective-permute-start(bf16[4,128,1024]{2,1,0:T(8,128)(2,1)} %collective-permute-done.3), channel_id=1, source_target_pairs={{0,1},{1,0},{2,3},{3,2},{4,5},{5,4},{6,7},{7,6},{8,9},{9,8},{10,11... | collective-permute-start | bytes 3145736 | tf_op jit(solution)/shard_map/ppermute | solution.py:147
  87.7 3.6 collective-permute-start.6
  87.7 109.1 %copy-start.82 = (f32[1,4,256]{2,0,1:T(1,128)}, f32[1,4,256]{2,0,1:T(1,128)S(1)}, u32[]{:S(2)}) copy-start(f32[1,4,256]{2,0,1:T(1,128)S(1)} %get-tuple-element.303) | copy-start | bytes 12292
  87.7 113.2 %copy-start.84 = (f32[1,4,256]{2,0,1:T(1,128)}, f32[1,4,256]{2,0,1:T(1,128)S(1)}, u32[]{:S(2)}) copy-start(f32[1,4,256]{2,0,1:T(1,128)S(1)} %get-tuple-element.302) | copy-start | bytes 12292
  88.3 45.8 %copy-start.106 = (f32[1,4,256]{2,0,1:T(1,128)}, f32[1,4,256]{2,0,1:T(1,128)S(1)}, u32[]{:S(2)}) copy-start(f32[1,4,256]{2,0,1:T(1,128)S(1)} %get-tuple-element.289) | copy-start | bytes 12292
  89.0 81.8 %collective-permute-start.17 = (bf16[4,256,1024]{2,1,0:T(8,128)(2,1)}, bf16[4,256,1024]{2,1,0:T(8,128)(2,1)}, u32[]{:S(2)}, u32[]{:S(2)}) collective-permute-start(bf16[4,256,1024]{2,1,0:T(8,128)(2,1)} %param.30), channel_id=1, source_target_pairs={{0,1},{1,0},{2,3},{3,2},{4,5},{5,4},{6,7},{7,6},{8,9},{9,8},{10,11... | collective-permute-start | bytes 6291464 | tf_op jit(solution)/shard_map/ppermute | solution.py:147
  89.6 35.2 %collective-permute-start.13 = (bf16[512,1024]{1,0:T(8,128)(2,1)}, bf16[512,1024]{1,0:T(8,128)(2,1)}, u32[]{:S(2)}, u32[]{:S(2)}) collective-permute-start(bf16[512,1024]{1,0:T(8,128)(2,1)} %constant_dynamic-slice_fusion.4), channel_id=1, source_target_pairs={{0,2},{1,3},{2,0},{3,1},{4,6},{5,7},{6,4},{7,5},{8,10},{9,11},{10,... | collective-permute-start | bytes 3145736 | tf_op jit(solution)/shard_map/ppermute | solution.py:147
  91.3 25.2 %collective-permute-start.10 = (bf16[128,4096]{1,0:T(8,128)(2,1)}, bf16[128,4096]{1,0:T(8,128)(2,1)}, u32[]{:S(2)}, u32[]{:S(2)}) collective-permute-start(bf16[128,4096]{1,0:T(8,128)(2,1)} %collective-permute-done.8), channel_id=1, source_target_pairs={{0,4},{4,0},{8,12},{12,8},{16,20},{20,16},{24,28},{28,24},{1,5},{5... | collective-permute-start | bytes 3145736 | tf_op jit(solution)/shard_map/ppermute | solution.py:147
  91.6 35.0 %collective-permute-start.9 = (bf16[128,4096]{1,0:T(8,128)(2,1)}, bf16[128,4096]{1,0:T(8,128)(2,1)}, u32[]{:S(2)}, u32[]{:S(2)}) collective-permute-start(bf16[128,4096]{1,0:T(8,128)(2,1)} %collective-permute-done.8), channel_id=1, source_target_pairs={{0,1},{1,0},{2,3},{3,2},{4,5},{5,4},{6,7},{7,6},{8,9},{9,8},{10,11... | collective-permute-start | bytes 3145736 | tf_op jit(solution)/shard_map/ppermute | solution.py:147
  116.5 10.1 collective-permute-start.11
  124.8 77.9 %collective-permute-start.22 = (bf16[4,256,1024]{2,1,0:T(8,128)(2,1)S(1)}, bf16[4,256,1024]{2,1,0:T(8,128)(2,1)S(1)}, u32[]{:S(2)}, u32[]{:S(2)}) collective-permute-start(bf16[4,256,1024]{2,1,0:T(8,128)(2,1)S(1)} %copy-done.36), channel_id=1, source_target_pairs={{0,1},{1,0},{2,3},{3,2},{4,5},{5,4},{6,7},{7,6},{8,9},{9,8},{10,11... | collective-permute-start | bytes 6291464 | tf_op jit(solution)/shard_map/ppermute | solution.py:147
  125.3 44.9 %collective-permute-start.18 = (bf16[4,128,1024]{2,1,0:T(8,128)(2,1)}, bf16[4,128,1024]{2,1,0:T(8,128)(2,1)}, u32[]{:S(2)}, u32[]{:S(2)}) collective-permute-start(bf16[4,128,1024]{2,1,0:T(8,128)(2,1)} %constant_dynamic-slice_fusion.3), channel_id=1, source_target_pairs={{0,2},{1,3},{2,0},{3,1},{4,6},{5,7},{6,4},{7,5},{8,10},{9,11},{10,... | collective-permute-start | bytes 3145736 | tf_op jit(solution)/shard_map/ppermute | solution.py:147
  126.7 25.2 %collective-permute-start.15 = (bf16[512,1024]{1,0:T(8,128)(2,1)}, bf16[512,1024]{1,0:T(8,128)(2,1)}, u32[]{:S(2)}, u32[]{:S(2)}) collective-permute-start(bf16[512,1024]{1,0:T(8,128)(2,1)} %collective-permute-done.13), channel_id=1, source_target_pairs={{0,4},{4,0},{8,12},{12,8},{16,20},{20,16},{24,28},{28,24},{1,5},{5... | collective-permute-start | bytes 3145736 | tf_op jit(solution)/shard_map/ppermute | solution.py:147
  126.9 44.6 %collective-permute-start.14 = (bf16[512,1024]{1,0:T(8,128)(2,1)}, bf16[512,1024]{1,0:T(8,128)(2,1)}, u32[]{:S(2)}, u32[]{:S(2)}) collective-permute-start(bf16[512,1024]{1,0:T(8,128)(2,1)} %collective-permute-done.13), channel_id=1, source_target_pairs={{0,1},{1,0},{2,3},{3,2},{4,5},{5,4},{6,7},{7,6},{8,9},{9,8},{10,11... | collective-permute-start | bytes 3145736 | tf_op jit(solution)/shard_map/ppermute | solution.py:147
  127.2 69.6 %copy-start.6 = (f32[384,1024]{1,0:T(8,128)}, f32[384,1024]{1,0:T(8,128)S(1)}, u32[]{:S(2)}) copy-start(f32[384,1024]{1,0:T(8,128)S(1)} %get-tuple-element.249) | copy-start | bytes 4718596
  127.2 69.6 %copy-start.88 = (f32[384]{0:T(512)}, f32[384]{0:T(512)S(1)}, u32[]{:S(2)}) copy-start(f32[384]{0:T(512)S(1)} %broadcast_multiply_fusion.5) | copy-start | bytes 4612
  127.5 69.3 %copy-start.96 = (f32[384]{0:T(512)}, f32[384]{0:T(512)S(1)}, u32[]{:S(2)}) copy-start(f32[384]{0:T(512)S(1)} %add_rsqrt_fusion.1) | copy-start | bytes 4612
  134.5 35.7 %copy-start.47 = (bf16[384,1024]{1,0:T(8,128)(2,1)}, bf16[384,1024]{1,0:T(8,128)(2,1)S(1)}, u32[]{:S(2)}) copy-start(bf16[384,1024]{1,0:T(8,128)(2,1)S(1)} %fusion.90.left) | copy-start | bytes 2359300
  136.3 33.9 %copy-start.23 = (bf16[1024,4096]{1,0:T(8,128)(2,1)}, bf16[1024,4096]{1,0:T(8,128)(2,1)S(1)}, u32[]{:S(2)}) copy-start(bf16[1024,4096]{1,0:T(8,128)(2,1)S(1)} %constant_dynamic-update-slice_fusion.30) | copy-start | bytes 25165828
  151.8 19.7 %collective-permute-start.16 = (bf16[512,1024]{1,0:T(8,128)(2,1)}, bf16[512,1024]{1,0:T(8,128)(2,1)S(1)}, u32[]{:S(2)}, u32[]{:S(2)}) collective-permute-start(bf16[512,1024]{1,0:T(8,128)(2,1)} %collective-permute-done.15), channel_id=1, source_target_pairs={{0,1},{1,0},{2,3},{3,2},{4,5},{5,4},{6,7},{7,6},{8,9},{9,8},{10,11... | collective-permute-start | bytes 3145736 | tf_op jit(solution)/shard_map/ppermute | solution.py:147
  170.2 26.6 %copy-start.45 = (bf16[384,4096]{1,0:T(8,128)(2,1)}, bf16[384,4096]{1,0:T(8,128)(2,1)S(1)}, u32[]{:S(2)}) copy-start(bf16[384,4096]{1,0:T(8,128)(2,1)S(1)} %get-tuple-element.116.left) | copy-start | bytes 9437188
  170.2 62.4 %collective-permute-start.32 = (bf16[256,4096]{1,0:T(8,128)(2,1)}, bf16[256,4096]{1,0:T(8,128)(2,1)}, u32[]{:S(2)}, u32[]{:S(2)}) collective-permute-start(bf16[256,4096]{1,0:T(8,128)(2,1)} %param.32), channel_id=1, source_target_pairs={{0,1},{1,0},{2,3},{3,2},{4,5},{5,4},{6,7},{7,6},{8,9},{9,8},{10,11... | collective-permute-start | bytes 6291464 | tf_op jit(solution)/shard_map/ppermute | solution.py:147
  170.8 31.4 %collective-permute-start.23 = (bf16[4,128,1024]{2,1,0:T(8,128)(2,1)}, bf16[4,128,1024]{2,1,0:T(8,128)(2,1)}, u32[]{:S(2)}, u32[]{:S(2)}) collective-permute-start(bf16[4,128,1024]{2,1,0:T(8,128)(2,1)} %constant_dynamic-slice_fusion.2), channel_id=1, source_target_pairs={{0,2},{1,3},{2,0},{3,1},{4,6},{5,7},{6,4},{7,5},{8,10},{9,11},{10,... | collective-permute-start | bytes 3145736 | tf_op jit(solution)/shard_map/ppermute | solution.py:147
  171.6 25.3 %collective-permute-start.20 = (bf16[4,128,1024]{2,1,0:T(8,128)(2,1)}, bf16[4,128,1024]{2,1,0:T(8,128)(2,1)}, u32[]{:S(2)}, u32[]{:S(2)}) collective-permute-start(bf16[4,128,1024]{2,1,0:T(8,128)(2,1)} %collective-permute-done.18), channel_id=1, source_target_pairs={{0,4},{4,0},{8,12},{12,8},{16,20},{20,16},{24,28},{28,24},{1,5},{5... | collective-permute-start | bytes 3145736 | tf_op jit(solution)/shard_map/ppermute | solution.py:147
  172.5 59.1 %copy-start.86 = (f32[1,4,256]{2,0,1:T(1,128)}, f32[1,4,256]{2,0,1:T(1,128)S(1)}, u32[]{:S(2)}) copy-start(f32[1,4,256]{2,0,1:T(1,128)S(1)} %get-tuple-element.297) | copy-start | bytes 12292
  172.5 89.6 %copy-start.80 = (f32[1,4,256]{2,0,1:T(1,128)}, f32[1,4,256]{2,0,1:T(1,128)S(1)}, u32[]{:S(2)}) copy-start(f32[1,4,256]{2,0,1:T(1,128)S(1)} %get-tuple-element.296) | copy-start | bytes 12292
  172.6 31.4 %collective-permute-start.19 = (bf16[4,128,1024]{2,1,0:T(8,128)(2,1)}, bf16[4,128,1024]{2,1,0:T(8,128)(2,1)}, u32[]{:S(2)}, u32[]{:S(2)}) collective-permute-start(bf16[4,128,1024]{2,1,0:T(8,128)(2,1)} %collective-permute-done.18), channel_id=1, source_target_pairs={{0,1},{1,0},{2,3},{3,2},{4,5},{5,4},{6,7},{7,6},{8,9},{9,8},{10,11... | collective-permute-start | bytes 3145736 | tf_op jit(solution)/shard_map/ppermute | solution.py:147
  196.8 7.2 collective-permute-start.21
  202.2 60.1 %collective-permute-start.37 = (bf16[1024,1024]{1,0:T(8,128)(2,1)}, bf16[1024,1024]{1,0:T(8,128)(2,1)}, u32[]{:S(2)}, u32[]{:S(2)}) collective-permute-start(bf16[1024,1024]{1,0:T(8,128)(2,1)} %param.33), channel_id=1, source_target_pairs={{0,1},{1,0},{2,3},{3,2},{4,5},{5,4},{6,7},{7,6},{8,9},{9,8},{10,11... | collective-permute-start | bytes 6291464 | tf_op jit(solution)/shard_map/ppermute | solution.py:147
  202.7 29.2 %collective-permute-start.33 = (bf16[128,4096]{1,0:T(8,128)(2,1)}, bf16[128,4096]{1,0:T(8,128)(2,1)}, u32[]{:S(2)}, u32[]{:S(2)}) collective-permute-start(bf16[128,4096]{1,0:T(8,128)(2,1)} %constant_dynamic-slice_fusion.1), channel_id=1, source_target_pairs={{0,2},{1,3},{2,0},{3,1},{4,6},{5,7},{6,4},{7,5},{8,10},{9,11},{10,... | collective-permute-start | bytes 3145736 | tf_op jit(solution)/shard_map/ppermute | solution.py:147
  204.0 25.2 %collective-permute-start.30 = (bf16[4,128,1024]{2,1,0:T(8,128)(2,1)}, bf16[4,128,1024]{2,1,0:T(8,128)(2,1)}, u32[]{:S(2)}, u32[]{:S(2)}) collective-permute-start(bf16[4,128,1024]{2,1,0:T(8,128)(2,1)} %collective-permute-done.23), channel_id=1, source_target_pairs={{0,4},{4,0},{8,12},{12,8},{16,20},{20,16},{24,28},{28,24},{1,5},{5... | collective-permute-start | bytes 3145736 | tf_op jit(solution)/shard_map/ppermute | solution.py:147
  204.3 28.4 %collective-permute-start.29 = (bf16[4,128,1024]{2,1,0:T(8,128)(2,1)}, bf16[4,128,1024]{2,1,0:T(8,128)(2,1)}, u32[]{:S(2)}, u32[]{:S(2)}) collective-permute-start(bf16[4,128,1024]{2,1,0:T(8,128)(2,1)} %collective-permute-done.23), channel_id=1, source_target_pairs={{0,1},{1,0},{2,3},{3,2},{4,5},{5,4},{6,7},{7,6},{8,9},{9,8},{10,11... | collective-permute-start | bytes 3145736 | tf_op jit(solution)/shard_map/ppermute | solution.py:147
  229.2 3.5 collective-permute-start.31
  231.9 30.4 %collective-permute-start.38 = (bf16[512,1024]{1,0:T(8,128)(2,1)}, bf16[512,1024]{1,0:T(8,128)(2,1)}, u32[]{:S(2)}, u32[]{:S(2)}) collective-permute-start(bf16[512,1024]{1,0:T(8,128)(2,1)} %constant_dynamic-slice_fusion), channel_id=1, source_target_pairs={{0,2},{1,3},{2,0},{3,1},{4,6},{5,7},{6,4},{7,5},{8,10},{9,11},{10,... | collective-permute-start | bytes 3145736 | tf_op jit(solution)/shard_map/ppermute | solution.py:147
  232.7 26.5 %collective-permute-start.35 = (bf16[128,4096]{1,0:T(8,128)(2,1)}, bf16[128,4096]{1,0:T(8,128)(2,1)}, u32[]{:S(2)}, u32[]{:S(2)}) collective-permute-start(bf16[128,4096]{1,0:T(8,128)(2,1)} %collective-permute-done.33), channel_id=1, source_target_pairs={{0,4},{4,0},{8,12},{12,8},{16,20},{20,16},{24,28},{28,24},{1,5},{5... | collective-permute-start | bytes 3145736 | tf_op jit(solution)/shard_map/ppermute | solution.py:147
  233.0 29.3 %collective-permute-start.34 = (bf16[128,4096]{1,0:T(8,128)(2,1)}, bf16[128,4096]{1,0:T(8,128)(2,1)}, u32[]{:S(2)}, u32[]{:S(2)}) collective-permute-start(bf16[128,4096]{1,0:T(8,128)(2,1)} %collective-permute-done.33), channel_id=1, source_target_pairs={{0,1},{1,0},{2,3},{3,2},{4,5},{5,4},{6,7},{7,6},{8,9},{9,8},{10,11... | collective-permute-start | bytes 3145736 | tf_op jit(solution)/shard_map/ppermute | solution.py:147
  259.2 3.2 collective-permute-start.36
  262.4 25.5 %collective-permute-start.40 = (bf16[512,1024]{1,0:T(8,128)(2,1)}, bf16[512,1024]{1,0:T(8,128)(2,1)S(1)}, u32[]{:S(2)}, u32[]{:S(2)}) collective-permute-start(bf16[512,1024]{1,0:T(8,128)(2,1)} %collective-permute-done.38), channel_id=1, source_target_pairs={{0,4},{4,0},{8,12},{12,8},{16,20},{20,16},{24,28},{28,24},{1,5},{5... | collective-permute-start | bytes 3145736 | tf_op jit(solution)/shard_map/ppermute | solution.py:147
  264.2 30.7 %collective-permute-start.39 = (bf16[512,1024]{1,0:T(8,128)(2,1)}, bf16[512,1024]{1,0:T(8,128)(2,1)S(1)}, u32[]{:S(2)}, u32[]{:S(2)}) collective-permute-start(bf16[512,1024]{1,0:T(8,128)(2,1)} %collective-permute-done.38), channel_id=1, source_target_pairs={{0,1},{1,0},{2,3},{3,2},{4,5},{5,4},{6,7},{7,6},{8,9},{9,8},{10,11... | collective-permute-start | bytes 3145736 | tf_op jit(solution)/shard_map/ppermute | solution.py:147
  271.7 23.2 %copy-start.61 = (bf16[128,1024]{1,0:T(8,128)(2,1)}, bf16[128,1024]{1,0:T(8,128)(2,1)S(1)}, u32[]{:S(2)}) copy-start(bf16[128,1024]{1,0:T(8,128)(2,1)S(1)} %convert_element_type.286.left) | copy-start | bytes 786436
  273.3 21.6 %copy-start.4 = (bf16[1024,4096]{1,0:T(8,128)(2,1)}, bf16[1024,4096]{1,0:T(8,128)(2,1)S(1)}, u32[]{:S(2)}) copy-start(bf16[1024,4096]{1,0:T(8,128)(2,1)S(1)} %constant_dynamic-update-slice_fusion.6) | copy-start | bytes 25165828
  287.9 7.0 collective-permute-start.41
  306.5 163.3 %all-gather.7.cloned.1.call-start = ((), (), s32[]{:S(2)}) async-start(), calls=%async_computation.3 | async-start | bytes 1638912 | tf_op jit(solution)/shard_map/all_gather | solution.py:570
  416.1 230.0 %reduce-scatter.2.cloned.1.call-start = ((), (), s32[]{:S(2)}) async-start(), calls=%async_computation.2 | async-start | bytes 8650752 | tf_op jit(solution)/shard_map/reduce_scatter | solution.py:598
  503.7 142.5 %copy-start.17 = (f32[128,1024]{1,0:T(8,128)S(1)}, f32[128,1024]{1,0:T(8,128)}, u32[]{:S(2)}) copy-start(f32[128,1024]{1,0:T(8,128)} %copy-done.16) | copy-start | bytes 1572868
  699.5 96.2 %copy-start.51 = (bf16[16,64,128]{2,1,0:T(8,128)(2,1)}, bf16[16,64,128]{2,1,0:T(8,128)(2,1)S(1)}, u32[]{:S(2)}) copy-start(bf16[16,64,128]{2,1,0:T(8,128)(2,1)S(1)} %fusion.108) | copy-start | bytes 786436
  710.1 21.8 %slice-start = ((s8[8388608]{0:T(1024)(128)(4,1)}), s8[4194304]{0:T(1024)(128)(4,1)S(1)}, s32[]{:S(2)}) async-start(s8[8388608]{0:T(1024)(128)(4,1)} %bitcast.378), calls=%async_computation.4 | async-start | bytes 8388608
  710.7 21.2 %copy-start.7 = (f32[384,1024]{1,0:T(8,128)S(1)}, f32[384,1024]{1,0:T(8,128)}, u32[]{:S(2)}) copy-start(f32[384,1024]{1,0:T(8,128)} %copy-done.6) | copy-start | bytes 4718596
  775.6 24.1 %copy-start.29 = (bf16[16,64,384]{2,1,0:T(8,128)(2,1)}, bf16[16,64,384]{2,1,0:T(8,128)(2,1)S(1)}, u32[]{:S(2)}) copy-start(bf16[16,64,384]{2,1,0:T(8,128)(2,1)S(1)} %multiply_convert_fusion.3) | copy-start | bytes 2359300
  (114 other events, 698.3 us)
Sparse Core Ops, SparseCore 0:
  306.6 76.8 all-gather.4
  416.3 53.5 all-gather.6
  498.4 147.7 reduce-scatter.1

commit v2 on v1

--- a/solution.py
+++ b/solution.py
@@ -14,7 +14,6 @@
 TGT_LEN = 128
 MESH = pl.DeviceIdType.MESH
 UNIT = 256
-UNITS = 28
 RING = 8
 
 
@@ -156,6 +155,15 @@
     return masks_below(lax.axis_size(name))
 
 
+def natural_order(held, name):
+    count = held.shape[0]
+    for mask in masks_of(name):
+        pairs = held.reshape((count // (2 * mask), 2, mask) + held.shape[1:])
+        turned = jnp.where(bit_of(name, mask) == 0, pairs, pairs[:, ::-1])
+        held = turned.reshape(held.shape)
+    return held
+
+
 class Ticker:
     def __init__(self):
         self.active = []
@@ -221,11 +229,7 @@
     held = value[None]
     for name in names:
         for mask in masks_of(name):
-            side = bit_of(name, mask)
-            came = swap(held, name, mask)
-            held = jnp.concatenate(
-                [jnp.where(side == 0, held, came), jnp.where(side == 0, came, held)], axis=0
-            )
+            held = jnp.concatenate([held, swap(held, name, mask)], axis=0)
     held = yield held
     box.append(held)
 
@@ -238,34 +242,11 @@
     return jnp.where((value // mask) % 2 == 0, value + mask, value - mask)
 
 
-def sync_kernel(
-    slots,
-    count,
-    parts,
-    small,
-    out,
-    small_out,
-    keep,
-    core_in,
-    far_out,
-    far_keep,
-    far_in,
-    half_out,
-    half_keep,
-    half_in,
-    full,
-    small_core,
-    small_far,
-    small_in,
-    small_out_far,
-    small_out_slot,
-    load_sem,
-    store_sem,
-    send_sem,
-    recv_sem,
-    small_send,
-    small_recv,
-):
+def sync_kernel(slots, count, plan, operands, small, out, small_out, scratch):
+    left_buffer, right_buffer, parts, core_in, far_out, far_keep, far_in = scratch[:7]
+    half_out, half_keep, half_in, full = scratch[7:11]
+    small_core, small_far, small_in, small_out_far, small_out_slot = scratch[11:16]
+    load_sem, store_sem, send_sem, recv_sem, small_send, small_recv = scratch[16:]
     masks = masks_below(slots)
     levels = len(masks)
     rows = full.shape[1]
@@ -293,17 +274,65 @@
     def core_copies(c):
         at = lax.rem(c, RING)
         ring = lax.rem(c, 4)
+        pair = lax.rem(c, 2)
         return (
-            remote(parts.at[c, core], core_in.at[ring, 0], 0, at, partners[0]),
-            remote(parts.at[c, far_core], core_in.at[ring, 1], 1, at, partners[0]),
+            remote(parts.at[pair, core], core_in.at[ring, 0], 0, at, partners[0]),
+            remote(parts.at[pair, far_core], core_in.at[ring, 1], 1, at, partners[0]),
         )
 
-    def loads(c):
-        ring = lax.rem(c, 4)
-        return (
-            pltpu.make_async_copy(parts.at[c, pb], keep.at[ring, 0], load_sem.at[0, ring]),
-            pltpu.make_async_copy(parts.at[c, far], keep.at[ring, 1], load_sem.at[1, ring]),
-        )
+    def load(unit):
+        pair = lax.rem(unit, 2)
+        for at, (left, right, k, tall) in enumerate(plan):
+
+            @pl.when(unit == at)
+            def _():
+                tokens = operands[left].shape[0]
+                rows_at = pl.ds(0, tokens)
+                if tall:
+                    for p in range(4):
+                        pltpu.make_async_copy(
+                            operands[left].at[:, pl.ds((4 * p + k) * UNIT, UNIT)],
+                            left_buffer.at[pair, rows_at, pl.ds(p * UNIT, UNIT)],
+                            load_sem.at[0, pair],
+                        ).start()
+                else:
+                    pltpu.make_async_copy(
+                        operands[left], left_buffer.at[pair, rows_at], load_sem.at[0, pair]
+                    ).start()
+                column = 0 if tall else k * D
+                pltpu.make_async_copy(
+                    operands[right].at[:, pl.ds(column, D)],
+                    right_buffer.at[pair, rows_at],
+                    load_sem.at[1, pair],
+                ).start()
+
+    def product(unit, chunk, offset):
+        pair = lax.rem(unit, 2)
+        lengths = [operands[left].shape[0] for left, _, _, _ in plan]
+        for tokens in sorted(set(lengths)):
+            among = functools.reduce(
+                jnp.logical_or, [unit == at for at, n in enumerate(lengths) if n == tokens]
+            )
+
+            @pl.when(among)
+            def _():
+                rows_at = pl.ds(0, tokens)
+                for i, buffer in enumerate((left_buffer, right_buffer)):
+                    whole = buffer.at[pair, rows_at]
+                    pltpu.make_async_copy(whole, whole, load_sem.at[i, pair]).wait()
+
+                @pl.loop(0, 4)
+                def _(p):
+                    columns = pl.ds(pl.multiple_of(p * UNIT, UNIT), UNIT)
+                    total = lax.dot_general(
+                        left_buffer[pair, rows_at, columns],
+                        right_buffer[pair, rows_at, :],
+                        (((0,), (0,)), ((), ())),
+                        preferred_element_type=jnp.float32,
+                    )
+                    parts[lax.rem(chunk, 2), p, pl.ds(offset, UNIT), :] = total.astype(
+                        parts.dtype
+                    )
 
     def far_copy(c):
         ring = lax.rem(c, 4)
@@ -399,16 +428,17 @@
 
     def stage(step, c):
         ring = lax.rem(c, 4)
+        pair = lax.rem(c, 2)
         at = lax.rem(c, RING)
         if step == 0:
-            for copy in core_copies(c) + loads(c):
+            for copy in core_copies(c):
                 copy.start()
         elif step == 1:
-            for copy in core_copies(c) + loads(c):
+            for copy in core_copies(c):
                 copy.wait()
-            add(far_out.at[ring], keep.at[ring, 1], core_in.at[ring, 1], rows)
+            add(far_out.at[ring], parts.at[pair, far], core_in.at[ring, 1], rows)
             far_copy(c).start()
-            add(far_keep.at[ring], keep.at[ring, 0], core_in.at[ring, 0], rows)
+            add(far_keep.at[ring], parts.at[pair, pb], core_in.at[ring, 0], rows)
         elif step < 2 + levels:
             level = step - 2
             size = rows >> (level + 1)
@@ -443,7 +473,10 @@
 
     stages = 4 + 2 * levels
 
-    @pl.loop(0, count + stages - 1)
+    per = rows // UNIT
+    load(jnp.int32(0))
+
+    @pl.loop(0, count + stages)
     def _(it):
         for step in range(3 + levels):
 
@@ -452,37 +485,53 @@
                 small_stage(step)
 
         for step in range(stages):
-            c = it - step
+            c = it - 1 - step
 
             @pl.when(jnp.logical_and(c >= 0, c < count))
             def _():
                 stage(step, c)
 
-
-def sync_gradients(parts, small):
+        for i in range(per):
+
+            @pl.when(it < count)
+            def _():
+                unit = it * per + i
+                load(unit + 1)
+                product(unit, it, i * UNIT)
+
+
+def sync_gradients(plan, operands, small):
     slots = lax.axis_size("slot")
-    count, size, rows, columns = parts.shape
+    rows, columns = max(UNIT, 16 * slots), D
+    count = len(plan) * UNIT // rows
     levels = slots.bit_length() - 1
     small_rows = small.shape[1:]
     low = jnp.bfloat16
+    longest = max(operand.shape[0] for operand in operands)
     block = lambda *lead: pltpu.VMEM(lead + (columns,), low)
     halves = [block(4, rows >> (i + 1)) for i in range(levels)]
+    used = len(operands)
+
+    def kernel(*refs):
+        small_ref, out, small_out = refs[used : used + 3]
+        sync_kernel(slots, count, plan, refs[:used], small_ref, out, small_out, refs[used + 3 :])
+
     return pl.pallas_call(
-        functools.partial(sync_kernel, slots, count),
+        kernel,
         out_shape=(
             jax.ShapeDtypeStruct((count, rows, columns), low),
             jax.ShapeDtypeStruct(small_rows, jnp.float32),
         ),
-        in_specs=[
-            pl.BlockSpec(memory_space=pl.ANY),
-            pl.BlockSpec(memory_space=pltpu.VMEM),
-        ],
+        in_specs=[pl.BlockSpec(memory_space=pl.ANY)] * used
+        + [pl.BlockSpec(memory_space=pltpu.VMEM)],
         out_specs=(
             pl.BlockSpec(memory_space=pl.ANY),
             pl.BlockSpec(memory_space=pltpu.VMEM),
         ),
         scratch_shapes=[
-            block(4, 2, rows),
+            block(2, longest),
+            block(2, longest),
+            block(2, 4, rows),
             block(4, 2, rows),
             block(4, rows),
             block(4, rows),
@@ -496,7 +545,7 @@
             pltpu.VMEM((levels,) + small_rows, jnp.float32),
             pltpu.VMEM(small_rows, jnp.float32),
             pltpu.VMEM((levels,) + small_rows, jnp.float32),
-            pltpu.SemaphoreType.DMA((2, 4)),
+            pltpu.SemaphoreType.DMA((2, 2)),
             pltpu.SemaphoreType.DMA((RING,)),
             pltpu.SemaphoreType.DMA((3 + 2 * levels, RING)),
             pltpu.SemaphoreType.DMA((3 + 2 * levels, RING)),
@@ -504,77 +553,299 @@
             pltpu.SemaphoreType.DMA((3 + levels,)),
         ],
         compiler_params=pltpu.CompilerParams(
-            collective_id=1, has_side_effects=True, vmem_limit_bytes=54 << 20
+            collective_id=1, has_side_effects=True, vmem_limit_bytes=56 << 20
         ),
-    )(parts, small)
-
-
-def weight_grad_kernel(left, right, *rest):
-    out = rest[-1]
-    product = lax.dot_general(
-        left[...], right[...], (((0,), (0,)), ((), ())), preferred_element_type=jnp.float32
-    )
-    out[0, 0] = product.astype(out.dtype)
-
-
-def weight_grad(stack, left, right, first, tall=False):
-    slots, parts = lax.axis_size("slot"), lax.axis_size("pb")
-    rows = max(UNIT, 16 * slots)
-    per = rows // UNIT
-    tokens = left.shape[0]
-    units = left.shape[1] * right.shape[1] // (D * D)
-    left_map = (lambda k, p: (0, p * units + k)) if tall else (lambda k, p: (0, p))
-    right_map = (lambda k, p: (0, 0)) if tall else (lambda k, p: (0, k))
-    specs = [pl.BlockSpec((tokens, UNIT), left_map), pl.BlockSpec((tokens, D), right_map)]
-    operands = [left, right]
-    if stack is not None:
-        specs.append(pl.BlockSpec(memory_space=pl.ANY))
-        operands.append(stack)
+    )(*operands, small)
+
+
+EVERY = ("slot", "pb")
+
+
+def code_bits():
+    return [("slot", mask) for mask in masks_below(lax.axis_size("slot"))[::-1]] + [
+        ("pb", mask) for mask in masks_below(lax.axis_size("pb"))[::-1]
+    ]
+
+
+def exchange_parts(bits):
+    slot_bits = [i for i, (name, mask) in enumerate(bits) if name == "slot"]
+    pb_bits = [i for i, (name, mask) in enumerate(bits) if name == "pb"]
+    high, low, far, near = slot_bits[:-1], slot_bits[-1:], pb_bits[:-1], pb_bits[-1:]
+    first, second = high + low + far + near, far + high + low + near
+    return [
+        (0, 256, first),
+        (256, 256, second),
+        (512, 256, first),
+        (768, 128, second),
+        (896, 128, low + far + high + near),
+    ]
+
+
+def partner_of(bit):
+    name, mask = bit
+    slot, pb = lax.axis_index("slot"), lax.axis_index("pb")
+    return (xor(slot, mask), pb) if name == "slot" else (slot, xor(pb, mask))
+
+
+def meet(partners):
+    barrier = pltpu.get_barrier_semaphore()
+    for partner in partners:
+        pl.semaphore_signal(barrier, inc=1, device_id=partner, device_id_type=MESH)
+    pl.semaphore_wait(barrier, len(partners))
+
+
+def within(held, count, fixed, value, columns):
+    lead = [pl.ds(0, 2) if i in held else 0 for i in range(count)]
+    if fixed is not None:
+        lead[fixed] = value
+    return tuple(lead) + (slice(None), columns)
+
+
+def gather_kernel(bits, parts, own, out, local_sem, send_sem, recv_sem):
+    count = len(bits)
+    partners = [partner_of(bit) for bit in bits]
+    meet(partners)
+    local = pltpu.make_async_copy(
+        own, out.at[within([], count, None, 0, slice(None))], local_sem
+    )
+    local.start()
+    pending = [None] * len(parts)
+    for step in range(count):
+        for p, (start, width, order) in enumerate(parts):
+            columns = pl.ds(start, width)
+            if step > 0:
+                pending[p].wait()
+            if step == 1 and p == 0:
+                local.wait()
+            bit = order[step]
+            held = order[:step]
+            source = (
+                own.at[:, columns] if step == 0 else out.at[within(held, count, None, 0, columns)]
+            )
+            pending[p] = pltpu.make_async_remote_copy(
+                src_ref=source,
+                dst_ref=out.at[within(held, count, bit, 1, columns)],
+                send_sem=send_sem.at[p, step],
+                recv_sem=recv_sem.at[p, step],
+                device_id=partners[bit],
+                device_id_type=MESH,
+            )
+            pending[p].start()
+    for copy in pending:
+        copy.wait()
+
+
+def gather_states(own):
+    bits = code_bits()
+    parts = exchange_parts(bits)
+    out = pl.pallas_call(
+        functools.partial(gather_kernel, bits, parts),
+        out_shape=jax.ShapeDtypeStruct((2,) * len(bits) + own.shape, own.dtype),
+        in_specs=[pl.BlockSpec(memory_space=pl.ANY)],
+        out_specs=pl.BlockSpec(memory_space=pl.ANY),
+        scratch_shapes=[
+            pltpu.SemaphoreType.DMA,
+            pltpu.SemaphoreType.DMA((len(parts), len(bits))),
+            pltpu.SemaphoreType.DMA((len(parts), len(bits))),
+        ],
+        compiler_params=pltpu.CompilerParams(collective_id=2, has_side_effects=True),
+    )(own)
+    return out.reshape(-1, own.shape[-1])
+
+
+def scatter_kernel(bits, parts, shares, out, held, near_in, came, load_sem, send_sem, recv_sem):
+    count = len(bits)
+    partners = [partner_of(bit) for bit in bits]
+    near = count - 1
+    meet(partners)
+
+    def codes(free):
+        out = [()]
+        for i in range(near):
+            out = [code + (bit,) for code in out for bit in ((0, 1) if i in free else (0,))]
+        return out
+
+    def add(target, left, right):
+        rows = target.shape[0]
+
+        @pl.loop(0, rows // 32)
+        def _(i):
+            at = pl.ds(pl.multiple_of(i * 32, 32), 32)
+            total = left[at, :].astype(jnp.float32) + right[at, :].astype(jnp.float32)
+            target[at, :] = total.astype(target.dtype)
+
+    pending = [None] * len(parts)
+    loads = [None] * len(parts)
+    for p, (start, width, order) in enumerate(parts):
+        columns = pl.ds(start, width)
+        every = list(range(near))
+        pending[p] = pltpu.make_async_remote_copy(
+            src_ref=shares.at[within(every, count, near, 1, columns)],
+            dst_ref=near_in[p],
+            send_sem=send_sem.at[p, 0],
+            recv_sem=recv_sem.at[p, 0],
+            device_id=partners[near],
+            device_id_type=MESH,
+        )
+        pending[p].start()
+        loads[p] = pltpu.make_async_copy(
+            shares.at[within(every, count, near, 0, columns)], held[p], load_sem.at[p]
+        )
+        loads[p].start()
+    for step in range(near):
+        for p, (start, width, order) in enumerate(parts):
+            turns = order[:-1][::-1]
+            bit = turns[step]
+            free = turns[step:]
+            left = turns[step + 1 :]
+            if step == 0:
+                loads[p].wait()
+            pending[p].wait()
+            arrived = near_in[p] if step == 0 else came[p][step - 1]
+
+            def merge(code):
+                other = code if step == 0 else tuple(code[i] for i in sorted(free))
+                add(held[p].at[code], held[p].at[code], arrived.at[other])
+
+            for code in codes(free):
+                if code[bit] == 1:
+                    merge(code)
+            lead = tuple(pl.ds(0, 2) if i in left else int(i == bit) for i in range(near))
+            pending[p] = pltpu.make_async_remote_copy(
+                src_ref=held[p].at[lead],
+                dst_ref=came[p][step],
+                send_sem=send_sem.at[p, step + 1],
+                recv_sem=recv_sem.at[p, step + 1],
+                device_id=partners[bit],
+                device_id_type=MESH,
+            )
+            pending[p].start()
+            for code in codes(free):
+                if code[bit] == 0:
+                    merge(code)
+    for p, (start, width, order) in enumerate(parts):
+        pending[p].wait()
+        mine = (0,) * near
+        out[:, pl.ds(start, width)] = held[p][mine].astype(jnp.float32) + came[p][near - 1][
+            ...
+        ].astype(jnp.float32)
+
+
+def scatter_states(shares):
+    bits = code_bits()
+    parts = exchange_parts(bits)
+    count = len(bits)
+    low = jnp.bfloat16
+    held = [pltpu.VMEM((2,) * (count - 1) + (TGT_LEN, width), low) for _, width, _ in parts]
+    came = [
+        [
+            pltpu.VMEM((2,) * (count - 2 - step) + (TGT_LEN, width), low)
+            for step in range(count - 1)
+        ]
+        for _, width, _ in parts
+    ]
     return pl.pallas_call(
-        weight_grad_kernel,
-        grid=(units, parts),
-        out_shape=jax.ShapeDtypeStruct((UNITS // per, parts, rows, D), jnp.bfloat16),
-        in_specs=specs,
-        out_specs=pl.BlockSpec(
-            (1, 1, UNIT, D),
-            lambda k, p: ((first + k) // per, p, (first + k) % per, 0),
+        functools.partial(scatter_kernel, bits, parts),
+        out_shape=jax.ShapeDtypeStruct((TGT_LEN, D), jnp.float32),
+        in_specs=[pl.BlockSpec(memory_space=pl.ANY)],
+        out_specs=pl.BlockSpec(memory_space=pltpu.VMEM),
+        scratch_shapes=[
+            held,
+            held,
+            came,
+            pltpu.SemaphoreType.DMA((len(parts),)),
+            pltpu.SemaphoreType.DMA((len(parts), count)),
+            pltpu.SemaphoreType.DMA((len(parts), count)),
+        ],
+        compiler_params=pltpu.CompilerParams(
+            collective_id=3, has_side_effects=True, vmem_limit_bytes=56 << 20
         ),
-        input_output_aliases={2: 0} if stack is not None else {},
-    )(*operands)
-
-
-EVERY = ("slot", "pb")
-
-
-def own_targets(targets, owner):
+    )(shares.reshape((2,) * count + (TGT_LEN, D)))
+
+
+def merge_kernel(bits, stats, out, came, sent, send_sem, recv_sem):
+    partners = [partner_of(bit) for bit in bits]
+    meet(partners)
+    count = len(bits)
+    size = 1 << count
+    out[...] = stats[...]
+    position = lax.broadcasted_iota(jnp.int32, (size, TGT_LEN), 0)
+    for step in range(count):
+        mask = 1 << (count - 1 - step)
+        sent[step] = out[...]
+        copy = pltpu.make_async_remote_copy(
+            src_ref=sent.at[step],
+            dst_ref=came.at[step],
+            send_sem=send_sem.at[step],
+            recv_sem=recv_sem.at[step],
+            device_id=partners[step],
+            device_id_type=MESH,
+        )
+        copy.start()
+        copy.wait()
+        lower = (position // mask) % 2 == 0
+        other = [
+            jnp.where(
+                lower,
+                pltpu.roll(came[step, i], size - mask, 0),
+                pltpu.roll(came[step, i], mask, 0),
+            )
+            for i in range(3)
+        ]
+        top = jnp.maximum(out[0], other[0])
+        out[1] = out[1] * jnp.exp(out[0] - top) + other[1] * jnp.exp(other[0] - top)
+        out[0] = top
+        out[2] = out[2] + other[2]
+
+
+def merge_stats(stats):
+    bits = code_bits()
+    shape = stats.shape
+    return pl.pallas_call(
+        functools.partial(merge_kernel, bits),
+        out_shape=jax.ShapeDtypeStruct(shape, jnp.float32),
+        in_specs=[pl.BlockSpec(memory_space=pltpu.VMEM)],
+        out_specs=pl.BlockSpec(memory_space=pltpu.VMEM),
+        scratch_shapes=[
+            pltpu.VMEM((len(bits),) + shape, jnp.float32),
+            pltpu.VMEM((len(bits),) + shape, jnp.float32),
+            pltpu.SemaphoreType.DMA((len(bits),)),
+            pltpu.SemaphoreType.DMA((len(bits),)),
+        ],
+        compiler_params=pltpu.CompilerParams(collective_id=4, has_side_effects=True),
+    )(stats)
+
+
+def own_facts(targets, owner, doc_scores):
     serving = jnp.arange(targets.shape[1]) == owner[0, 0]
     own = jnp.sum(jnp.where(serving[:, None], targets[0], 0), axis=0)
-    return jnp.concatenate([own, jnp.broadcast_to(owner[0, 0], (TGT_LEN,))])
-
-
-def vocabulary_head(state_low, target_slots, owner_slots, questions, doc_scores, embed):
+    half = (TGT_LEN // 2,)
+    return jnp.concatenate(
+        [
+            own.astype(jnp.float32),
+            jnp.broadcast_to(owner[0, 0].astype(jnp.float32), half),
+            jnp.broadcast_to(doc_scores[0, 0], half),
+        ]
+    )
+
+
+def vocabulary_head(state_low, facts, questions, embed):
     slots, groups = lax.axis_size("slot"), lax.axis_size("pb")
     me = lax.axis_index("slot") * groups + lax.axis_index("pb")
     entries = embed.shape[0]
     tokens = slots * groups * TGT_LEN
-    states = lax.all_gather(state_low, EVERY, axis=0, tiled=True)
+    target_ids = facts[:, :TGT_LEN].astype(jnp.int32).reshape(tokens, 1)
+    owners = facts[:, TGT_LEN].astype(jnp.int32).reshape(slots, groups)
+    scores = facts[:, TGT_LEN + TGT_LEN // 2].reshape(slots, groups)
+    states = gather_states(state_low)
     logits = matmul_nt(states, embed)
-    hit = (
-        target_slots.reshape(tokens, 1) - me * entries
-        == lax.broadcasted_iota(jnp.int32, (tokens, entries), 1)
-    )
+    hit = target_ids - me * entries == lax.broadcasted_iota(jnp.int32, (tokens, entries), 1)
     top = jnp.max(logits, axis=1)
     total = jnp.sum(jnp.exp(logits - top[:, None]), axis=1)
     pick = jnp.sum(jnp.where(hit, logits, 0.0), axis=1)
-    own_score = jnp.broadcast_to(doc_scores.reshape(1), (TGT_LEN,))
-    stats = lax.all_gather(jnp.concatenate([top, total, pick, own_score]), EVERY, axis=0)
-    tops, totals = stats[:, :tokens], stats[:, tokens : 2 * tokens]
-    scores = stats[:, 3 * tokens].reshape(slots, groups)
-    best = jnp.max(tops, axis=0)
-    log_total = best + jnp.log(jnp.sum(totals * jnp.exp(tops - best[None]), axis=0))
-    picked = jnp.sum(stats[:, 2 * tokens : 3 * tokens], axis=0) - log_total
-    picked = picked.reshape(slots, groups, TGT_LEN)
-    owners = owner_slots.reshape(slots, groups)
+    merged = merge_stats(jnp.stack([top, total, pick]).reshape(3, -1, TGT_LEN))
+    log_total = (merged[0] + jnp.log(merged[1])).reshape(tokens)
+    picked = merged[2].reshape(slots, groups, TGT_LEN) - log_total.reshape(slots, groups, TGT_LEN)
     serving = owners[:, :, None] == jnp.arange(questions)
     score_terms = jnp.where(serving, scores[:, :, None], BIG_NEGATIVE)
     token_terms = jnp.where(
@@ -595,13 +866,8 @@
     delta = to_low(
         token_grad * (jnp.where(hit, 1.0, 0.0) - jnp.exp(logits - log_total[:, None]))
     )
-    grad_state = lax.psum_scatter(
-        to_low(matmul(delta, embed)), EVERY, scatter_dimension=0, tiled=True
-    ).astype(jnp.float32)
-    slot, group = lax.axis_index("slot"), lax.axis_index("pb")
-    loss = lax.dynamic_slice(losses, (group,), (1,))
-    score_grad = lax.dynamic_slice(score_grads, (slot, group), (1, 1))
-    return (loss, score_grad, grad_state, delta, states)
+    grad_state = scatter_states(to_low(matmul(delta, embed)))
+    return (losses[:1], score_grads[:1, :1], grad_state, delta, states)
 
 
 def local(
@@ -642,7 +908,7 @@
     )
     ticker.add(gather_rows(enc_attn, 1, full))
     ticker.tick()
-    packed = full[0].astype(jnp.float32)
+    packed = natural_order(full[0], "pb").astype(jnp.float32)
     unpacked = [packed[:, starts[i] : starts[i + 1], :] for i in range(len(rows))]
     encoder_upbias = unpacked[0].reshape(-1)
     encoder_bias = unpacked[1].transpose(1, 0, 2).reshape(-1, D)
@@ -673,14 +939,13 @@
     enc_hidden_low, enc_before = ticker.tick(enc_hidden_low, enc_before)
     encoder_down = full[3]
     ticker.add(gather_rows(dec_cross, 1, full))
-    ticker.add(gather_small(own_targets(targets, owner), EVERY[::-1], full))
+    ticker.add(gather_small(own_facts(targets, owner, doc_scores), EVERY[::-1], full))
     ffn_out = matmul(enc_hidden_low, encoder_down) + encoder_bias[4]
     encoded, enc_norm_two = norm_forward(enc_first + ffn_out, encoder_gain[1], encoder_bias[5])
     memory_low = to_low(encoded)
     memory_low = ticker.tick(memory_low)
     decoder_self = full[4]
-    targets_all = full[5]
-    target_slots, owner_slots = targets_all[:, :TGT_LEN], targets_all[:, TGT_LEN]
+    facts = full[5]
     ticker.add(gather_rows(dec_up, 0, full))
     self_out, self_saved = attend_forward(
         question_low,
@@ -718,7 +983,7 @@
     state_low = to_low(state)
 
     loss, score_grad, grad_state_sum, delta, states = vocabulary_head(
-        state_low, target_slots, owner_slots, targets.shape[1], doc_scores, embed
+        state_low, facts, targets.shape[1], embed
     )
 
     embed_grad = matmul_tn(delta, states)
@@ -758,16 +1023,26 @@
         enc_grad_one, passage_low, passage_low, encoder_attn, enc_saved
     )
     passage_grad = enc_grad_one + enc_query + enc_memory
-    stack = weight_grad(None, dec_hidden_low, third_low, 24, tall=True)
-    stack = weight_grad(stack, dec_second_low, before_low, 20)
-    for i, (left, right) in enumerate(dec_cross_pairs):
-        stack = weight_grad(stack, left, right, 16 + i)
-    for i, (left, right) in enumerate(dec_self_pairs):
-        stack = weight_grad(stack, left, right, 12 + i)
-    stack = weight_grad(stack, enc_hidden_low, enc_two_low, 8, tall=True)
-    stack = weight_grad(stack, enc_first_low, enc_before_low, 4)
-    for i, (left, right) in enumerate(enc_attn_pairs):
-        stack = weight_grad(stack, left, right, i)
+    operands, plan = [], []
+
+    def share(left, right, tall=False):
+        where = []
+        for operand in (left, right):
+            known = [i for i, other in enumerate(operands) if other is operand]
+            where.append(known[0] if known else len(operands))
+            if not known:
+                operands.append(operand)
+        for i in range(left.shape[1] * right.shape[1] // (D * D)):
+            plan.append((where[0], where[1], i, tall))
+
+    for left, right in enc_attn_pairs:
+        share(left, right)
+    share(enc_first_low, enc_before_low)
+    share(enc_hidden_low, enc_two_low, tall=True)
+    for left, right in dec_self_pairs + dec_cross_pairs:
+        share(left, right)
+    share(dec_second_low, before_low)
+    share(dec_hidden_low, third_low, tall=True)
     enc_bias_grad = jnp.stack(
         [
             enc_biases[0],
@@ -807,8 +1082,8 @@
     )
     spare = -starts[-1] % 32
     small = jnp.pad(vector_grads, ((0, 0), (0, spare), (0, 0))).reshape(pb_size, -1, D)
-    summed_parts, small_sum = sync_gradients(stack, small)
-    units = summed_parts.reshape(UNITS, width, D)
+    summed_parts, small_sum = sync_gradients(plan, operands, small)
+    units = summed_parts.reshape(-1, width, D)
     square = lambda at: units[at : at + 4].astype(jnp.float32)
     wide = lambda at: jnp.concatenate([units[at + i].astype(jnp.float32) for i in range(4)], axis=1)
     tall = lambda at: square(at).reshape(-1, D)

time: 1320 us -> 1080 us (0.82)
  waiting for transfers between devices: 348 us -> 89.6 us
  Pallas kernels: 473 us -> 501 us
    all_gather x2 -> x0, waiting for transfers between devices: 130 us -> none  [the longest x1 76.3 us: vocabulary_head(): states = lax.all_gather(state_low, EVERY, axis=0, tiled=True)]
    reduce_scatter x1 -> x0, waiting for transfers between devices: 121 us -> none  [vocabulary_head(): lax.psum_scatter(to_low(matmul(delta, embed)), EVERY, scatter_dimension=0...]
    pallas_call x17 -> x4, Pallas kernels: 473 us -> 501 us  [the longest x1 375 us: sync_gradients(): pl.pallas_call(kernel, out_shape=(jax.ShapeDtypeStruct((count, rows, colu...]
  transfers between devices with their start and end apart: 45 -> 42, of which waited for: 12 -> 9; matrix products, arithmetic and copies ran while one was open for 14% -> 15% of each run, Pallas kernels for 0% -> 0%
where the time goes in v2:
time: 1080 us; the launch traced here: 1060 us
  Pallas kernels  501 us (46%)
  matrix products  256 us (24%)
  local copies, waits for them, and re-layouts  118 us (11%)
  waiting for transfers between devices  89.6 us (8%)
  other arithmetic  64.7 us (6%)
  starting transfers between devices  30.1 us (3%)
    pallas_call x1, Pallas kernels, sync_gradients(): pl.pallas_call(kernel, out_shape=(jax.ShapeDtypeStruct((count, rows, colu...  375 us
    dot_general x17, matrix products, matmul_nt(): lax.dot_general(left, right, (((1,), (1,)), ((), ())), preferred_element_...  101 us
    ppermute x42, waiting for transfers between devices, swap(): return lax.ppermute(value, name, [(i, i ^ mask) for i in range(size)])  89.6 us
    dot_general x17, matrix products, matmul(): return jnp.dot(left, right, preferred_element_type=jnp.float32)  78.3 us
    pallas_call x1, Pallas kernels, gather_states(): pl.pallas_call(functools.partial(gather_kernel, bits, parts), out_shape=j...  57.5 us
    pallas_call x1, Pallas kernels, scatter_states(): pl.pallas_call(functools.partial(scatter_kernel, bits, parts), out_shape=...  53.3 us
    dynamic_update_slice x42, local copies, waits for them, and re-layouts, gather_rows(): full = lax.dynamic_update_slice_in_dim(full, piece, start, axis)  43.3 us
    ppermute x42, starting transfers between devices, swap(): return lax.ppermute(value, name, [(i, i ^ mask) for i in range(size)])  30.1 us
  transfers between devices with their start and end apart: 42, of which 9 were waited for; matrix products, arithmetic and copies ran while one was open for 15% of the time, Pallas kernels for 0%

profile of v2, /device:TPU:0, one launch (start us, length us, event | category | flops | bytes accessed | tf_op | source)
XLA Modules:
  0.0 1064.9 jit_solution(13661298733207710143)
XLA Ops:
  5.0 2.9 concatenate.52
  10.7 2.5 collective-permute-start.3
  13.4 2.4 constant_dynamic-slice_fusion.4
  24.0 13.3 %collective-permute-done.25 = f32[2,256]{1,0:T(2,128)S(1)} collective-permute-done((f32[2,256]{1,0:T(2,128)S(1)}, f32[2,256]{1,0:T(2,128)S(1)}, u32[]{:S(2)}, u32[]{:S(2)}) %collective-permute-start.25) | collective-permute-done | bytes 2080 | tf_op jit(solution)/shard_map/ppermute | solution.py:146
  45.2 2.6 collective-permute-start.28
  53.1 24.0 %collective-permute-done.5 = bf16[4,128,1024]{2,1,0:T(8,128)(2,1)S(1)} collective-permute-done((bf16[4,128,1024]{2,1,0:T(8,128)(2,1)}, bf16[4,128,1024]{2,1,0:T(8,128)(2,1)S(1)}, u32[]{:S(2)}, u32[]{:S(2)}) %collective-permute-start.5) | collective-permute-done | bytes 1048608 | tf_op jit(solution)/shard_map/ppermute | solution.py:146
  86.1 2.8 add_convert_fusion.2
  93.3 7.8 fusion.171
  101.1 4.2 collective-permute-done.10
  105.2 4.8 fusion.84
  110.1 3.3 fusion.82
  125.2 14.4 %collective-permute-done.15 = bf16[512,1024]{1,0:T(8,128)(2,1)S(1)} collective-permute-done((bf16[512,1024]{1,0:T(8,128)(2,1)}, bf16[512,1024]{1,0:T(8,128)(2,1)S(1)}, u32[]{:S(2)}, u32[]{:S(2)}) %collective-permute-start.15) | collective-permute-done | bytes 1048608 | tf_op jit(solution)/shard_map/ppermute | solution.py:146
  139.6 18.6 %fusion.6 = (bf16[384,4096]{1,0:T(8,128)(2,1)}, f32[384,4096]{1,0:T(8,128)}) fusion(f32[4096]{0:T(1024)S(1)} %bitcast.514, bf16[384,1024]{1,0:T(8,128)(2,1)S(1)} %fusion.90.refs_6_, bf16[1024,4096]{1,0:T(8,128)(2,1)S(1)} %constant_dynamic-update-slice_fusion.30), kind=kOutput, calls=%fused_computation.17 | convolution fusion | flops 3325034496 | bytes 18628608 | tf_op jit(solution)/shard_map/dot_general | solution.py:25
  163.5 2.3 copy.181.refs_4_
  171.7 15.6 %collective-permute-done.20 = bf16[4,128,1024]{2,1,0:T(8,128)(2,1)} collective-permute-done((bf16[4,128,1024]{2,1,0:T(8,128)(2,1)}, bf16[4,128,1024]{2,1,0:T(8,128)(2,1)}, u32[]{:S(2)}, u32[]{:S(2)}) %collective-permute-start.20) | collective-permute-done | bytes 1048608 | tf_op jit(solution)/shard_map/ppermute | solution.py:146
  187.4 3.7 fusion.172
  211.3 2.5 fusion.173
  213.8 2.5 convolution_convert_fusion.2
  233.5 2.3 fusion.87
  240.0 2.4 copy.159
  242.4 2.3 copy.161
  244.7 3.9 fusion.175
  248.6 3.7 convolution_convert_fusion.1
  254.7 2.3 fusion.176
  268.0 14.8 %collective-permute-done.40 = bf16[512,1024]{1,0:T(8,128)(2,1)S(1)} collective-permute-done((bf16[512,1024]{1,0:T(8,128)(2,1)}, bf16[512,1024]{1,0:T(8,128)(2,1)S(1)}, u32[]{:S(2)}, u32[]{:S(2)}) %collective-permute-start.40) | collective-permute-done | bytes 1048608 | tf_op jit(solution)/shard_map/ppermute | solution.py:146
  282.8 7.0 fusion.37
  301.4 57.5 %shard_map.322 = bf16[2,2,2,2,2,128,1024]{6,5,4,3,2,1,0:T(8,128)(2,1)} custom-call(bf16[128,1024]{1,0:T(8,128)(2,1)} %add_convert_fusion.4.own), custom_call_target="tpu_custom_call" | custom-call | tf_op jit(solution)/shard_map/pallas_call | solution.py:641
  358.9 20.3 %fusion.178 = (f32[4096]{0:T(1024)S(1)}, f32[4096,1536]{0,1:T(8,128)}) fusion(bf16[4096,1024]{1,0:T(8,128)(2,1)} %bitcast.404, bf16[1536,1024]{1,0:T(8,128)(2,1)S(1)} %copy-done), kind=kOutput, calls=%fused_computation.421 | convolution fusion | flops 12891189248 | bytes 36716544 | tf_op jit(solution)/shard_map/dot_general | solution.py:29
  379.2 11.6 %exponential_reduce_fusion = (f32[4096]{0:T(1024)S(1)}, f32[4096]{0:T(1024)S(1)}) fusion(f32[4096,1536]{0,1:T(8,128)} %get-tuple-element.275, f32[4096]{0:T(1024)S(1)} %get-tuple-element.274, s32[4096]{0:T(1024)S(1)} %subtract_bitcast_fusion), kind=kLoop, calls=%fused_computation.6 | loop fusion | flops 31449088 | bytes 25231360 | tf_op jit(solution)/shard_map/reduce_sum | solution.py:844
  391.4 15.5 %shard_map.323 = f32[3,32,128]{2,1,0:T(8,128)} custom-call(f32[3,32,128]{2,1,0:T(8,128)} %pad_maximum_fusion.1.stats), custom_call_target="tpu_custom_call" | custom-call | tf_op jit(solution)/shard_map/pallas_call | solution.py:804
  410.2 21.8 %fusion.150 = f32[1536,1024]{1,0:T(8,128)} fusion(bf16[4096,1024]{1,0:T(8,128)(2,1)} %bitcast.405, f32[4096,1536]{0,1:T(8,128)} %get-tuple-element.275, f32[4096]{0:T(1024)S(1)} %get-tuple-element.205, f32[4096]{0:T(1024)S(1)} %get-tuple-element.204, s32[4096]{0:T(1024)S(1)} %subtract_bitcast_fusion), kind=kOutput, calls=%fused_computation.396 | convolution fusion | flops 12922650624 | bytes 39895040 | tf_op jit(solution)/shard_map/dot_general | solution.py:35
  432.0 22.4 %convolution_convert_fusion = bf16[4096,1024]{1,0:T(8,128)(2,1)} fusion(bf16[1536,1024]{1,0:T(8,128)(2,1)S(1)} %copy-done, f32[4096,1536]{0,1:T(8,128)} %get-tuple-element.275, f32[4096]{0:T(1024)S(1)} %get-tuple-element.205, f32[4096]{0:T(1024)S(1)} %get-tuple-element.204, s32[4096]{0:T(1024)S(1)} %subtract_bitcast_fusion), kind=kOutput, calls=%fused_computation.14 | convolution fusion | flops 12926844928 | bytes 36749312 | tf_op jit(solution)/shard_map/dot_general | solution.py:25
  454.3 53.3 %shard_map.324 = f32[128,1024]{1,0:T(8,128)} custom-call(bf16[2,2,2,2,2,128,1024]{6,5,4,3,2,1,0:T(8,128)(2,1)} %bitcast.406), custom_call_target="tpu_custom_call" | custom-call | tf_op jit(solution)/shard_map/pallas_call | solution.py:747
  511.5 9.9 fusion.154
  521.5 3.0 multiply_reduce_fusion.14
  524.9 2.7 fusion.109
  527.7 3.8 bitcast_convert_fusion.4
  531.5 2.5 copy.188.refs_20_
  534.0 4.1 fusion.72
  543.2 3.2 multiply_reduce_fusion.15
  547.5 2.5 fusion.110
  552.8 3.2 fusion.64
  557.8 3.2 fusion.103
  561.9 2.3 copy.187.refs_19_
  564.2 4.4 multiply_reduce_fusion.4
  569.4 20.9 %fusion.158 = (f32[4096]{0:T(1024)S(1)}, bf16[384,4096]{1,0:T(8,128)(2,1)S(1)}) fusion(f32[384,4096]{1,0:T(8,128)} %get-tuple-element.165, bf16[384,1024]{1,0:T(8,128)(2,1)S(1)} %convert_element_type.326.refs_9_, bf16[4096,1024]{1,0:T(8,128)(2,1)} %copy-done.20), kind=kOutput, calls=%fused_computation.403 | convolution fusion | flops 3336040448 | bytes 18628608 | tf_op jit(solution)/shard_map/dot_general | solution.py:29
  590.4 4.4 multiply_reduce_fusion.5
  595.5 3.8 fusion.88
  600.7 6.9 bitcast_convert_fusion.2
  607.6 2.4 copy.180.refs_3_
  610.0 4.0 fusion.56
  614.0 7.0 multiply_reduce_fusion
  621.0 10.5 multiply_convert_fusion.1
  631.5 4.3 multiply_convert_fusion.3
  639.0 3.8 fusion.58
  651.3 374.9 %shard_map.325 = (bf16[28,256,1024]{2,1,0:T(8,128)(2,1)}, f32[8,1024]{1,0:T(8,128)}) custom-call(bf16[384,1024]{1,0:T(8,128)(2,1)} %bitcast.413, bf16[384,1024]{1,0:T(8,128)(2,1)} %copy.178.refs_1_, bf16[384,1024]{1,0:T(8,128)(2,1)} %copy.179.refs_2_, bf16[384,1024]{1,0:T(8,128)(2,1)} %copy.180.refs_3_, bf16[384,1024]{1,0:T(8,128)(2,1)} %copy.181.refs_4_, ...), custom_call_target="tpu_custom_call" | custom-call | tf_op jit(solution)/shard_map/pallas_call | solution.py:519
  1030.8 4.2 slice_bitcast_fusion.93
  1035.0 8.8 fusion.162
  1045.2 4.2 bitcast_convert_fusion
  1049.4 2.7 bitcast_convert_fusion.1
  1052.1 3.3 fusion.101
  1055.4 4.0 add_bitcast_fusion
  1059.5 2.6 maximum_convert_fusion.1
  1062.1 2.5 maximum_convert_fusion
  (557 shorter events, 168.5 us)
Async XLA Ops:
  0.7 358.3 %copy-start = (bf16[1536,1024]{1,0:T(8,128)(2,1)S(1)}, bf16[1536,1024]{1,0:T(8,128)(2,1)}, u32[]{:S(2)}) copy-start(bf16[1536,1024]{1,0:T(8,128)(2,1)} %param.37) | copy-start | bytes 9437188
  3.1 19.5 %collective-permute-start.24 = (f32[1,256]{1,0:T(1,128)S(1)}, f32[1,256]{1,0:T(1,128)S(1)}, u32[]{:S(2)}, u32[]{:S(2)}) collective-permute-start(f32[1,256]{1,0:T(1,128)S(1)} %bitcast.489), channel_id=1, source_target_pairs={{0,1},{1,0},{2,3},{3,2},{4,5},{5,4},{6,7},{7,6},{8,9},{9,8},{10,11... | collective-permute-start | bytes 3080 | tf_op jit(solution)/shard_map/ppermute | solution.py:146
  7.9 35.2 %collective-permute-start = (bf16[1,29,256]{2,1,0:T(8,128)(2,1)S(1)}, bf16[1,29,256]{2,1,0:T(8,128)(2,1)S(1)}, u32[]{:S(2)}, u32[]{:S(2)}) collective-permute-start(bf16[1,29,256]{2,1,0:T(8,128)(2,1)S(1)} %bitcast.463), channel_id=1, source_target_pairs={{0,1},{1,0},{2,3},{3,2},{4,5},{5,4},{6,7},{7,6},{8,9},{9,8},{10,11... | collective-permute-start | bytes 44552 | tf_op jit(solution)/shard_map/ppermute | solution.py:146
  7.9 43.6 %collective-permute-start.2 = (bf16[4,256,1024]{2,1,0:T(8,128)(2,1)}, bf16[4,256,1024]{2,1,0:T(8,128)(2,1)}, u32[]{:S(2)}, u32[]{:S(2)}) collective-permute-start(bf16[4,256,1024]{2,1,0:T(8,128)(2,1)} %param.24), channel_id=1, source_target_pairs={{0,1},{1,0},{2,3},{3,2},{4,5},{5,4},{6,7},{7,6},{8,9},{9,8},{10,11... | collective-permute-start | bytes 6291464 | tf_op jit(solution)/shard_map/ppermute | solution.py:146
  10.7 40.8 %collective-permute-start.3 = (bf16[4,128,1024]{2,1,0:T(8,128)(2,1)}, bf16[4,128,1024]{2,1,0:T(8,128)(2,1)}, u32[]{:S(2)}, u32[]{:S(2)}) collective-permute-start(bf16[4,128,1024]{2,1,0:T(8,128)(2,1)} %constant_dynamic-slice_fusion.6), channel_id=1, source_target_pairs={{0,2},{1,3},{2,0},{3,1},{4,6},{5,7},{6,4},{7,5},{8,10},{9,11},{10,... | collective-permute-start | bytes 3145736 | tf_op jit(solution)/shard_map/ppermute | solution.py:146
  13.2 65.1 %collective-permute-start.7 = (bf16[256,4096]{1,0:T(8,128)(2,1)}, bf16[256,4096]{1,0:T(8,128)(2,1)}, u32[]{:S(2)}, u32[]{:S(2)}) collective-permute-start(bf16[256,4096]{1,0:T(8,128)(2,1)} %param.25), channel_id=1, source_target_pairs={{0,1},{1,0},{2,3},{3,2},{4,5},{5,4},{6,7},{7,6},{8,9},{9,8},{10,11... | collective-permute-start | bytes 6291464 | tf_op jit(solution)/shard_map/ppermute | solution.py:146
  22.6 14.7 %collective-permute-start.25 = (f32[2,256]{1,0:T(2,128)S(1)}, f32[2,256]{1,0:T(2,128)S(1)}, u32[]{:S(2)}, u32[]{:S(2)}) collective-permute-start(f32[2,256]{1,0:T(2,128)S(1)} %pad_maximum_fusion.5), channel_id=1, source_target_pairs={{0,2},{1,3},{2,0},{3,1},{4,6},{5,7},{6,4},{7,5},{8,10},{9,11},{10,... | collective-permute-start | bytes 6152 | tf_op jit(solution)/shard_map/ppermute | solution.py:146
  37.3 4.1 collective-permute-start.26
  41.4 3.7 collective-permute-start.27
  43.1 6.8 collective-permute-start.1
  45.2 4.7 collective-permute-start.28
  47.8 166.0 %copy-start.107 = (pred[128,128]{0,1:T(8,128)(4,1)}, pred[128,128]{0,1:T(8,128)(4,1)S(1)}, u32[]{:S(2)}) copy-start(pred[128,128]{0,1:T(8,128)(4,1)S(1)} %iota_compare_fusion.1) | copy-start | bytes 49156
  49.9 64.1 %collective-permute-start.12 = (bf16[1024,1024]{1,0:T(8,128)(2,1)}, bf16[1024,1024]{1,0:T(8,128)(2,1)}, u32[]{:S(2)}, u32[]{:S(2)}) collective-permute-start(bf16[1024,1024]{1,0:T(8,128)(2,1)} %param.26), channel_id=1, source_target_pairs={{0,1},{1,0},{2,3},{3,2},{4,5},{5,4},{6,7},{7,6},{8,9},{9,8},{10,11... | collective-permute-start | bytes 6291464 | tf_op jit(solution)/shard_map/ppermute | solution.py:146
  49.9 27.9 %collective-permute-start.8 = (bf16[128,4096]{1,0:T(8,128)(2,1)}, bf16[128,4096]{1,0:T(8,128)(2,1)}, u32[]{:S(2)}, u32[]{:S(2)}) collective-permute-start(bf16[128,4096]{1,0:T(8,128)(2,1)} %constant_dynamic-slice_fusion.5), channel_id=1, source_target_pairs={{0,2},{1,3},{2,0},{3,1},{4,6},{5,7},{6,4},{7,5},{8,10},{9,11},{10,... | collective-permute-start | bytes 3145736 | tf_op jit(solution)/shard_map/ppermute | solution.py:146
  51.5 25.6 %collective-permute-start.5 = (bf16[4,128,1024]{2,1,0:T(8,128)(2,1)}, bf16[4,128,1024]{2,1,0:T(8,128)(2,1)S(1)}, u32[]{:S(2)}, u32[]{:S(2)}) collective-permute-start(bf16[4,128,1024]{2,1,0:T(8,128)(2,1)} %collective-permute-done.3), channel_id=1, source_target_pairs={{0,4},{4,0},{8,12},{12,8},{16,20},{20,16},{24,28},{28,24},{1,5},{5... | collective-permute-start | bytes 3145736 | tf_op jit(solution)/shard_map/ppermute | solution.py:146
  52.9 25.9 %collective-permute-start.4 = (bf16[4,128,1024]{2,1,0:T(8,128)(2,1)}, bf16[4,128,1024]{2,1,0:T(8,128)(2,1)S(1)}, u32[]{:S(2)}, u32[]{:S(2)}) collective-permute-start(bf16[4,128,1024]{2,1,0:T(8,128)(2,1)} %collective-permute-done.3), channel_id=1, source_target_pairs={{0,1},{1,0},{2,3},{3,2},{4,5},{5,4},{6,7},{7,6},{8,9},{9,8},{10,11... | collective-permute-start | bytes 3145736 | tf_op jit(solution)/shard_map/ppermute | solution.py:146
  77.1 2.7 collective-permute-start.6
  77.1 110.3 %copy-start.84 = (f32[1,4,256]{2,0,1:T(1,128)}, f32[1,4,256]{2,0,1:T(1,128)S(1)}, u32[]{:S(2)}) copy-start(f32[1,4,256]{2,0,1:T(1,128)S(1)} %get-tuple-element.255) | copy-start | bytes 12292
  77.1 114.3 %copy-start.86 = (f32[1,4,256]{2,0,1:T(1,128)}, f32[1,4,256]{2,0,1:T(1,128)S(1)}, u32[]{:S(2)}) copy-start(f32[1,4,256]{2,0,1:T(1,128)S(1)} %get-tuple-element.254) | copy-start | bytes 12292
  77.8 80.9 %collective-permute-start.17 = (bf16[4,256,1024]{2,1,0:T(8,128)(2,1)}, bf16[4,256,1024]{2,1,0:T(8,128)(2,1)}, u32[]{:S(2)}, u32[]{:S(2)}) collective-permute-start(bf16[4,256,1024]{2,1,0:T(8,128)(2,1)} %param.30), channel_id=1, source_target_pairs={{0,1},{1,0},{2,3},{3,2},{4,5},{5,4},{6,7},{7,6},{8,9},{9,8},{10,11... | collective-permute-start | bytes 6291464 | tf_op jit(solution)/shard_map/ppermute | solution.py:146
  78.3 35.1 %collective-permute-start.13 = (bf16[512,1024]{1,0:T(8,128)(2,1)}, bf16[512,1024]{1,0:T(8,128)(2,1)}, u32[]{:S(2)}, u32[]{:S(2)}) collective-permute-start(bf16[512,1024]{1,0:T(8,128)(2,1)} %constant_dynamic-slice_fusion.4), channel_id=1, source_target_pairs={{0,2},{1,3},{2,0},{3,1},{4,6},{5,7},{6,4},{7,5},{8,10},{9,11},{10,... | collective-permute-start | bytes 3145736 | tf_op jit(solution)/shard_map/ppermute | solution.py:146
  79.7 25.5 %collective-permute-start.10 = (bf16[128,4096]{1,0:T(8,128)(2,1)}, bf16[128,4096]{1,0:T(8,128)(2,1)}, u32[]{:S(2)}, u32[]{:S(2)}) collective-permute-start(bf16[128,4096]{1,0:T(8,128)(2,1)} %collective-permute-done.8), channel_id=1, source_target_pairs={{0,4},{4,0},{8,12},{12,8},{16,20},{20,16},{24,28},{28,24},{1,5},{5... | collective-permute-start | bytes 3145736 | tf_op jit(solution)/shard_map/ppermute | solution.py:146
  81.1 33.4 %collective-permute-start.9 = (bf16[128,4096]{1,0:T(8,128)(2,1)}, bf16[128,4096]{1,0:T(8,128)(2,1)}, u32[]{:S(2)}, u32[]{:S(2)}) collective-permute-start(bf16[128,4096]{1,0:T(8,128)(2,1)} %collective-permute-done.8), channel_id=1, source_target_pairs={{0,1},{1,0},{2,3},{3,2},{4,5},{5,4},{6,7},{7,6},{8,9},{9,8},{10,11... | collective-permute-start | bytes 3145736 | tf_op jit(solution)/shard_map/ppermute | solution.py:146
  105.2 9.3 collective-permute-start.11
  113.4 80.6 %collective-permute-start.22 = (bf16[4,256,1024]{2,1,0:T(8,128)(2,1)}, bf16[4,256,1024]{2,1,0:T(8,128)(2,1)}, u32[]{:S(2)}, u32[]{:S(2)}) collective-permute-start(bf16[4,256,1024]{2,1,0:T(8,128)(2,1)} %param.31), channel_id=1, source_target_pairs={{0,1},{1,0},{2,3},{3,2},{4,5},{5,4},{6,7},{7,6},{8,9},{9,8},{10,11... | collective-permute-start | bytes 6291464 | tf_op jit(solution)/shard_map/ppermute | solution.py:146
  114.0 44.2 %collective-permute-start.18 = (bf16[4,128,1024]{2,1,0:T(8,128)(2,1)S(1)}, bf16[4,128,1024]{2,1,0:T(8,128)(2,1)}, u32[]{:S(2)}, u32[]{:S(2)}) collective-permute-start(bf16[4,128,1024]{2,1,0:T(8,128)(2,1)S(1)} %copy-done.63), channel_id=1, source_target_pairs={{0,2},{1,3},{2,0},{3,1},{4,6},{5,7},{6,4},{7,5},{8,10},{9,11},{10,... | collective-permute-start | bytes 3145736 | tf_op jit(solution)/shard_map/ppermute | solution.py:146
  114.5 25.1 %collective-permute-start.15 = (bf16[512,1024]{1,0:T(8,128)(2,1)}, bf16[512,1024]{1,0:T(8,128)(2,1)S(1)}, u32[]{:S(2)}, u32[]{:S(2)}) collective-permute-start(bf16[512,1024]{1,0:T(8,128)(2,1)} %collective-permute-done.13), channel_id=1, source_target_pairs={{0,4},{4,0},{8,12},{12,8},{16,20},{20,16},{24,28},{28,24},{1,5},{5... | collective-permute-start | bytes 3145736 | tf_op jit(solution)/shard_map/ppermute | solution.py:146
  115.8 44.4 %collective-permute-start.14 = (bf16[512,1024]{1,0:T(8,128)(2,1)}, bf16[512,1024]{1,0:T(8,128)(2,1)S(1)}, u32[]{:S(2)}, u32[]{:S(2)}) collective-permute-start(bf16[512,1024]{1,0:T(8,128)(2,1)} %collective-permute-done.13), channel_id=1, source_target_pairs={{0,1},{1,0},{2,3},{3,2},{4,5},{5,4},{6,7},{7,6},{8,9},{9,8},{10,11... | collective-permute-start | bytes 3145736 | tf_op jit(solution)/shard_map/ppermute | solution.py:146
  116.1 71.2 %copy-start.90 = (f32[384]{0:T(512)}, f32[384]{0:T(512)S(1)}, u32[]{:S(2)}) copy-start(f32[384]{0:T(512)S(1)} %broadcast_multiply_fusion.5) | copy-start | bytes 4612
  116.4 70.9 %copy-start.98 = (f32[384]{0:T(512)}, f32[384]{0:T(512)S(1)}, u32[]{:S(2)}) copy-start(f32[384]{0:T(512)S(1)} %add_rsqrt_fusion.1) | copy-start | bytes 4612
  123.4 34.7 %copy-start.35 = (bf16[384,1024]{1,0:T(8,128)(2,1)}, bf16[384,1024]{1,0:T(8,128)(2,1)S(1)}, u32[]{:S(2)}) copy-start(bf16[384,1024]{1,0:T(8,128)(2,1)S(1)} %fusion.90.refs_6_) | copy-start | bytes 2359300
  125.2 33.0 %copy-start.19 = (bf16[1024,4096]{1,0:T(8,128)(2,1)}, bf16[1024,4096]{1,0:T(8,128)(2,1)S(1)}, u32[]{:S(2)}) copy-start(bf16[1024,4096]{1,0:T(8,128)(2,1)S(1)} %constant_dynamic-update-slice_fusion.30) | copy-start | bytes 25165828
  139.6 20.6 %collective-permute-start.16 = (bf16[512,1024]{1,0:T(8,128)(2,1)S(1)}, bf16[512,1024]{1,0:T(8,128)(2,1)S(1)}, u32[]{:S(2)}, u32[]{:S(2)}) collective-permute-start(bf16[512,1024]{1,0:T(8,128)(2,1)S(1)} %collective-permute-done.15), channel_id=1, source_target_pairs={{0,1},{1,0},{2,3},{3,2},{4,5},{5,4},{6,7},{7,6},{8,9},{9,8},{10,11... | collective-permute-start | bytes 3145736 | tf_op jit(solution)/shard_map/ppermute | solution.py:146
  158.2 65.5 %collective-permute-start.32 = (bf16[256,4096]{1,0:T(8,128)(2,1)}, bf16[256,4096]{1,0:T(8,128)(2,1)}, u32[]{:S(2)}, u32[]{:S(2)}) collective-permute-start(bf16[256,4096]{1,0:T(8,128)(2,1)} %param.32), channel_id=1, source_target_pairs={{0,1},{1,0},{2,3},{3,2},{4,5},{5,4},{6,7},{7,6},{8,9},{9,8},{10,11... | collective-permute-start | bytes 6291464 | tf_op jit(solution)/shard_map/ppermute | solution.py:146
  158.7 34.7 %collective-permute-start.23 = (bf16[4,128,1024]{2,1,0:T(8,128)(2,1)}, bf16[4,128,1024]{2,1,0:T(8,128)(2,1)}, u32[]{:S(2)}, u32[]{:S(2)}) collective-permute-start(bf16[4,128,1024]{2,1,0:T(8,128)(2,1)} %constant_dynamic-slice_fusion.2), channel_id=1, source_target_pairs={{0,2},{1,3},{2,0},{3,1},{4,6},{5,7},{6,4},{7,5},{8,10},{9,11},{10,... | collective-permute-start | bytes 3145736 | tf_op jit(solution)/shard_map/ppermute | solution.py:146
  162.2 25.2 %collective-permute-start.20 = (bf16[4,128,1024]{2,1,0:T(8,128)(2,1)}, bf16[4,128,1024]{2,1,0:T(8,128)(2,1)}, u32[]{:S(2)}, u32[]{:S(2)}) collective-permute-start(bf16[4,128,1024]{2,1,0:T(8,128)(2,1)} %collective-permute-done.18), channel_id=1, source_target_pairs={{0,4},{4,0},{8,12},{12,8},{16,20},{20,16},{24,28},{28,24},{1,5},{5... | collective-permute-start | bytes 3145736 | tf_op jit(solution)/shard_map/ppermute | solution.py:146
  163.5 58.4 %copy-start.88 = (f32[1,4,256]{2,0,1:T(1,128)}, f32[1,4,256]{2,0,1:T(1,128)S(1)}, u32[]{:S(2)}) copy-start(f32[1,4,256]{2,0,1:T(1,128)S(1)} %get-tuple-element.253) | copy-start | bytes 12292
  163.5 93.7 %copy-start.82 = (f32[1,4,256]{2,0,1:T(1,128)}, f32[1,4,256]{2,0,1:T(1,128)S(1)}, u32[]{:S(2)}) copy-start(f32[1,4,256]{2,0,1:T(1,128)S(1)} %get-tuple-element.252) | copy-start | bytes 12292
  165.9 28.6 %collective-permute-start.19 = (bf16[4,128,1024]{2,1,0:T(8,128)(2,1)}, bf16[4,128,1024]{2,1,0:T(8,128)(2,1)}, u32[]{:S(2)}, u32[]{:S(2)}) collective-permute-start(bf16[4,128,1024]{2,1,0:T(8,128)(2,1)} %collective-permute-done.18), channel_id=1, source_target_pairs={{0,1},{1,0},{2,3},{3,2},{4,5},{5,4},{6,7},{7,6},{8,9},{9,8},{10,11... | collective-permute-start | bytes 3145736 | tf_op jit(solution)/shard_map/ppermute | solution.py:146
  187.3 7.1 collective-permute-start.21
  193.4 63.9 %collective-permute-start.37 = (bf16[1024,1024]{1,0:T(8,128)(2,1)}, bf16[1024,1024]{1,0:T(8,128)(2,1)}, u32[]{:S(2)}, u32[]{:S(2)}) collective-permute-start(bf16[1024,1024]{1,0:T(8,128)(2,1)} %param.33), channel_id=1, source_target_pairs={{0,1},{1,0},{2,3},{3,2},{4,5},{5,4},{6,7},{7,6},{8,9},{9,8},{10,11... | collective-permute-start | bytes 6291464 | tf_op jit(solution)/shard_map/ppermute | solution.py:146
  193.9 28.1 %collective-permute-start.33 = (bf16[128,4096]{1,0:T(8,128)(2,1)}, bf16[128,4096]{1,0:T(8,128)(2,1)}, u32[]{:S(2)}, u32[]{:S(2)}) collective-permute-start(bf16[128,4096]{1,0:T(8,128)(2,1)} %constant_dynamic-slice_fusion.1), channel_id=1, source_target_pairs={{0,2},{1,3},{2,0},{3,1},{4,6},{5,7},{6,4},{7,5},{8,10},{9,11},{10,... | collective-permute-start | bytes 3145736 | tf_op jit(solution)/shard_map/ppermute | solution.py:146
  194.7 26.7 %copy-start.116 = (f32[32]{0:T(128)}, f32[32]{0:T(128)S(1)}, u32[]{:S(2)}) copy-start(f32[32]{0:T(128)S(1)} %slice_reduce_fusion) | copy-start | bytes 388
  194.8 25.6 %collective-permute-start.30 = (bf16[4,128,1024]{2,1,0:T(8,128)(2,1)}, bf16[4,128,1024]{2,1,0:T(8,128)(2,1)}, u32[]{:S(2)}, u32[]{:S(2)}) collective-permute-start(bf16[4,128,1024]{2,1,0:T(8,128)(2,1)} %collective-permute-done.23), channel_id=1, source_target_pairs={{0,4},{4,0},{8,12},{12,8},{16,20},{20,16},{24,28},{28,24},{1,5},{5... | collective-permute-start | bytes 3145736 | tf_op jit(solution)/shard_map/ppermute | solution.py:146
  196.2 27.4 %collective-permute-start.29 = (bf16[4,128,1024]{2,1,0:T(8,128)(2,1)}, bf16[4,128,1024]{2,1,0:T(8,128)(2,1)}, u32[]{:S(2)}, u32[]{:S(2)}) collective-permute-start(bf16[4,128,1024]{2,1,0:T(8,128)(2,1)} %collective-permute-done.23), channel_id=1, source_target_pairs={{0,1},{1,0},{2,3},{3,2},{4,5},{5,4},{6,7},{7,6},{8,9},{9,8},{10,11... | collective-permute-start | bytes 3145736 | tf_op jit(solution)/shard_map/ppermute | solution.py:146
  220.4 3.2 collective-permute-start.31
  222.1 35.3 %collective-permute-start.38 = (bf16[512,1024]{1,0:T(8,128)(2,1)}, bf16[512,1024]{1,0:T(8,128)(2,1)}, u32[]{:S(2)}, u32[]{:S(2)}) collective-permute-start(bf16[512,1024]{1,0:T(8,128)(2,1)} %constant_dynamic-slice_fusion), channel_id=1, source_target_pairs={{0,2},{1,3},{2,0},{3,1},{4,6},{5,7},{6,4},{7,5},{8,10},{9,11},{10,... | collective-permute-start | bytes 3145736 | tf_op jit(solution)/shard_map/ppermute | solution.py:146
  223.6 30.5 %collective-permute-start.35 = (bf16[128,4096]{1,0:T(8,128)(2,1)}, bf16[128,4096]{1,0:T(8,128)(2,1)}, u32[]{:S(2)}, u32[]{:S(2)}) collective-permute-start(bf16[128,4096]{1,0:T(8,128)(2,1)} %collective-permute-done.33), channel_id=1, source_target_pairs={{0,4},{4,0},{8,12},{12,8},{16,20},{20,16},{24,28},{28,24},{1,5},{5... | collective-permute-start | bytes 3145736 | tf_op jit(solution)/shard_map/ppermute | solution.py:146
  224.4 33.0 %collective-permute-start.34 = (bf16[128,4096]{1,0:T(8,128)(2,1)}, bf16[128,4096]{1,0:T(8,128)(2,1)}, u32[]{:S(2)}, u32[]{:S(2)}) collective-permute-start(bf16[128,4096]{1,0:T(8,128)(2,1)} %collective-permute-done.33), channel_id=1, source_target_pairs={{0,1},{1,0},{2,3},{3,2},{4,5},{5,4},{6,7},{7,6},{8,9},{9,8},{10,11... | collective-permute-start | bytes 3145736 | tf_op jit(solution)/shard_map/ppermute | solution.py:146
  254.2 3.3 collective-permute-start.36
  257.4 25.4 %collective-permute-start.40 = (bf16[512,1024]{1,0:T(8,128)(2,1)}, bf16[512,1024]{1,0:T(8,128)(2,1)S(1)}, u32[]{:S(2)}, u32[]{:S(2)}) collective-permute-start(bf16[512,1024]{1,0:T(8,128)(2,1)} %collective-permute-done.38), channel_id=1, source_target_pairs={{0,4},{4,0},{8,12},{12,8},{16,20},{20,16},{24,28},{28,24},{1,5},{5... | collective-permute-start | bytes 3145736 | tf_op jit(solution)/shard_map/ppermute | solution.py:146
  258.8 31.0 %collective-permute-start.39 = (bf16[512,1024]{1,0:T(8,128)(2,1)}, bf16[512,1024]{1,0:T(8,128)(2,1)S(1)}, u32[]{:S(2)}, u32[]{:S(2)}) collective-permute-start(bf16[512,1024]{1,0:T(8,128)(2,1)} %collective-permute-done.38), channel_id=1, source_target_pairs={{0,1},{1,0},{2,3},{3,2},{4,5},{5,4},{6,7},{7,6},{8,9},{9,8},{10,11... | collective-permute-start | bytes 3145736 | tf_op jit(solution)/shard_map/ppermute | solution.py:146
  266.4 23.4 %copy-start.58 = (bf16[128,1024]{1,0:T(8,128)(2,1)}, bf16[128,1024]{1,0:T(8,128)(2,1)S(1)}, u32[]{:S(2)}) copy-start(bf16[128,1024]{1,0:T(8,128)(2,1)S(1)} %convert_element_type.310.refs_23_) | copy-start | bytes 786436
  267.9 21.9 %copy-start.4 = (bf16[1024,4096]{1,0:T(8,128)(2,1)}, bf16[1024,4096]{1,0:T(8,128)(2,1)S(1)}, u32[]{:S(2)}) copy-start(bf16[1024,4096]{1,0:T(8,128)(2,1)S(1)} %constant_dynamic-update-slice_fusion.6) | copy-start | bytes 25165828
  282.8 7.0 collective-permute-start.41
  454.3 53.3 %copy-start.16 = (f32[128,1024]{1,0:T(8,128)S(1)}, f32[128,1024]{1,0:T(8,128)}, u32[]{:S(2)}) copy-start(f32[128,1024]{1,0:T(8,128)} %copy-done.15) | copy-start | bytes 1572868
  454.3 67.1 %slice-start = ((s8[8388608]{0:T(1024)(128)(4,1)}), s8[4194304]{0:T(1024)(128)(4,1)S(1)}, s32[]{:S(2)}) async-start(s8[8388608]{0:T(1024)(128)(4,1)} %bitcast.402), calls=%async_computation | async-start | bytes 8388608
  568.7 21.7 %slice-start.2 = ((s8[8388608]{0:T(1024)(128)(4,1)}), s8[4194304]{0:T(1024)(128)(4,1)S(1)}, s32[]{:S(2)}) async-start(s8[8388608]{0:T(1024)(128)(4,1)} %bitcast.407), calls=%async_computation.2 | async-start | bytes 8388608
  569.3 21.0 %copy-start.37 = (bf16[384,1024]{1,0:T(8,128)(2,1)}, bf16[384,1024]{1,0:T(8,128)(2,1)S(1)}, u32[]{:S(2)}) copy-start(bf16[384,1024]{1,0:T(8,128)(2,1)S(1)} %convert_element_type.326.refs_9_) | copy-start | bytes 2359300
  569.3 21.0 %copy-start.8 = (f32[384,1024]{1,0:T(8,128)S(1)}, f32[384,1024]{1,0:T(8,128)}, u32[]{:S(2)}) copy-start(f32[384,1024]{1,0:T(8,128)} %copy-done.6) | copy-start | bytes 4718596
  569.3 21.0 %slice-start.3 = ((s8[8388608]{0:T(1024)(128)(4,1)}), s8[4194304]{0:T(1024)(128)(4,1)S(1)}, s32[]{:S(2)}) async-start(s8[8388608]{0:T(1024)(128)(4,1)} %bitcast.407), calls=%async_computation.3 | async-start | bytes 8388608
  569.3 21.0 %copy-start.85 = (f32[1,4,256]{2,0,1:T(1,128)S(1)}, f32[1,4,256]{2,0,1:T(1,128)}, u32[]{:S(2)}) copy-start(f32[1,4,256]{2,0,1:T(1,128)} %copy-done.84) | copy-start | bytes 12292
  569.3 21.0 %copy-start.91 = (f32[384]{0:T(512)S(1)}, f32[384]{0:T(512)}, u32[]{:S(2)}) copy-start(f32[384]{0:T(512)} %copy-done.90) | copy-start | bytes 4612
  569.3 21.0 %copy-start.99 = (f32[384]{0:T(512)S(1)}, f32[384]{0:T(512)}, u32[]{:S(2)}) copy-start(f32[384]{0:T(512)} %copy-done.98) | copy-start | bytes 4612
  (110 other events, 608.7 us)

commit v3 on v2

--- a/solution.py
+++ b/solution.py
@@ -1,4 +1,5 @@
 import functools
+import math
 
 import jax
 import jax.numpy as jnp
@@ -59,52 +60,113 @@
     return (inverse * inner, jnp.sum(upstream * normed, axis=0), jnp.sum(upstream, axis=0))
 
 
+def head_mask(which):
+    return lax.broadcasted_iota(jnp.int32, (1, 2 * HEAD_DIM), 1) // HEAD_DIM == which
+
+
+def only_head(pair, which):
+    return jnp.where(head_mask(which), pair.astype(jnp.float32), 0.0).astype(pair.dtype)
+
+
+def both_heads(first, second):
+    return jnp.where(head_mask(0), first, second)
+
+
+def attention_weights(queries, keys, causal):
+    scores = matmul_nt(queries, keys) * HEAD_DIM ** (-0.5)
+    if causal:
+        rows = lax.broadcasted_iota(jnp.int32, scores.shape, 0)
+        columns = lax.broadcasted_iota(jnp.int32, scores.shape, 1)
+        scores = jnp.where(rows >= columns, scores, MASK_FILL)
+    shifted = jnp.exp(scores - jnp.max(scores, axis=-1, keepdims=True))
+    return shifted / jnp.sum(shifted, axis=-1, keepdims=True)
+
+
+def attend_kernel(causal, queries, keys, values, out):
+    parts = []
+    for which in range(2):
+        probs = attention_weights(only_head(queries[...], which), keys[...], causal)
+        parts.append(matmul(to_low(probs), values[...]))
+    out[...] = to_low(both_heads(*parts))
+
+
+def attend_grad_kernel(
+    causal, queries, keys, values, upstream, grad_q, grad_k, grad_v, sum_q, sum_v
+):
+    parts = []
+    for which in range(2):
+        probs = attention_weights(only_head(queries[...], which), keys[...], causal)
+        grad_probs = matmul_nt(only_head(upstream[...], which), values[...])
+        inner = jnp.sum(grad_probs * probs, axis=-1, keepdims=True)
+        grad_scores = to_low(probs * (grad_probs - inner))
+        parts.append(
+            (
+                matmul(grad_scores, keys[...]),
+                matmul_tn(grad_scores, queries[...]),
+                matmul_tn(to_low(probs), upstream[...]),
+            )
+        )
+    scale = HEAD_DIM ** (-0.5)
+    query, key, value = [both_heads(*pair) for pair in zip(*parts)]
+    query = query * scale
+    grad_q[...] = to_low(query)
+    grad_k[...] = to_low(key * scale)
+    grad_v[...] = to_low(value)
+    sum_q[...] = jnp.broadcast_to(jnp.sum(query, axis=0, keepdims=True), sum_q.shape)
+    sum_v[...] = jnp.broadcast_to(jnp.sum(value, axis=0, keepdims=True), sum_v.shape)
+
+
+def head_pairs(rows):
+    return pl.BlockSpec((rows, 2 * HEAD_DIM), lambda pair: (0, pair))
+
+
+def attention_cost(rows, columns, products):
+    return pl.CostEstimate(
+        flops=2 * products * rows * columns * D,
+        bytes_accessed=4 * (rows + columns) * D * products,
+        transcendentals=HEADS * rows * columns,
+    )
+
+
 def attend_forward(query_low, memory_low, matrices, bias_query, bias_value, bias_out, causal):
-    rows = query_low.shape[0]
-    columns = memory_low.shape[0]
-    queries = to_low(matmul(query_low, matrices[0]) + bias_query).reshape(rows, HEADS, HEAD_DIM)
-    keys = to_low(matmul(memory_low, matrices[1])).reshape(columns, HEADS, HEAD_DIM)
-    values = to_low(matmul(memory_low, matrices[2]) + bias_value).reshape(columns, HEADS, HEAD_DIM)
-    scores = jnp.einsum(
-        "qhd,khd->hqk", queries, keys, preferred_element_type=jnp.float32
-    ) * HEAD_DIM ** (-0.5)
-    if causal:
-        visible = jnp.arange(rows)[:, None] >= jnp.arange(columns)[None, :]
-        scores = jnp.where(visible[None], scores, MASK_FILL)
-    shifted = jnp.exp(scores - jnp.max(scores, axis=-1, keepdims=True))
-    probs = shifted / jnp.sum(shifted, axis=-1, keepdims=True)
-    context = to_low(
-        jnp.einsum(
-            "hqk,khd->qhd", to_low(probs), values, preferred_element_type=jnp.float32
-        ).reshape(rows, D)
-    )
+    rows, columns = query_low.shape[0], memory_low.shape[0]
+    queries = to_low(matmul(query_low, matrices[0]) + bias_query)
+    keys = to_low(matmul(memory_low, matrices[1]))
+    values = to_low(matmul(memory_low, matrices[2]) + bias_value)
+    context = pl.pallas_call(
+        functools.partial(attend_kernel, causal),
+        grid=(HEADS // 2,),
+        out_shape=jax.ShapeDtypeStruct((rows, D), jnp.bfloat16),
+        in_specs=[head_pairs(rows), head_pairs(columns), head_pairs(columns)],
+        out_specs=head_pairs(rows),
+        cost_estimate=attention_cost(rows, columns, 2),
+        compiler_params=pltpu.CompilerParams(vmem_limit_bytes=24 << 20),
+    )(queries, keys, values)
     output = matmul(context, matrices[3]) + bias_out
-    return (output, (queries, keys, values, probs, context))
-
-
-def attend_backward(upstream, query_low, memory_low, matrices, saved):
-    queries, keys, values, probs, context = saved
-    rows = query_low.shape[0]
-    columns = memory_low.shape[0]
-    scale = HEAD_DIM ** (-0.5)
+    return (output, (queries, keys, values, context))
+
+
+def attend_backward(upstream, query_low, memory_low, matrices, saved, causal):
+    queries, keys, values, context = saved
+    rows, columns = query_low.shape[0], memory_low.shape[0]
     upstream_low = to_low(upstream)
-    grad_context = to_low(matmul_nt(upstream_low, matrices[3])).reshape(rows, HEADS, HEAD_DIM)
-    grad_probs = jnp.einsum(
-        "qhd,khd->hqk", grad_context, values, preferred_element_type=jnp.float32
-    )
-    grad_values = jnp.einsum(
-        "hqk,qhd->khd", to_low(probs), grad_context, preferred_element_type=jnp.float32
-    ).reshape(columns, D)
-    grad_scores = to_low(probs * (grad_probs - jnp.sum(grad_probs * probs, axis=-1, keepdims=True)))
-    grad_queries = (
-        jnp.einsum("hqk,khd->qhd", grad_scores, keys, preferred_element_type=jnp.float32) * scale
-    ).reshape(rows, D)
-    grad_keys = (
-        jnp.einsum("hqk,qhd->khd", grad_scores, queries, preferred_element_type=jnp.float32) * scale
-    ).reshape(columns, D)
-    queries_low = to_low(grad_queries)
-    keys_low = to_low(grad_keys)
-    values_low = to_low(grad_values)
+    grad_context = to_low(matmul_nt(upstream_low, matrices[3]))
+    low, sums = jnp.bfloat16, jax.ShapeDtypeStruct((8, D), jnp.float32)
+    queries_low, keys_low, values_low, query_sum, value_sum = pl.pallas_call(
+        functools.partial(attend_grad_kernel, causal),
+        grid=(HEADS // 2,),
+        out_shape=(
+            jax.ShapeDtypeStruct((rows, D), low),
+            jax.ShapeDtypeStruct((columns, D), low),
+            jax.ShapeDtypeStruct((columns, D), low),
+            sums,
+            sums,
+        ),
+        in_specs=[head_pairs(n) for n in (rows, columns, columns, rows)],
+        out_specs=tuple(head_pairs(n) for n in (rows, columns, columns, 8, 8)),
+        cost_estimate=attention_cost(rows, columns, 5),
+        compiler_params=pltpu.CompilerParams(vmem_limit_bytes=24 << 20),
+    )(queries, keys, values, grad_context)
     grad_query_input = matmul_nt(queries_low, matrices[0])
     grad_memory_input = matmul_nt(keys_low, matrices[1]) + matmul_nt(values_low, matrices[2])
     grad_pairs = [
@@ -113,125 +175,14 @@
         (memory_low, values_low),
         (context, upstream_low),
     ]
-    bias_grads = (
-        jnp.sum(grad_queries, axis=0),
-        jnp.sum(grad_values, axis=0),
-        jnp.sum(upstream, axis=0),
-    )
+    bias_grads = (query_sum[0], value_sum[0], jnp.sum(upstream, axis=0))
     return (grad_query_input, grad_memory_input, grad_pairs, bias_grads)
 
 
-def gelu_exact(value):
-    return jax.nn.gelu(value, approximate=False)
-
-
-def feed_forward(input_low, weight_up, bias_up, weight_down, bias_down):
-    before = matmul(input_low, weight_up) + bias_up
-    hidden_low = to_low(gelu_exact(before))
-    return (matmul(hidden_low, weight_down) + bias_down, (before, hidden_low))
-
-
-def hidden_backward(upstream_low, weight_down, before):
-    grad_hidden = matmul_nt(upstream_low, weight_down)
-    unused, pullback = jax.vjp(gelu_exact, before)
-    return pullback(grad_hidden)[0]
-
-
-def bit_of(name, mask):
-    return (lax.axis_index(name) // mask) % 2
-
-
-def swap(value, name, mask):
-    size = lax.axis_size(name)
-    return lax.ppermute(value, name, [(i, i ^ mask) for i in range(size)])
-
-
-def take(value, index, count, axis):
-    size = value.shape[axis] // count
-    return lax.dynamic_slice_in_dim(value, index * size, size, axis)
-
-
-def masks_of(name):
-    return masks_below(lax.axis_size(name))
-
-
-def natural_order(held, name):
-    count = held.shape[0]
-    for mask in masks_of(name):
-        pairs = held.reshape((count // (2 * mask), 2, mask) + held.shape[1:])
-        turned = jnp.where(bit_of(name, mask) == 0, pairs, pairs[:, ::-1])
-        held = turned.reshape(held.shape)
-    return held
-
-
-class Ticker:
-    def __init__(self):
-        self.active = []
-
-    def add(self, steps):
-        self.active.append((steps, next(steps)))
-
-    def tick(self, *values):
-        held, tree = jax.tree.flatten((values, [arrays for _, arrays in self.active]))
-        values, arrays = jax.tree.unflatten(tree, lax.optimization_barrier(held))
-        going = []
-        for (steps, _), mine in zip(self.active, arrays):
-            try:
-                going.append((steps, steps.send(mine)))
-            except StopIteration:
-                pass
-        self.active = going
-        return values if len(values) != 1 else values[0]
-
-    def drain(self):
-        while self.active:
-            self.tick()
-
-
-def gather_rows(shard, axis, box):
-    size = lax.axis_size("pb")
-    me = lax.axis_index("pb")
-    side = bit_of("slot", 1)
-    rows = shard.shape[axis]
-    far = size // 2
-    half = rows // 2
-
-    def spread(pieces):
-        mask = 1
-        while mask < far:
-            pieces = pieces + [
-                ((start // rows ^ mask) * rows + start % rows, swap(piece, "pb", mask))
-                for start, piece in pieces
-            ]
-            mask *= 2
-        return pieces
-
-    first = swap(take(shard, side, 2, axis), "pb", far)
-    near = spread([(me * rows, shard)])
-    starts = [start for start, _ in near]
-    arrays = yield ([piece for _, piece in near], first)
-    near = list(zip(starts, arrays[0]))
-    first = arrays[1]
-    second = swap(first, "slot", 1)
-    pieces = near + spread([((me ^ far) * rows + side * half, first)])
-    pieces = pieces + spread([((me ^ far) * rows + (1 - side) * half, second)])
-    starts = [start for start, _ in pieces]
-    arrays = yield [piece for _, piece in pieces]
-    shape = list(shard.shape)
-    shape[axis] = rows * size
-    full = jnp.zeros(tuple(shape), shard.dtype)
-    for start, piece in zip(starts, arrays):
-        full = lax.dynamic_update_slice_in_dim(full, piece, start, axis)
-    box.append(full)
-
-
-def gather_small(value, names, box):
-    held = value[None]
-    for name in names:
-        for mask in masks_of(name):
-            held = jnp.concatenate([held, swap(held, name, mask)], axis=0)
-    held = yield held
-    box.append(held)
+def gelu_with_slope(value):
+    share = 0.5 * (1.0 + lax.erf(value * 0.5**0.5))
+    density = jnp.exp(-0.5 * value * value) * (2.0 * math.pi) ** -0.5
+    return value * share, share + value * density
 
 
 def masks_below(size):
@@ -558,9 +509,6 @@
     )(*operands, small)
 
 
-EVERY = ("slot", "pb")
-
-
 def code_bits():
     return [("slot", mask) for mask in masks_below(lax.axis_size("slot"))[::-1]] + [
         ("pb", mask) for mask in masks_below(lax.axis_size("pb"))[::-1]
@@ -816,17 +764,207 @@
     )(stats)
 
 
+def weights_kernel(slots, groups, shards, vector, fact, fulls, vectors, facts, sems):
+    holds, local_sem, send_sem, recv_sem, small_local, small_send, small_recv = sems
+    slot, pb = lax.axis_index("slot"), lax.axis_index("pb")
+    core, far = xor(pb, 1), xor(pb, 2)
+    to_core, to_far = (slot, core), (slot, far)
+    across = [(xor(slot, mask), pb) for mask in masks_below(slots)]
+    meet([to_core, to_far] + across)
+
+    jobs = []
+    for shard, full in zip(shards, fulls):
+        if len(shard.shape) == 3:
+            for half in range(2):
+                lead = pl.ds(half * (shard.shape[0] // 2), shard.shape[0] // 2)
+                view = lambda ref, at, size, lead=lead: ref.at[lead, pl.ds(at, size)]
+                jobs.append((shard, full, shard.shape[1], shard.shape[1], 0, view))
+        elif shard.shape[1] > D:
+            for half in range(2):
+                lanes = pl.ds(half * (shard.shape[1] // 2), shard.shape[1] // 2)
+                view = lambda ref, at, size, lanes=lanes: ref.at[pl.ds(at, size), lanes]
+                jobs.append((shard, full, shard.shape[0], shard.shape[0], 0, view))
+        else:
+            for half in range(2):
+                rows = shard.shape[0] // 2
+                view = lambda ref, at, size: ref.at[pl.ds(at, size)]
+                jobs.append((shard, full, shard.shape[0], rows, half * rows, view))
+
+    def remote(source, target, job, kind, partner):
+        return pltpu.make_async_remote_copy(
+            src_ref=source,
+            dst_ref=target,
+            send_sem=send_sem.at[job, kind],
+            recv_sem=recv_sem.at[job, kind],
+            device_id=partner,
+            device_id_type=MESH,
+        )
+
+    def describe(job):
+        shard, full, block, rows, base, view = jobs[job]
+        turn = job % 2
+        first, second = (slot // (1 << turn)) % 2, (slot // (2 >> turn)) % 2
+        to_first, to_second = across[turn], across[1 - turn]
+        quarter, half = 3 * rows // 16, rows // 8
+        split = base + 3 * rows // 4
+        mine = pl.multiple_of(base + (second * 2 + first) * quarter, 16)
+        pair = pl.multiple_of(base + second * 2 * quarter, 16)
+        side = pl.multiple_of(split + second * half, 16)
+
+        def there(owner, at):
+            return pl.multiple_of(owner * block + at, 16)
+
+        def send(kind, partner, owner, at, size, source=None):
+            target = view(full, there(owner, at), size)
+            return remote(target if source is None else source, target, job, kind, partner)
+
+        own = view(shard, base, rows)
+        stages = [
+            [
+                send(0, to_far, pb, mine, quarter, view(shard, mine, quarter)),
+                send(1, to_far, pb, side, half, view(shard, side, half)),
+                send(2, to_core, pb, base, rows, own),
+            ],
+            [
+                send(3, to_first, far, mine, quarter),
+                send(4, to_second, far, side, half),
+            ],
+            [send(5, to_second, far, pair, 2 * quarter)],
+            [send(6, to_core, far, base, rows)],
+        ]
+        held = holds[job]
+        into = pltpu.make_async_copy(own, held, local_sem.at[job, 0])
+        onto = pltpu.make_async_copy(held, view(full, there(pb, base), rows), local_sem.at[job, 1])
+        return stages, (into, onto)
+
+    bits = [("pb", mask) for mask in masks_below(groups)] + [
+        ("slot", mask) for mask in masks_below(slots)
+    ]
+
+    def small_copy(kind, source, target, partner):
+        return pltpu.make_async_remote_copy(
+            src_ref=source,
+            dst_ref=target,
+            send_sem=small_send.at[kind],
+            recv_sem=small_recv.at[kind],
+            device_id=partner,
+            device_id_type=MESH,
+        )
+
+    def fact_copy(step):
+        name, mask = bits[step]
+        partner = (slot, xor(pb, mask)) if name == "pb" else (xor(slot, mask), pb)
+        count = 1 << step
+        source = fact if step == 0 else facts.at[pl.ds(0, count)]
+        return small_copy(step, source, facts.at[pl.ds(count, count)], partner)
+
+    near = len(bits)
+    vector_copies = [
+        small_copy(near, vector, vectors.at[pb], to_core),
+        small_copy(near + 1, vector, vectors.at[pb], to_far),
+    ]
+    vector_last = small_copy(near + 2, vectors.at[far], vectors.at[far], to_core)
+    small_own = [
+        pltpu.make_async_copy(fact.at[0], facts.at[0], small_local.at[0]),
+        pltpu.make_async_copy(vector, vectors.at[pb], small_local.at[1]),
+    ]
+    for copy in small_own + vector_copies:
+        copy.start()
+    plans = [describe(job) for job in range(len(jobs))]
+    for step in range(max(len(jobs) + 4, len(bits) + 1)):
+        for stage in range(5):
+            job = step - stage
+            if not 0 <= job < len(jobs):
+                continue
+            stages, (into, onto) = plans[job]
+            if stage == 0:
+                into.start()
+            else:
+                for copy in stages[stage - 1]:
+                    copy.wait()
+            if stage < 4:
+                for copy in stages[stage]:
+                    copy.start()
+                if stage == 1:
+                    into.wait()
+                    onto.start()
+            else:
+                onto.wait()
+        if step == 0:
+            for copy in small_own:
+                copy.wait()
+        if step == 1:
+            for copy in vector_copies:
+                copy.wait()
+            vector_last.start()
+        if step == 2:
+            vector_last.wait()
+        if 0 < step <= len(bits):
+            fact_copy(step - 1).wait()
+        if step < len(bits):
+            fact_copy(step).start()
+
+
+def gather_weights(shards, vector, fact):
+    slots, groups = lax.axis_size("slot"), lax.axis_size("pb")
+    bits = (slots * groups).bit_length() - 1
+
+    def widened(shard):
+        axis = 1 if shard.ndim == 3 else 0
+        shape = list(shard.shape)
+        shape[axis] *= groups
+        return jax.ShapeDtypeStruct(tuple(shape), shard.dtype)
+
+    used = len(shards)
+
+    def kernel(*refs):
+        ins, outs, sems = refs[: used + 2], refs[used + 2 : 2 * used + 4], refs[2 * used + 4 :]
+        weights_kernel(
+            slots, groups, ins[:used], ins[used], ins[used + 1], outs[:used], outs[used],
+            outs[used + 1], sems,
+        )
+
+    jobs = 2 * used
+    holds = []
+    for shard in shards:
+        axis = 1 if shard.ndim == 2 and shard.shape[1] > D else 0
+        shape = list(shard.shape)
+        shape[axis] //= 2
+        holds += [pltpu.VMEM(tuple(shape), shard.dtype)] * 2
+    return pl.pallas_call(
+        kernel,
+        out_shape=[widened(shard) for shard in shards]
+        + [
+            jax.ShapeDtypeStruct((groups,) + vector.shape, vector.dtype),
+            jax.ShapeDtypeStruct((slots * groups,) + fact.shape[1:], fact.dtype),
+        ],
+        in_specs=[pl.BlockSpec(memory_space=pl.ANY)] * (used + 2),
+        out_specs=[pl.BlockSpec(memory_space=pl.ANY)] * (used + 2),
+        scratch_shapes=[
+            holds,
+            pltpu.SemaphoreType.DMA((jobs, 2)),
+            pltpu.SemaphoreType.DMA((jobs, 7)),
+            pltpu.SemaphoreType.DMA((jobs, 7)),
+            pltpu.SemaphoreType.DMA((2,)),
+            pltpu.SemaphoreType.DMA((bits + 3,)),
+            pltpu.SemaphoreType.DMA((bits + 3,)),
+        ],
+        compiler_params=pltpu.CompilerParams(
+            collective_id=5, has_side_effects=True, vmem_limit_bytes=32 << 20
+        ),
+    )(*shards, vector, fact)
+
+
 def own_facts(targets, owner, doc_scores):
     serving = jnp.arange(targets.shape[1]) == owner[0, 0]
     own = jnp.sum(jnp.where(serving[:, None], targets[0], 0), axis=0)
     half = (TGT_LEN // 2,)
-    return jnp.concatenate(
-        [
-            own.astype(jnp.float32),
-            jnp.broadcast_to(owner[0, 0].astype(jnp.float32), half),
-            jnp.broadcast_to(doc_scores[0, 0], half),
-        ]
-    )
+    facts = [
+        own.astype(jnp.float32),
+        jnp.broadcast_to(owner[0, 0].astype(jnp.float32), half),
+        jnp.broadcast_to(doc_scores[0, 0], half),
+    ]
+    return jnp.pad(jnp.concatenate(facts).reshape(1, 2, TGT_LEN), ((0, 0), (0, 6), (0, 0)))
 
 
 def vocabulary_head(state_low, facts, questions, embed):
@@ -834,9 +972,9 @@
     me = lax.axis_index("slot") * groups + lax.axis_index("pb")
     entries = embed.shape[0]
     tokens = slots * groups * TGT_LEN
-    target_ids = facts[:, :TGT_LEN].astype(jnp.int32).reshape(tokens, 1)
-    owners = facts[:, TGT_LEN].astype(jnp.int32).reshape(slots, groups)
-    scores = facts[:, TGT_LEN + TGT_LEN // 2].reshape(slots, groups)
+    target_ids = facts[:, 0].astype(jnp.int32).reshape(tokens, 1)
+    owners = facts[:, 1, 0].astype(jnp.int32).reshape(slots, groups)
+    scores = facts[:, 1, TGT_LEN // 2].reshape(slots, groups)
     states = gather_states(state_low)
     logits = matmul_nt(states, embed)
     hit = target_ids - me * entries == lax.broadcasted_iota(jnp.int32, (tokens, entries), 1)
@@ -901,14 +1039,24 @@
     question_low = dec_input[0, 0]
     question = question_low.astype(jnp.float32)
 
-    full = []
-    ticker = Ticker()
-    ticker.add(
-        gather_small(jnp.concatenate([v.reshape(-1, width) for v in vectors]), ("pb",), full)
-    )
-    ticker.add(gather_rows(enc_attn, 1, full))
-    ticker.tick()
-    packed = natural_order(full[0], "pb").astype(jnp.float32)
+    own_vectors = jnp.concatenate([v.reshape(-1, width) for v in vectors])
+    (
+        encoder_attn,
+        encoder_up,
+        encoder_down,
+        decoder_self,
+        decoder_cross,
+        decoder_down,
+        packed,
+        facts,
+    ) = gather_weights(
+        (enc_attn, enc_up, enc_down, dec_self, dec_cross, dec_down),
+        jnp.pad(own_vectors, ((0, -starts[-1] % 32), (0, 0))),
+        own_facts(targets, owner, doc_scores),
+    )
+    packed, dec_up = lax.optimization_barrier((packed, dec_up))
+    decoder_up = lax.all_gather(dec_up, "pb", axis=0, tiled=True)
+    packed = packed.astype(jnp.float32)
     unpacked = [packed[:, starts[i] : starts[i + 1], :] for i in range(len(rows))]
     encoder_upbias = unpacked[0].reshape(-1)
     encoder_bias = unpacked[1].transpose(1, 0, 2).reshape(-1, D)
@@ -916,10 +1064,6 @@
     decoder_upbias = unpacked[3].reshape(-1)
     decoder_bias = unpacked[4].transpose(1, 0, 2).reshape(-1, D)
     decoder_gain = unpacked[5].transpose(1, 0, 2).reshape(-1, D)
-    ticker.add(gather_rows(enc_up, 0, full))
-    ticker.tick()
-    encoder_attn = full[1]
-    ticker.add(gather_rows(enc_down, 0, full))
     attn_out, enc_saved = attend_forward(
         passage_low,
         passage_low,
@@ -929,24 +1073,13 @@
         encoder_bias[2],
         False,
     )
-    attn_out = ticker.tick(attn_out)
-    encoder_up = full[2]
-    ticker.add(gather_rows(dec_self, 1, full))
     enc_first, enc_norm_one = norm_forward(passage + attn_out, encoder_gain[0], encoder_bias[3])
     enc_first_low = to_low(enc_first)
-    enc_before = matmul(enc_first_low, encoder_up) + encoder_upbias
-    enc_hidden_low = to_low(gelu_exact(enc_before))
-    enc_hidden_low, enc_before = ticker.tick(enc_hidden_low, enc_before)
-    encoder_down = full[3]
-    ticker.add(gather_rows(dec_cross, 1, full))
-    ticker.add(gather_small(own_facts(targets, owner, doc_scores), EVERY[::-1], full))
+    enc_hidden, enc_slope = gelu_with_slope(matmul(enc_first_low, encoder_up) + encoder_upbias)
+    enc_hidden_low = to_low(enc_hidden)
     ffn_out = matmul(enc_hidden_low, encoder_down) + encoder_bias[4]
     encoded, enc_norm_two = norm_forward(enc_first + ffn_out, encoder_gain[1], encoder_bias[5])
     memory_low = to_low(encoded)
-    memory_low = ticker.tick(memory_low)
-    decoder_self = full[4]
-    facts = full[5]
-    ticker.add(gather_rows(dec_up, 0, full))
     self_out, self_saved = attend_forward(
         question_low,
         question_low,
@@ -957,10 +1090,7 @@
         True,
     )
     dec_first, dec_norm_one = norm_forward(question + self_out, decoder_gain[0], decoder_bias[3])
-    dec_first = ticker.tick(dec_first)
     dec_first_low = to_low(dec_first)
-    decoder_cross = full[6]
-    ticker.add(gather_rows(dec_down, 0, full))
     cross_out, cross_saved = attend_forward(
         dec_first_low,
         memory_low,
@@ -971,13 +1101,9 @@
         False,
     )
     dec_second, dec_norm_two = norm_forward(dec_first + cross_out, decoder_gain[1], decoder_bias[7])
-    dec_second = ticker.tick(dec_second)
     dec_second_low = to_low(dec_second)
-    decoder_up = full[7]
-    dec_before = matmul(dec_second_low, decoder_up) + decoder_upbias
-    dec_hidden_low = to_low(gelu_exact(dec_before))
-    dec_hidden_low, dec_before = ticker.tick(dec_hidden_low, dec_before)
-    decoder_down = full[8]
+    dec_hidden, dec_slope = gelu_with_slope(matmul(dec_second_low, decoder_up) + decoder_upbias)
+    dec_hidden_low = to_low(dec_hidden)
     dec_ffn_out = matmul(dec_hidden_low, decoder_down) + decoder_bias[8]
     state, dec_norm_three = norm_forward(dec_second + dec_ffn_out, decoder_gain[2], decoder_bias[9])
     state_low = to_low(state)
@@ -992,20 +1118,20 @@
     )
     dec_downbias_grad = jnp.sum(grad_third, axis=0)
     third_low = to_low(grad_third)
-    grad_before = hidden_backward(third_low, decoder_down, dec_before)
+    grad_before = matmul_nt(third_low, decoder_down) * dec_slope
     dec_upbias_grad = jnp.sum(grad_before, axis=0)
     before_low = to_low(grad_before)
     grad_second, gain_second, shift_second = norm_backward(
         grad_third + matmul_nt(before_low, decoder_up), dec_norm_two, decoder_gain[1]
     )
     cross_query, grad_memory, dec_cross_pairs, cross_biases = attend_backward(
-        grad_second, dec_first_low, memory_low, decoder_cross, cross_saved
+        grad_second, dec_first_low, memory_low, decoder_cross, cross_saved, False
     )
     grad_first, gain_first, shift_first = norm_backward(
         grad_second + cross_query, dec_norm_one, decoder_gain[0]
     )
     self_query, self_memory, dec_self_pairs, self_biases = attend_backward(
-        grad_first, question_low, question_low, decoder_self, self_saved
+        grad_first, question_low, question_low, decoder_self, self_saved, True
     )
     question_grad = grad_first + self_query + self_memory
     enc_grad_two, enc_gain_two, enc_shift_two = norm_backward(
@@ -1013,14 +1139,14 @@
     )
     enc_downbias_grad = jnp.sum(enc_grad_two, axis=0)
     enc_two_low = to_low(enc_grad_two)
-    enc_grad_before = hidden_backward(enc_two_low, encoder_down, enc_before)
+    enc_grad_before = matmul_nt(enc_two_low, encoder_down) * enc_slope
     enc_upbias_grad = jnp.sum(enc_grad_before, axis=0)
     enc_before_low = to_low(enc_grad_before)
     enc_grad_one, enc_gain_one, enc_shift_one = norm_backward(
         enc_grad_two + matmul_nt(enc_before_low, encoder_up), enc_norm_one, encoder_gain[0]
     )
     enc_query, enc_memory, enc_attn_pairs, enc_biases = attend_backward(
-        enc_grad_one, passage_low, passage_low, encoder_attn, enc_saved
+        enc_grad_one, passage_low, passage_low, encoder_attn, enc_saved, False
     )
     passage_grad = enc_grad_one + enc_query + enc_memory
     operands, plan = [], []

time: 1080 us -> 956 us (0.89)
  Pallas kernels: 501 us -> 675 us
  matrix products: 256 us -> 166 us
  waiting for transfers between devices: 89.6 us -> 0.02 us
  local copies, waits for them, and re-layouts: 118 us -> 43.2 us
  starting transfers between devices: 30.1 us -> 0.04 us
  other arithmetic: 64.7 us -> 45.9 us
  between operations: 5.18 us -> 18.2 us
    pallas_call x0 -> x7, Pallas kernels: none -> 178 us  [the longest x1 120 us: gather_weights(): pl.pallas_call(kernel, out_shape=[widened(shard) for shard in shards] + [...]
    ppermute x42 -> x0, waiting for transfers between devices: 89.6 us -> none  [swap(): return lax.ppermute(value, name, [(i, i ^ mask) for i in range(size)])]
    dynamic_update_slice x42 -> x0, local copies, waits for them, and re-layouts: 43.3 us -> none  [gather_rows(): full = lax.dynamic_update_slice_in_dim(full, piece, start, axis)]
    dot_general x15 -> x0, matrix products: 41.1 us -> none  [the longest x3 12.4 us: attend_backward(): jnp.einsum('hqk,qhd->khd', to_low(probs), grad_context, preferred_element...]
    ppermute x42 -> x0, starting transfers between devices: 30.1 us -> none  [swap(): return lax.ppermute(value, name, [(i, i ^ mask) for i in range(size)])]
    convert_element_type x20 -> x2, local copies, waits for them, and re-layouts: 26.6 us -> 0.18 us  [vocabulary_head(): owners = facts[:, 1, 0].astype(jnp.int32).reshape(slots, groups)]
    dot_general x17, matrix products: 101 us -> 82.3 us  [matmul_nt(): lax.dot_general(left, right, (((1,), (1,)), ((), ())), preferred_element_...]
    dot_general x17, matrix products: 78.3 us -> 62.2 us  [matmul(): return jnp.dot(left, right, preferred_element_type=jnp.float32)]
  transfers between devices with their start and end apart: 42 -> 1, of which waited for: 9 -> 0; matrix products, arithmetic and copies ran while one was open for 15% -> 4% of each run, Pallas kernels for 0% -> 2%
where the time goes in v3:
time: 956 us; the launch traced here: 948 us
  Pallas kernels  675 us (71%)
  matrix products  166 us (17%)
  other arithmetic  45.9 us (5%)
  local copies, waits for them, and re-layouts  43.2 us (5%)
  between operations  18.2 us (2%)
    pallas_call x1, Pallas kernels, sync_gradients(): pl.pallas_call(kernel, out_shape=(jax.ShapeDtypeStruct((count, rows, colu...  373 us
    pallas_call x1, Pallas kernels, gather_weights(): pl.pallas_call(kernel, out_shape=[widened(shard) for shard in shards] + [...  120 us
    dot_general x17, matrix products, matmul_nt(): lax.dot_general(left, right, (((1,), (1,)), ((), ())), preferred_element_...  82.3 us
    dot_general x17, matrix products, matmul(): return jnp.dot(left, right, preferred_element_type=jnp.float32)  62.2 us
    pallas_call x1, Pallas kernels, gather_states(): pl.pallas_call(functools.partial(gather_kernel, bits, parts), out_shape=j...  54.3 us
    pallas_call x1, Pallas kernels, scatter_states(): pl.pallas_call(functools.partial(scatter_kernel, bits, parts), out_shape=...  53.3 us
    pallas_call x3, Pallas kernels, attend_backward(): pl.pallas_call(functools.partial(attend_grad_kernel, causal), grid=(HEADS...  34.5 us
    unnamed x289, local copies, waits for them, and re-layouts  23.5 us
  transfers between devices with their start and end apart: 1, of which 0 were waited for; matrix products, arithmetic and copies ran while one was open for 4% of the time, Pallas kernels for 2%

profile of v3, /device:TPU:0, one launch (start us, length us, event | category | flops | bytes accessed | tf_op | source)
XLA Modules:
  0.0 947.8 jit_solution(6225246628889695527)
XLA Ops:
  11.1 2.9 concatenate.26
  14.0 1.6 copy-done.8
  15.6 1.6 copy-done.9
  17.2 1.6 copy-done.10
  18.7 1.6 copy-done.11
  20.3 1.6 copy-done.12
  21.9 1.6 copy-done.13
  23.5 120.3 %shard_map.322 = (bf16[4,1024,1024]{2,1,0:T(8,128)(2,1)S(1)}, bf16[1024,4096]{1,0:T(8,128)(2,1)}, bf16[4096,1024]{1,0:T(8,128)(2,1)}, bf16[4,1024,1024]{2,1,0:T(...) custom-call(bf16[4,256,1024]{2,1,0:T(8,128)(2,1)S(1)} %copy-done.8, ...), custom_call_target="tpu_custom_call" | custom-call | tf_op jit(solution)/shard_map/pallas_call | solution.py:934
  143.9 3.2 copy-done.33
  152.3 2.6 fusion.174.keys
  154.9 3.9 fusion.171.values
  158.8 2.2 fusion.168.queries
  161.0 6.6 shard_map.323.refs_14_
  167.6 1.0 fusion.110.keys
  168.6 1.0 fusion.107.values
  169.6 1.0 fusion.104.queries
  170.6 9.3 shard_map.324.refs_4_
  180.0 2.5 fusion.214
  182.8 1.1 fusion.215
  185.3 6.0 multiply_convert_fusion.1
  191.4 3.6 fusion.216
  196.7 1.0 fusion.100.keys
  197.7 1.0 add_convert_fusion.values
  198.7 7.3 shard_map.325.refs_21_
  209.0 6.4 multiply_convert_fusion.2
  215.4 5.2 fusion.218
  222.3 54.3 %shard_map.326 = bf16[2,2,2,2,2,128,1024]{6,5,4,3,2,1,0:T(8,128)(2,1)} custom-call(bf16[128,1024]{1,0:T(8,128)(2,1)} %add_convert_fusion.4.own), custom_call_target="tpu_custom_call" | custom-call | tf_op jit(solution)/shard_map/pallas_call | solution.py:589
  276.7 20.4 %fusion.219 = (f32[4096]{0:T(1024)S(1)}, f32[4096,1536]{0,1:T(8,128)}) fusion(bf16[4096,1024]{1,0:T(8,128)(2,1)} %bitcast.337, bf16[1536,1024]{1,0:T(8,128)(2,1)S(1)} %copy-done), kind=kOutput, calls=%fused_computation.278 | convolution fusion | flops 12891189248 | bytes 36716544 | tf_op jit(solution)/shard_map/dot_general | solution.py:30
  297.1 11.6 %exponential_reduce_fusion = (f32[4096]{0:T(1024)S(1)}, f32[4096]{0:T(1024)S(1)}) fusion(f32[4096,1536]{0,1:T(8,128)} %get-tuple-element.167, f32[4096]{0:T(1024)S(1)} %get-tuple-element.166, s32[4096]{0:T(1024)S(1)} %bitcast.354), kind=kLoop, calls=%fused_computation.3 | loop fusion | flops 31449088 | bytes 25231360 | tf_op jit(solution)/shard_map/reduce_sum | solution.py:982
  309.4 16.1 %shard_map.327 = f32[3,32,128]{2,1,0:T(8,128)} custom-call(f32[3,32,128]{2,1,0:T(8,128)} %pad_maximum_fusion.stats), custom_call_target="tpu_custom_call" | custom-call | tf_op jit(solution)/shard_map/pallas_call | solution.py:752
  328.8 21.4 %fusion.199 = f32[1536,1024]{1,0:T(8,128)} fusion(bf16[4096,1024]{1,0:T(8,128)(2,1)} %bitcast.338, f32[4096,1536]{0,1:T(8,128)} %get-tuple-element.167, f32[4096]{0:T(1024)S(1)} %get-tuple-element.105, f32[4096]{0:T(1024)S(1)} %get-tuple-element.104, s32[4096]{0:T(1024)S(1)} %bitcast.355), kind=kOutput, calls=%fused_computation.259 | convolution fusion | flops 12922650624 | bytes 39895040 | tf_op jit(solution)/shard_map/dot_general | solution.py:36
  350.2 22.8 %convolution_convert_fusion = bf16[4096,1024]{1,0:T(8,128)(2,1)} fusion(bf16[1536,1024]{1,0:T(8,128)(2,1)S(1)} %copy-done, f32[4096,1536]{0,1:T(8,128)} %get-tuple-element.167, f32[4096]{0:T(1024)S(1)} %get-tuple-element.105, f32[4096]{0:T(1024)S(1)} %get-tuple-element.104, s32[4096]{0:T(1024)S(1)} %bitcast.356), kind=kOutput, calls=%fused_computation.5 | convolution fusion | flops 12926844928 | bytes 36749312 | tf_op jit(solution)/shard_map/dot_general | solution.py:26
  373.0 53.3 %shard_map.328 = f32[128,1024]{1,0:T(8,128)} custom-call(bf16[2,2,2,2,2,128,1024]{6,5,4,3,2,1,0:T(8,128)(2,1)} %bitcast.339), custom_call_target="tpu_custom_call" | custom-call | tf_op jit(solution)/shard_map/pallas_call | solution.py:695
  426.4 2.0 multiply_reduce_fusion.8
  428.4 1.8 fusion.200
  430.3 6.6 fusion.208
  437.6 7.2 multiply_reduce_fusion.9
  446.3 2.6 fusion.156.upstream
  448.9 10.6 %shard_map.329 = (bf16[128,1024]{1,0:T(8,128)(2,1)S(1)}, bf16[384,1024]{1,0:T(8,128)(2,1)S(1)}, bf16[384,1024]{1,0:T(8,128)(2,1)S(1)}, f32[8,1024]{1,0:T(8,128)S(1)}, f32[8,1024]{1,0:T(8,128)S(1)}) custom-call(bf16[128,1024]{1,0:T(8,128)(2,1)S(1)} %fusion.159.queries, bf16[384,1024]{1,0:T(8,128)(2,1)S(1)} %copy-done.5, bf16[384,1024]{1,0:T(8,128)(2,1)S(1)} %copy-done.7, ...), custom_call_target="tpu_custom_call" | custom-call | flops 503316480 | bytes 10485760 | tf_op jit(solution)/shard_map/pallas_call | solution.py:155
  459.6 3.2 multiply_reduce_fusion.10
  463.9 2.5 fusion.153.upstream
  466.4 9.1 shard_map.331
  475.6 3.5 fusion.45
  479.1 1.0 fusion.13
  480.5 1.5 multiply_reduce_fusion
  482.7 8.1 fusion.207
  490.9 5.0 multiply_reduce_fusion.1
  495.9 1.9 fusion.204
  497.8 1.1 copy-done.49
  500.0 2.8 fusion.97.upstream
  502.9 14.8 %shard_map.330 = (bf16[384,1024]{1,0:T(8,128)(2,1)S(1)}, bf16[384,1024]{1,0:T(8,128)(2,1)S(1)}, bf16[384,1024]{1,0:T(8,128)(2,1)S(1)}, f32[8,1024]{1,0:T(8,128)S(1)}, f32[8,1024]{1,0:T(8,128)S(1)}) custom-call(bf16[384,1024]{1,0:T(8,128)(2,1)S(1)} %copy-done.42, bf16[384,1024]{1,0:T(8,128)(2,1)S(1)} %copy-done.38, bf16[384,1024]{1,0:T(8,128)(2,1)S(1)} %copy-done.40, ...), custom_call_target="tpu_custom_call" | custom-call | flops 1509949440 | bytes 15728640 | tf_op jit(solution)/shard_map/pallas_call | solution.py:155
  521.5 372.8 %shard_map.332 = (bf16[28,256,1024]{2,1,0:T(8,128)(2,1)}, f32[8,1024]{1,0:T(8,128)}) custom-call(bf16[384,1024]{1,0:T(8,128)(2,1)} %bitcast.340, bf16[384,1024]{1,0:T(8,128)(2,1)} %copy-done.2, bf16[384,1024]{1,0:T(8,128)(2,1)} %copy-done.29, bf16[384,1024]{1,0:T(8,128)(2,1)} %copy-done.31, bf16[384,1024]{1,0:T(8,128)(2,1)} %copy-done.26, ...), custom_call_target="tpu_custom_call" | custom-call | tf_op jit(solution)/shard_map/pallas_call | solution.py:470
  894.3 1.4 fusion.210
  898.9 3.9 fusion.25
  902.8 4.5 fusion.29
  907.3 4.2 slice_bitcast_fusion.3
  911.6 5.6 fusion.206
  918.5 2.5 fusion.125
  921.0 3.2 fusion.122
  924.3 2.6 bitcast_convert_fusion
  926.9 2.7 bitcast_convert_fusion.1
  931.0 4.0 add_bitcast_fusion
  935.1 2.5 maximum_convert_fusion.1
  937.6 2.5 maximum_convert_fusion
  (400 shorter events, 34.4 us)
Async XLA Ops:
  7.2 269.5 %copy-start = (bf16[1536,1024]{1,0:T(8,128)(2,1)S(1)}, bf16[1536,1024]{1,0:T(8,128)(2,1)}, u32[]{:S(2)}) copy-start(bf16[1536,1024]{1,0:T(8,128)(2,1)} %param.37) | copy-start | bytes 9437188
  7.2 201.8 %all-gather.2.cloned.1.call-start = ((), (), s32[]{:S(2)}) async-start(), calls=%async_computation | async-start | bytes 10485760 | tf_op jit(solution)/shard_map/all_gather | solution.py:1058
  148.6 177.6 %copy-start.92 = (f32[8,4]{1,0:T(8,128)}, f32[8,4]{1,0:T(8,128)S(1)}, u32[]{:S(2)}) copy-start(f32[8,4]{1,0:T(8,128)S(1)} %add.367) | copy-start | bytes 388
  152.3 15.3 %copy-start.34 = (bf16[4,1024,1024]{2,1,0:T(8,128)(2,1)S(1)}, bf16[4,1024,1024]{2,1,0:T(8,128)(2,1)}, u32[]{:S(2)}) copy-start(bf16[4,1024,1024]{2,1,0:T(8,128)(2,1)} %copy-done.33) | copy-start | bytes 25165828
  158.8 8.8 copy-start.22
  158.8 8.8 copy-start.83
  161.0 7.6 copy-start.24
  167.5 12.5 %copy-start.14 = (bf16[128,1024]{1,0:T(8,128)(2,1)}, bf16[128,1024]{1,0:T(8,128)(2,1)S(1)}, u32[]{:S(2)}) copy-start(bf16[128,1024]{1,0:T(8,128)(2,1)S(1)} %shard_map.323.refs_14_) | copy-start | bytes 786436
  170.6 9.3 copy-start.41
  182.5 23.5 %copy-start.59 = (f32[128,1024]{1,0:T(8,128)}, f32[128,1024]{1,0:T(8,128)S(1)}, u32[]{:S(2)}) copy-start(f32[128,1024]{1,0:T(8,128)S(1)} %get-tuple-element.153) | copy-start | bytes 1572868
  182.5 23.5 %copy-start.124 = (f32[128]{0:T(128)}, f32[128]{0:T(128)S(1)}, u32[]{:S(2)}) copy-start(f32[128]{0:T(128)S(1)} %broadcast_multiply_fusion.14) | copy-start | bytes 1540
  183.8 7.5 copy-start.45
  183.9 7.5 copy-start.99
  184.2 7.2 copy-start.104
  184.2 7.2 copy-start.93
  184.2 11.4 %copy-start.95 = (f32[1,4,256]{2,0,1:T(1,128)}, f32[1,4,256]{2,0,1:T(1,128)S(1)}, u32[]{:S(2)}) copy-start(f32[1,4,256]{2,0,1:T(1,128)S(1)} %get-tuple-element.150) | copy-start | bytes 12292
  184.2 7.1 slice-start.4
  184.6 6.7 copy-start.62
  185.3 6.1 slice-start.5
  195.4 10.7 %copy-start.126 = (f32[128]{0:T(128)}, f32[128]{0:T(128)S(1)}, u32[]{:S(2)}) copy-start(f32[128]{0:T(128)S(1)} %add_rsqrt_fusion.4) | copy-start | bytes 1540
  195.4 10.6 %copy-start.97 = (f32[1,4,256]{2,0,1:T(1,128)}, f32[1,4,256]{2,0,1:T(1,128)S(1)}, u32[]{:S(2)}) copy-start(f32[1,4,256]{2,0,1:T(1,128)S(1)} %get-tuple-element.149) | copy-start | bytes 12292
  195.4 19.9 %copy-start.86 = (f32[1,4,256]{2,0,1:T(1,128)}, f32[1,4,256]{2,0,1:T(1,128)S(1)}, u32[]{:S(2)}) copy-start(f32[1,4,256]{2,0,1:T(1,128)S(1)} %get-tuple-element.148) | copy-start | bytes 12292
  195.4 25.5 %copy-start.88 = (f32[1,4,256]{2,0,1:T(1,128)}, f32[1,4,256]{2,0,1:T(1,128)S(1)}, u32[]{:S(2)}) copy-start(f32[1,4,256]{2,0,1:T(1,128)S(1)} %get-tuple-element.147) | copy-start | bytes 12292
  198.7 8.0 copy-start.6
  209.0 6.4 copy-start.52
  209.0 6.4 copy-start.115
  209.0 6.4 copy-start.117
  209.0 6.4 copy-start.119
  276.7 20.4 %copy-start.90 = (s32[32,1,128]{2,1,0:T(1,128)S(1)}, s32[32,1,128]{2,1,0:T(1,128)}, u32[]{:S(2)}) copy-start(s32[32,1,128]{2,1,0:T(1,128)} %convert_subtract_fusion) | copy-start | bytes 49156
  297.1 29.2 %copy-start.103 = (pred[8,4,2]{0,2,1:T(4,128)(4,1)S(1)}, pred[8,4,2]{0,2,1:T(4,128)(4,1)}, u32[]{:S(2)}) copy-start(pred[8,4,2]{0,2,1:T(4,128)(4,1)} %copy.82) | copy-start | bytes 196
  297.1 29.4 %copy-start.120 = (f32[4,2]{1,0:T(4,128)S(1)}, f32[4,2]{1,0:T(4,128)}, u32[]{:S(2)}) copy-start(f32[4,2]{1,0:T(4,128)} %copy.91) | copy-start | bytes 100
  373.0 53.3 %copy-start.55 = (f32[128,1024]{1,0:T(8,128)S(1)}, f32[128,1024]{1,0:T(8,128)}, u32[]{:S(2)}) copy-start(f32[128,1024]{1,0:T(8,128)} %copy-done.54) | copy-start | bytes 1572868
  373.0 53.3 %copy-start.89 = (f32[1,4,256]{2,0,1:T(1,128)S(1)}, f32[1,4,256]{2,0,1:T(1,128)}, u32[]{:S(2)}) copy-start(f32[1,4,256]{2,0,1:T(1,128)} %copy-done.88) | copy-start | bytes 12292
  430.3 6.6 copy-start.79
  430.3 7.3 copy-start.53
  430.3 7.3 copy-start.87
  436.9 7.9 copy-start.61
  437.6 41.4 %slice-start.8 = ((s8[8388608]{0:T(1024)(128)(4,1)}), s8[4194304]{0:T(1024)(128)(4,1)S(1)}, s32[]{:S(2)}) async-start(s8[8388608]{0:T(1024)(128)(4,1)} %bitcast.424), calls=%async_computation.9 | async-start | bytes 8388608
  446.3 13.3 %copy-start.60 = (f32[128,1024]{1,0:T(8,128)S(1)}, f32[128,1024]{1,0:T(8,128)}, u32[]{:S(2)}) copy-start(f32[128,1024]{1,0:T(8,128)} %copy-done.59) | copy-start | bytes 1572868
  446.3 13.3 %copy-start.98 = (f32[1,4,256]{2,0,1:T(1,128)S(1)}, f32[1,4,256]{2,0,1:T(1,128)}, u32[]{:S(2)}) copy-start(f32[1,4,256]{2,0,1:T(1,128)} %copy-done.97) | copy-start | bytes 12292
  446.3 13.3 %copy-start.125 = (f32[128]{0:T(128)S(1)}, f32[128]{0:T(128)}, u32[]{:S(2)}) copy-start(f32[128]{0:T(128)} %copy-done.124) | copy-start | bytes 1540
  446.3 13.3 %copy-start.127 = (f32[128]{0:T(128)S(1)}, f32[128]{0:T(128)}, u32[]{:S(2)}) copy-start(f32[128]{0:T(128)} %copy-done.126) | copy-start | bytes 1540
  446.3 32.7 %slice-start.9 = ((s8[8388608]{0:T(1024)(128)(4,1)}), s8[4194304]{0:T(1024)(128)(4,1)S(1)}, s32[]{:S(2)}) async-start(s8[8388608]{0:T(1024)(128)(4,1)} %bitcast.424), calls=%async_computation.10 | async-start | bytes 8388608
  448.9 33.7 %slice-start.10 = ((s8[6291456]{0:T(1024)(128)(4,1)}), s8[4194304]{0:T(1024)(128)(4,1)S(1)}, s32[]{:S(2)}) async-start(s8[6291456]{0:T(1024)(128)(4,1)} %bitcast.427), calls=%async_computation.11 | async-start | bytes 8388608
  459.5 19.5 %copy-start.28 = (bf16[384,1024]{1,0:T(8,128)(2,1)}, bf16[384,1024]{1,0:T(8,128)(2,1)S(1)}, u32[]{:S(2)}) copy-start(bf16[384,1024]{1,0:T(8,128)(2,1)S(1)} %get-tuple-element.56.refs_20_) | copy-start | bytes 2359300
  459.6 20.6 %copy-start.27 = (bf16[384,1024]{1,0:T(8,128)(2,1)}, bf16[384,1024]{1,0:T(8,128)(2,1)S(1)}, u32[]{:S(2)}) copy-start(bf16[384,1024]{1,0:T(8,128)(2,1)S(1)} %get-tuple-element.55.refs_19_) | copy-start | bytes 2359300
  463.9 15.2 %copy-start.81 = (bf16[128,1024]{1,0:T(8,128)(2,1)}, bf16[128,1024]{1,0:T(8,128)(2,1)S(1)}, u32[]{:S(2)}) copy-start(bf16[128,1024]{1,0:T(8,128)(2,1)S(1)} %convert_element_type.219.refs_15_) | copy-start | bytes 786436
  482.0 8.8 slice-start.2
  482.6 8.2 copy-start.64
  482.7 8.2 copy-start.46
  482.7 8.2 copy-start.94
  482.7 8.2 copy-start.100
  482.7 8.2 copy-start.105
  482.7 8.2 slice-start.3
  502.8 17.6 %copy-start.108 = (f32[1024]{0:T(1024)S(1)}, f32[1024]{0:T(1024)}, u32[]{:S(2)}) copy-start(f32[1024]{0:T(1024)} %get-tuple-element.84) | copy-start | bytes 12292
  502.8 17.6 %copy-start.110 = (f32[1024]{0:T(1024)S(1)}, f32[1024]{0:T(1024)}, u32[]{:S(2)}) copy-start(f32[1024]{0:T(1024)} %get-tuple-element.86) | copy-start | bytes 12292
  502.8 17.7 %copy-start.109 = (f32[1024]{0:T(1024)S(1)}, f32[1024]{0:T(1024)}, u32[]{:S(2)}) copy-start(f32[1024]{0:T(1024)} %get-tuple-element.92) | copy-start | bytes 12292
  502.8 17.7 %copy-start.112 = (f32[1024]{0:T(1024)S(1)}, f32[1024]{0:T(1024)}, u32[]{:S(2)}) copy-start(f32[1024]{0:T(1024)} %get-tuple-element.93) | copy-start | bytes 12292
  502.8 17.7 %copy-start.113 = (f32[1024]{0:T(1024)S(1)}, f32[1024]{0:T(1024)}, u32[]{:S(2)}) copy-start(f32[1024]{0:T(1024)} %get-tuple-element.94) | copy-start | bytes 12292
  502.8 17.7 %copy-start.114 = (f32[1024]{0:T(1024)S(1)}, f32[1024]{0:T(1024)}, u32[]{:S(2)}) copy-start(f32[1024]{0:T(1024)} %get-tuple-element.96) | copy-start | bytes 12292
  502.9 17.7 %copy-start.91 = (f32[4,4,256]{2,1,0:T(4,128)S(1)}, f32[4,4,256]{2,1,0:T(4,128)}, u32[]{:S(2)}) copy-start(f32[4,4,256]{2,1,0:T(4,128)} %reshape.436) | copy-start | bytes 49156
  521.5 377.5 %copy-start.32 = (bf16[384,1024]{1,0:T(8,128)(2,1)S(1)}, bf16[384,1024]{1,0:T(8,128)(2,1)}, u32[]{:S(2)}) copy-start(bf16[384,1024]{1,0:T(8,128)(2,1)} %copy-done.31) | copy-start | bytes 2359300
  898.9 12.6 %copy-start.44 = (bf16[28,256,1024]{2,1,0:T(8,128)(2,1)S(1)}, bf16[28,256,1024]{2,1,0:T(8,128)(2,1)}, u32[]{:S(2)}) copy-start(bf16[28,256,1024]{2,1,0:T(8,128)(2,1)} %get-tuple-element.70) | copy-start | bytes 44040196
  911.6 6.9 copy-start.17
  (80 other events, 222.7 us)
Sparse Core Ops, SparseCore 0:
  147.3 56.6 all-gather.1

commit v4 on v3

--- a/solution.py
+++ b/solution.py
@@ -16,6 +16,7 @@
 MESH = pl.DeviceIdType.MESH
 UNIT = 256
 RING = 8
+SIDE_STEPS = 16
 
 
 BIG_NEGATIVE = -1e30
@@ -193,11 +194,13 @@
     return jnp.where((value // mask) % 2 == 0, value + mask, value - mask)
 
 
-def sync_kernel(slots, count, plan, operands, small, out, small_out, scratch):
+def sync_kernel(slots, count, plan, operands, small, side, out, small_out, side_out, scratch):
     left_buffer, right_buffer, parts, core_in, far_out, far_keep, far_in = scratch[:7]
     half_out, half_keep, half_in, full = scratch[7:11]
     small_core, small_far, small_in, small_out_far, small_out_slot = scratch[11:16]
-    load_sem, store_sem, send_sem, recv_sem, small_send, small_recv = scratch[16:]
+    load_sem, store_sem, send_sem, recv_sem, small_send, small_recv = scratch[16:22]
+    if side:
+        side_left, side_right, side_total, side_sem, side_store = scratch[22:]
     masks = masks_below(slots)
     levels = len(masks)
     rows = full.shape[1]
@@ -424,8 +427,32 @@
 
     stages = 4 + 2 * levels
 
+    def side_loads(step):
+        pair = lax.rem(step, 2)
+        tokens = side_right.shape[1]
+        at = pl.ds(pl.multiple_of(step * tokens, tokens), tokens)
+        return (
+            pltpu.make_async_copy(side[0].at[:, at], side_left.at[pair], side_sem.at[0, pair]),
+            pltpu.make_async_copy(side[1].at[at], side_right.at[pair], side_sem.at[1, pair]),
+        )
+
+    def side_product(step):
+        pair = lax.rem(step, 2)
+        for copy in side_loads(step):
+            copy.wait()
+
+        @pl.loop(0, side_total.shape[0] // UNIT)
+        def _(i):
+            at = pl.ds(pl.multiple_of(i * UNIT, UNIT), UNIT)
+            side_total[at, :] += matmul(side_left[pair, at, :], side_right[pair])
+
     per = rows // UNIT
     load(jnp.int32(0))
+    if side:
+        side_total[...] = jnp.zeros_like(side_total)
+        side_copy = pltpu.make_async_copy(side_total, side_out, side_store)
+        for copy in side_loads(jnp.int32(0)):
+            copy.start()
 
     @pl.loop(0, count + stages)
     def _(it):
@@ -450,8 +477,26 @@
                 load(unit + 1)
                 product(unit, it, i * UNIT)
 
-
-def sync_gradients(plan, operands, small):
+        if side:
+
+            @pl.when(it < SIDE_STEPS - 1)
+            def _():
+                for copy in side_loads(it + 1):
+                    copy.start()
+
+            @pl.when(it < SIDE_STEPS)
+            def _():
+                side_product(it)
+
+            @pl.when(it == SIDE_STEPS)
+            def _():
+                side_copy.start()
+
+    if side:
+        side_copy.wait()
+
+
+def sync_gradients(plan, operands, small, side=()):
     slots = lax.axis_size("slot")
     rows, columns = max(UNIT, 16 * slots), D
     count = len(plan) * UNIT // rows
@@ -461,24 +506,48 @@
     longest = max(operand.shape[0] for operand in operands)
     block = lambda *lead: pltpu.VMEM(lead + (columns,), low)
     halves = [block(4, rows >> (i + 1)) for i in range(levels)]
-    used = len(operands)
+    used, more = len(operands), len(side)
+    outs = 3 if side else 2
+    shapes = [
+        jax.ShapeDtypeStruct((count, rows, columns), low),
+        jax.ShapeDtypeStruct(small_rows, jnp.float32),
+    ]
+    places = [pl.BlockSpec(memory_space=pl.ANY), pl.BlockSpec(memory_space=pltpu.VMEM)]
+    side_scratch = []
+    if side:
+        entries, tokens = side[0].shape
+        shapes.append(jax.ShapeDtypeStruct((entries, columns), jnp.float32))
+        places.append(pl.BlockSpec(memory_space=pl.ANY))
+        side_scratch = [
+            pltpu.VMEM((2, entries, tokens // SIDE_STEPS), low),
+            pltpu.VMEM((2, tokens // SIDE_STEPS, columns), low),
+            pltpu.VMEM((entries, columns), jnp.float32),
+            pltpu.SemaphoreType.DMA((2, 2)),
+            pltpu.SemaphoreType.DMA,
+        ]
 
     def kernel(*refs):
-        small_ref, out, small_out = refs[used : used + 3]
-        sync_kernel(slots, count, plan, refs[:used], small_ref, out, small_out, refs[used + 3 :])
+        ins, results = refs[: used + 1 + more], refs[used + 1 + more :]
+        sync_kernel(
+            slots,
+            count,
+            plan,
+            ins[:used],
+            ins[used],
+            ins[used + 1 :],
+            results[0],
+            results[1],
+            results[2] if side else None,
+            results[outs:],
+        )
 
     return pl.pallas_call(
         kernel,
-        out_shape=(
-            jax.ShapeDtypeStruct((count, rows, columns), low),
-            jax.ShapeDtypeStruct(small_rows, jnp.float32),
-        ),
+        out_shape=shapes,
         in_specs=[pl.BlockSpec(memory_space=pl.ANY)] * used
-        + [pl.BlockSpec(memory_space=pltpu.VMEM)],
-        out_specs=(
-            pl.BlockSpec(memory_space=pl.ANY),
-            pl.BlockSpec(memory_space=pltpu.VMEM),
-        ),
+        + [pl.BlockSpec(memory_space=pltpu.VMEM)]
+        + [pl.BlockSpec(memory_space=pl.ANY)] * more,
+        out_specs=places,
         scratch_shapes=[
             block(2, longest),
             block(2, longest),
@@ -502,11 +571,12 @@
             pltpu.SemaphoreType.DMA((3 + 2 * levels, RING)),
             pltpu.SemaphoreType.DMA((3 + levels,)),
             pltpu.SemaphoreType.DMA((3 + levels,)),
-        ],
+        ]
+        + side_scratch,
         compiler_params=pltpu.CompilerParams(
             collective_id=1, has_side_effects=True, vmem_limit_bytes=56 << 20
         ),
-    )(*operands, small)
+    )(*operands, small, *side)
 
 
 def code_bits():
@@ -1001,8 +1071,8 @@
     prior = jnp.exp(scores - own_norm)
     token_grad = (-posterior / count).reshape(tokens, 1)
     score_grads = -jnp.sum(posterior - prior[:, :, None], axis=2) / count
-    delta = to_low(
-        token_grad * (jnp.where(hit, 1.0, 0.0) - jnp.exp(logits - log_total[:, None]))
+    delta = lax.optimization_barrier(
+        to_low(token_grad * (jnp.where(hit, 1.0, 0.0) - jnp.exp(logits - log_total[:, None])))
     )
     grad_state = scatter_states(to_low(matmul(delta, embed)))
     return (losses[:1], score_grads[:1, :1], grad_state, delta, states)
@@ -1112,7 +1182,6 @@
         state_low, facts, targets.shape[1], embed
     )
 
-    embed_grad = matmul_tn(delta, states)
     grad_third, gain_third, shift_third = norm_backward(
         grad_state_sum, dec_norm_three, decoder_gain[2]
     )
@@ -1208,7 +1277,13 @@
     )
     spare = -starts[-1] % 32
     small = jnp.pad(vector_grads, ((0, 0), (0, spare), (0, 0))).reshape(pb_size, -1, D)
-    summed_parts, small_sum = sync_gradients(plan, operands, small)
+    if lax.axis_size("slot") * 16 <= UNIT:
+        summed_parts, small_sum, embed_grad = sync_gradients(
+            plan, operands, small, (delta.T, states)
+        )
+    else:
+        embed_grad = matmul_tn(delta, states)
+        summed_parts, small_sum = sync_gradients(plan, operands, small)
     units = summed_parts.reshape(-1, width, D)
     square = lambda at: units[at : at + 4].astype(jnp.float32)
     wide = lambda at: jnp.concatenate([units[at + i].astype(jnp.float32) for i in range(4)], axis=1)

time: 956 us -> 940 us (0.983)
  matrix products: 166 us -> 138 us
    dot_general x1 -> x0, matrix products: 21.4 us -> none  [matmul_tn(): lax.dot_general(left, right, (((0,), (0,)), ((), ())), preferred_element_...]
    convert_element_type x10 -> x11, other arithmetic: 2.84 us -> 13.9 us  [to_low(): return value.astype(jnp.bfloat16)]
    unnamed x289 -> x230, local copies, waits for them, and re-layouts: 23.5 us -> 26.3 us
where the time goes in v4:
time: 940 us; the launch traced here: 931 us
  Pallas kernels  678 us (72%)
  matrix products  138 us (15%)
  other arithmetic  54.5 us (6%)
  local copies, waits for them, and re-layouts  42.8 us (5%)
  between operations  18.1 us (2%)
    pallas_call x1, Pallas kernels, sync_gradients(): pl.pallas_call(kernel, out_shape=shapes, in_specs=[pl.BlockSpec(memory_sp...  376 us
    pallas_call x1, Pallas kernels, gather_weights(): pl.pallas_call(kernel, out_shape=[widened(shard) for shard in shards] + [...  120 us
    dot_general x17, matrix products, matmul_nt(): lax.dot_general(left, right, (((1,), (1,)), ((), ())), preferred_element_...  82.5 us
    pallas_call x1, Pallas kernels, gather_states(): pl.pallas_call(functools.partial(gather_kernel, bits, parts), out_shape=j...  55.8 us
    dot_general x17, matrix products, matmul(): return jnp.dot(left, right, preferred_element_type=jnp.float32)  55.1 us
    pallas_call x1, Pallas kernels, scatter_states(): pl.pallas_call(functools.partial(scatter_kernel, bits, parts), out_shape=...  54.5 us
    pallas_call x3, Pallas kernels, attend_backward(): pl.pallas_call(functools.partial(attend_grad_kernel, causal), grid=(HEADS...  34.3 us
    unnamed x230, local copies, waits for them, and re-layouts  26.3 us
  transfers between devices with their start and end apart: 1, of which 0 were waited for; matrix products, arithmetic and copies ran while one was open for 4% of the time, Pallas kernels for 2%

profile of v4, /device:TPU:0, one launch (start us, length us, event | category | flops | bytes accessed | tf_op | source)
XLA Modules:
  0.0 931.1 jit_solution(12878782256842531925)
XLA Ops:
  11.1 2.9 concatenate.26
  14.0 1.6 copy-done.8
  15.6 1.6 copy-done.9
  17.2 1.6 copy-done.10
  18.8 1.6 copy-done.11
  20.3 1.6 copy-done.12
  21.9 1.6 copy-done.13
  23.5 120.3 %shard_map.322 = (bf16[4,1024,1024]{2,1,0:T(8,128)(2,1)S(1)}, bf16[1024,4096]{1,0:T(8,128)(2,1)}, bf16[4096,1024]{1,0:T(8,128)(2,1)}, bf16[4,1024,1024]{2,1,0:T(...) custom-call(bf16[4,256,1024]{2,1,0:T(8,128)(2,1)S(1)} %copy-done.8, ...), custom_call_target="tpu_custom_call" | custom-call | tf_op jit(solution)/shard_map/pallas_call | solution.py:1004
  143.9 3.2 copy-done.35
  150.0 2.5 fusion.174.keys
  152.5 3.6 fusion.171.values
  156.1 2.5 fusion.168.queries
  158.6 6.6 shard_map.323.refs_14_
  166.3 1.0 fusion.107.values
  167.3 1.0 fusion.104.queries
  168.3 9.3 %shard_map.324.refs_4_ = bf16[384,1024]{1,0:T(8,128)(2,1)S(1)} custom-call(bf16[384,1024]{1,0:T(8,128)(2,1)S(1)} %fusion.104.queries, bf16[384,1024]{1,0:T(8,128)(2,1)S(1)} %fusion.110.keys, bf16[384,1024]{1,0:T(8,128)(2,1)S(1)} %fusion.107.values), custom_call_target="tpu_custom_call" | custom-call | flops 603979776 | bytes 6291456 | tf_op jit(solution)/shard_map/pallas_call | solution.py:137
  177.7 2.4 fusion.213
  180.3 1.1 fusion.214
  183.0 6.0 multiply_convert_fusion.1
  189.1 3.6 fusion.215
  194.4 1.0 fusion.100.keys
  195.4 1.0 add_convert_fusion.values
  196.4 7.3 shard_map.325.refs_21_
  205.4 6.4 multiply_convert_fusion.2
  211.9 5.3 fusion.217
  218.8 55.8 %shard_map.326 = bf16[2,2,2,2,2,128,1024]{6,5,4,3,2,1,0:T(8,128)(2,1)} custom-call(bf16[128,1024]{1,0:T(8,128)(2,1)} %add_convert_fusion.4.own), custom_call_target="tpu_custom_call" | custom-call | tf_op jit(solution)/shard_map/pallas_call | solution.py:659
  274.6 20.7 %fusion.218 = (f32[4096]{0:T(1024)S(1)}, f32[4096,1536]{0,1:T(8,128)}) fusion(bf16[4096,1024]{1,0:T(8,128)(2,1)} %bitcast.339, bf16[1536,1024]{1,0:T(8,128)(2,1)S(1)} %copy-done), kind=kOutput, calls=%fused_computation.277 | convolution fusion | flops 12891189248 | bytes 36716544 | tf_op jit(solution)/shard_map/dot_general | solution.py:31
  295.3 11.6 %exponential_reduce_fusion = (f32[4096]{0:T(1024)S(1)}, f32[4096]{0:T(1024)S(1)}) fusion(f32[4096,1536]{0,1:T(8,128)} %get-tuple-element.169, f32[4096]{0:T(1024)S(1)} %get-tuple-element.168, s32[4096]{0:T(1024)S(1)} %bitcast.347), kind=kLoop, calls=%fused_computation.3 | loop fusion | flops 31449088 | bytes 25231360 | tf_op jit(solution)/shard_map/reduce_sum | solution.py:1052
  307.5 13.8 %shard_map.327 = f32[3,32,128]{2,1,0:T(8,128)} custom-call(f32[3,32,128]{2,1,0:T(8,128)} %pad_maximum_fusion.stats), custom_call_target="tpu_custom_call" | custom-call | tf_op jit(solution)/shard_map/pallas_call | solution.py:822
  323.5 11.8 %multiply_convert_fusion = bf16[4096,1536]{0,1:T(8,128)(2,1)S(1)} fusion(f32[4096,1536]{0,1:T(8,128)} %get-tuple-element.169, f32[4096]{0:T(1024)S(1)} %get-tuple-element.107, f32[4096]{0:T(1024)S(1)} %get-tuple-element.106, s32[4096]{0:T(1024)S(1)} %bitcast.348), kind=kLoop, calls=%fused_computation | loop fusion | flops 37748736 | bytes 37797888 | tf_op jit(solution)/shard_map/convert_element_type | solution.py:43
  335.3 15.8 %convolution_convert_fusion = bf16[4096,1024]{1,0:T(8,128)(2,1)} fusion(bf16[4096,1536]{0,1:T(8,128)(2,1)S(1)} %multiply_convert_fusion, bf16[1536,1024]{1,0:T(8,128)(2,1)S(1)} %copy-done), kind=kOutput, calls=%fused_computation.5 | convolution fusion | flops 12889096192 | bytes 24117248 | tf_op jit(solution)/shard_map/dot_general | solution.py:27
  351.2 54.5 %shard_map.328 = f32[128,1024]{1,0:T(8,128)} custom-call(bf16[2,2,2,2,2,128,1024]{6,5,4,3,2,1,0:T(8,128)(2,1)} %bitcast.341), custom_call_target="tpu_custom_call" | custom-call | tf_op jit(solution)/shard_map/pallas_call | solution.py:765
  405.7 1.5 multiply_reduce_fusion.8
  407.2 1.2 fusion.199
  408.5 6.6 fusion.207
  415.2 6.8 multiply_reduce_fusion.9
  422.4 2.6 fusion.156.upstream
  425.0 10.8 %shard_map.329 = (bf16[128,1024]{1,0:T(8,128)(2,1)S(1)}, bf16[384,1024]{1,0:T(8,128)(2,1)S(1)}, bf16[384,1024]{1,0:T(8,128)(2,1)S(1)}, f32[8,1024]{1,0:T(8,128)S(1)}, f32[8,1024]{1,0:T(8,128)S(1)}) custom-call(bf16[128,1024]{1,0:T(8,128)(2,1)S(1)} %copy-done.27, bf16[384,1024]{1,0:T(8,128)(2,1)S(1)} %copy-done.3, bf16[384,1024]{1,0:T(8,128)(2,1)S(1)} %copy-done.5, ...), custom_call_target="tpu_custom_call" | custom-call | flops 503316480 | bytes 10485760 | tf_op jit(solution)/shard_map/pallas_call | solution.py:156
  435.9 3.2 multiply_reduce_fusion.10
  440.2 2.5 fusion.153.upstream
  442.7 8.9 shard_map.331
  451.7 3.5 fusion.45
  455.2 1.0 fusion.13
  456.6 1.5 multiply_reduce_fusion
  458.8 8.3 fusion.206
  467.1 5.0 multiply_reduce_fusion.1
  472.2 1.9 fusion.203
  474.1 1.1 copy-done.52
  476.2 2.8 fusion.97.upstream
  479.0 14.6 %shard_map.330 = (bf16[384,1024]{1,0:T(8,128)(2,1)S(1)}, bf16[384,1024]{1,0:T(8,128)(2,1)S(1)}, bf16[384,1024]{1,0:T(8,128)(2,1)S(1)}, f32[8,1024]{1,0:T(8,128)S(1)}, f32[8,1024]{1,0:T(8,128)S(1)}) custom-call(bf16[384,1024]{1,0:T(8,128)(2,1)S(1)} %copy-done.44, bf16[384,1024]{1,0:T(8,128)(2,1)S(1)} %copy-done.40, bf16[384,1024]{1,0:T(8,128)(2,1)S(1)} %copy-done.42, ...), custom_call_target="tpu_custom_call" | custom-call | flops 1509949440 | bytes 15728640 | tf_op jit(solution)/shard_map/pallas_call | solution.py:156
  497.4 376.0 %shard_map.332 = (bf16[28,256,1024]{2,1,0:T(8,128)(2,1)}, f32[8,1024]{1,0:T(8,128)}, f32[1536,1024]{1,0:T(8,128)}) custom-call(bf16[384,1024]{1,0:T(8,128)(2,1)} %bitcast.344, bf16[384,1024]{1,0:T(8,128)(2,1)} %copy-done.6, bf16[384,1024]{1,0:T(8,128)(2,1)} %copy-done.31, bf16[384,1024]{1,0:T(8,128)(2,1)} %copy-done.33, bf16[384,1024]{1,0:T(8,128)(2,1)} %copy-done.28, ...), custom_call_target="tpu_custom_call" | custom-call | tf_op jit(solution)/shard_map/pallas_call | solution.py:544
  873.4 1.4 fusion.209
  878.0 3.9 fusion.25
  881.9 4.5 fusion.29
  886.4 4.2 slice_bitcast_fusion.3
  890.7 5.8 fusion.205
  897.8 2.5 fusion.125
  900.4 3.2 fusion.122
  903.6 2.6 bitcast_convert_fusion
  906.2 2.7 bitcast_convert_fusion.1
  910.3 4.0 add_bitcast_fusion
  914.4 2.6 maximum_convert_fusion.1
  917.1 2.5 maximum_convert_fusion
  919.6 3.2 copy.114
  (342 shorter events, 29.4 us)
Async XLA Ops:
  7.2 267.4 %copy-start = (bf16[1536,1024]{1,0:T(8,128)(2,1)S(1)}, bf16[1536,1024]{1,0:T(8,128)(2,1)}, u32[]{:S(2)}) copy-start(bf16[1536,1024]{1,0:T(8,128)(2,1)} %param.37) | copy-start | bytes 9437188
  7.2 198.2 %all-gather.2.cloned.1.call-start = ((), (), s32[]{:S(2)}) async-start(), calls=%async_computation | async-start | bytes 10485760 | tf_op jit(solution)/shard_map/all_gather | solution.py:1128
  149.9 15.3 %copy-start.36 = (bf16[4,1024,1024]{2,1,0:T(8,128)(2,1)S(1)}, bf16[4,1024,1024]{2,1,0:T(8,128)(2,1)}, u32[]{:S(2)}) copy-start(bf16[4,1024,1024]{2,1,0:T(8,128)(2,1)} %copy-done.35) | copy-start | bytes 25165828
  152.4 6.1 copy-start.20
  156.1 9.1 copy-start.22
  156.1 9.2 copy-start.88
  158.6 7.6 copy-start.24
  165.2 12.5 %copy-start.14 = (bf16[128,1024]{1,0:T(8,128)(2,1)}, bf16[128,1024]{1,0:T(8,128)(2,1)S(1)}, u32[]{:S(2)}) copy-start(bf16[128,1024]{1,0:T(8,128)(2,1)S(1)} %shard_map.323.refs_14_) | copy-start | bytes 786436
  168.3 9.3 %copy-start.43 = (bf16[384,1024]{1,0:T(8,128)(2,1)}, bf16[384,1024]{1,0:T(8,128)(2,1)S(1)}, u32[]{:S(2)}) copy-start(bf16[384,1024]{1,0:T(8,128)(2,1)S(1)} %fusion.104.queries) | copy-start | bytes 2359300
  177.6 3.8 copy-start.28
  177.6 4.5 slice-start.2
  180.1 23.7 %copy-start.62 = (f32[128,1024]{1,0:T(8,128)}, f32[128,1024]{1,0:T(8,128)S(1)}, u32[]{:S(2)}) copy-start(f32[128,1024]{1,0:T(8,128)S(1)} %get-tuple-element.155) | copy-start | bytes 1572868
  180.1 23.6 %copy-start.93 = (f32[128]{0:T(128)}, f32[128]{0:T(128)S(1)}, u32[]{:S(2)}) copy-start(f32[128]{0:T(128)S(1)} %broadcast_multiply_fusion.14) | copy-start | bytes 1540
  181.4 7.7 copy-start.48
  181.8 7.3 slice-start.6
  182.1 7.0 copy-start.68
  183.0 6.1 slice-start.7
  189.1 3.7 copy-start.66
  189.1 4.8 slice-start.8
  189.1 4.8 slice-start.9
  193.1 10.7 %copy-start.95 = (f32[128]{0:T(128)}, f32[128]{0:T(128)S(1)}, u32[]{:S(2)}) copy-start(f32[128]{0:T(128)S(1)} %add_rsqrt_fusion.4) | copy-start | bytes 1540
  196.4 8.0 copy-start.4
  205.4 6.5 copy-start.65
  205.4 6.4 copy-start.55
  211.8 5.3 copy-start.46
  335.3 15.8 %copy-start.45 = (bf16[4096,1536]{0,1:T(8,128)(2,1)}, bf16[4096,1536]{0,1:T(8,128)(2,1)S(1)}, u32[]{:S(2)}) copy-start(bf16[4096,1536]{0,1:T(8,128)(2,1)S(1)} %multiply_convert_fusion) | copy-start | bytes 37748740
  351.2 54.5 %copy-start.58 = (f32[128,1024]{1,0:T(8,128)S(1)}, f32[128,1024]{1,0:T(8,128)}, u32[]{:S(2)}) copy-start(f32[128,1024]{1,0:T(8,128)} %copy-done.57) | copy-start | bytes 1572868
  408.5 6.6 copy-start.83
  408.5 6.6 copy-start.56
  415.1 6.9 copy-start.64
  415.2 40.0 %slice-start.10 = ((s8[8388608]{0:T(1024)(128)(4,1)}), s8[4194304]{0:T(1024)(128)(4,1)S(1)}, s32[]{:S(2)}) async-start(s8[8388608]{0:T(1024)(128)(4,1)} %bitcast.427), calls=%async_computation.11 | async-start | bytes 8388608
  422.3 13.5 %copy-start.84 = (bf16[128,1024]{1,0:T(8,128)(2,1)}, bf16[128,1024]{1,0:T(8,128)(2,1)S(1)}, u32[]{:S(2)}) copy-start(bf16[128,1024]{1,0:T(8,128)(2,1)S(1)} %convert_element_type.213.refs_22_) | copy-start | bytes 786436
  422.3 13.5 %copy-start.63 = (f32[128,1024]{1,0:T(8,128)S(1)}, f32[128,1024]{1,0:T(8,128)}, u32[]{:S(2)}) copy-start(f32[128,1024]{1,0:T(8,128)} %copy-done.62) | copy-start | bytes 1572868
  422.3 13.5 %copy-start.94 = (f32[128]{0:T(128)S(1)}, f32[128]{0:T(128)}, u32[]{:S(2)}) copy-start(f32[128]{0:T(128)} %copy-done.93) | copy-start | bytes 1540
  422.3 13.5 %copy-start.96 = (f32[128]{0:T(128)S(1)}, f32[128]{0:T(128)}, u32[]{:S(2)}) copy-start(f32[128]{0:T(128)} %copy-done.95) | copy-start | bytes 1540
  422.4 32.8 %slice-start.11 = ((s8[8388608]{0:T(1024)(128)(4,1)}), s8[4194304]{0:T(1024)(128)(4,1)S(1)}, s32[]{:S(2)}) async-start(s8[8388608]{0:T(1024)(128)(4,1)} %bitcast.427), calls=%async_computation.12 | async-start | bytes 8388608
  435.8 19.3 %copy-start.30 = (bf16[384,1024]{1,0:T(8,128)(2,1)}, bf16[384,1024]{1,0:T(8,128)(2,1)S(1)}, u32[]{:S(2)}) copy-start(bf16[384,1024]{1,0:T(8,128)(2,1)S(1)} %get-tuple-element.57.refs_20_) | copy-start | bytes 2359300
  435.8 20.4 %copy-start.29 = (bf16[384,1024]{1,0:T(8,128)(2,1)}, bf16[384,1024]{1,0:T(8,128)(2,1)S(1)}, u32[]{:S(2)}) copy-start(bf16[384,1024]{1,0:T(8,128)(2,1)S(1)} %get-tuple-element.56.refs_19_) | copy-start | bytes 2359300
  440.2 14.9 %copy-start.85 = (bf16[128,1024]{1,0:T(8,128)(2,1)}, bf16[128,1024]{1,0:T(8,128)(2,1)S(1)}, u32[]{:S(2)}) copy-start(bf16[128,1024]{1,0:T(8,128)(2,1)S(1)} %convert_element_type.219.refs_15_) | copy-start | bytes 786436
  451.6 4.6 copy-start.16
  451.6 4.6 copy-start.18
  451.6 4.6 copy-start.38
  458.1 9.0 slice-start.4
  458.7 8.3 copy-start.70
  458.8 8.3 copy-start.49
  458.8 8.3 slice-start.5
  467.1 5.0 copy-start.67
  497.4 380.6 %copy-start.34 = (bf16[384,1024]{1,0:T(8,128)(2,1)S(1)}, bf16[384,1024]{1,0:T(8,128)(2,1)}, u32[]{:S(2)}) copy-start(bf16[384,1024]{1,0:T(8,128)(2,1)} %copy-done.33) | copy-start | bytes 2359300
  878.0 3.9 copy-start.32
  878.0 12.6 %copy-start.47 = (bf16[28,256,1024]{2,1,0:T(8,128)(2,1)S(1)}, bf16[28,256,1024]{2,1,0:T(8,128)(2,1)}, u32[]{:S(2)}) copy-start(bf16[28,256,1024]{2,1,0:T(8,128)(2,1)} %get-tuple-element.71) | copy-start | bytes 44040196
  890.6 6.4 copy-start.87
  890.6 6.4 copy-start.92
  890.6 6.4 copy-start.97
  890.6 7.2 copy-start.17
  896.5 3.8 copy-start.19
  896.5 3.8 copy-start.61
  906.2 4.1 copy-start.82
  910.3 4.0 copy-start.77
  910.3 4.0 copy-start.78
  910.3 4.0 copy-start.79
  910.3 4.0 copy-start.80
  910.3 9.2 slice-start
  914.4 5.2 slice-start.1
  919.6 4.2 copy-start.1
  (50 other events, 101.3 us)
Sparse Core Ops, SparseCore 0:
  147.3 56.5 all-gather.1

commit v5 on v4

--- a/solution.py
+++ b/solution.py
@@ -432,7 +432,7 @@
         tokens = side_right.shape[1]
         at = pl.ds(pl.multiple_of(step * tokens, tokens), tokens)
         return (
-            pltpu.make_async_copy(side[0].at[:, at], side_left.at[pair], side_sem.at[0, pair]),
+            pltpu.make_async_copy(side[0].at[at], side_left.at[pair], side_sem.at[0, pair]),
             pltpu.make_async_copy(side[1].at[at], side_right.at[pair], side_sem.at[1, pair]),
         )
 
@@ -444,7 +444,7 @@
         @pl.loop(0, side_total.shape[0] // UNIT)
         def _(i):
             at = pl.ds(pl.multiple_of(i * UNIT, UNIT), UNIT)
-            side_total[at, :] += matmul(side_left[pair, at, :], side_right[pair])
+            side_total[at, :] += matmul_tn(side_left[pair, :, at], side_right[pair])
 
     per = rows // UNIT
     load(jnp.int32(0))
@@ -515,11 +515,11 @@
     places = [pl.BlockSpec(memory_space=pl.ANY), pl.BlockSpec(memory_space=pltpu.VMEM)]
     side_scratch = []
     if side:
-        entries, tokens = side[0].shape
+        tokens, entries = side[0].shape
         shapes.append(jax.ShapeDtypeStruct((entries, columns), jnp.float32))
         places.append(pl.BlockSpec(memory_space=pl.ANY))
         side_scratch = [
-            pltpu.VMEM((2, entries, tokens // SIDE_STEPS), low),
+            pltpu.VMEM((2, tokens // SIDE_STEPS, entries), low),
             pltpu.VMEM((2, tokens // SIDE_STEPS, columns), low),
             pltpu.VMEM((entries, columns), jnp.float32),
             pltpu.SemaphoreType.DMA((2, 2)),
@@ -1037,21 +1037,62 @@
     return jnp.pad(jnp.concatenate(facts).reshape(1, 2, TGT_LEN), ((0, 0), (0, 6), (0, 0)))
 
 
+def logit_kernel(states, embed, facts, logits_out, stats):
+    logits = matmul_nt(states[...], embed[...])
+    logits_out[...] = logits
+    target = facts[...].T[:, 0:1]
+    entry = lax.broadcasted_iota(jnp.int32, logits.shape, 1).astype(jnp.float32)
+    top = jnp.max(logits, axis=1, keepdims=True)
+    total = jnp.sum(jnp.exp(logits - top), axis=1, keepdims=True)
+    pick = jnp.sum(jnp.where(entry == target, logits, 0.0), axis=1, keepdims=True)
+    lane = lax.broadcasted_iota(jnp.int32, (logits.shape[0], 128), 1)
+    stats[...] = jnp.where(lane == 0, top, jnp.where(lane == 1, total, pick)).T[:8]
+
+
+def delta_kernel(logits, embed, facts, delta_out, grad_state):
+    columns = facts[...].T
+    target, weight, log_total = columns[:, 0:1], columns[:, 1:2], columns[:, 2:3]
+    entry = lax.broadcasted_iota(jnp.int32, logits.shape, 1).astype(jnp.float32)
+    onehot = jnp.where(entry == target, 1.0, 0.0)
+    delta = to_low(weight * (onehot - jnp.exp(logits[...] - log_total)))
+    delta_out[...] = delta
+    grad_state[...] = to_low(matmul(delta, embed[...]))
+
+
+def token_tiles(kernel, left, embed, facts, outs):
+    tokens, tile = left.shape[0], 512
+    tall = lambda width: pl.BlockSpec((tile, width), lambda i: (i, 0))
+    wide = pl.BlockSpec((8, tile), lambda i: (0, i))
+    return pl.pallas_call(
+        kernel,
+        grid=(tokens // tile,),
+        out_shape=outs,
+        in_specs=[tall(left.shape[1]), pl.BlockSpec(embed.shape, lambda i: (0, 0)), wide],
+        out_specs=[wide if out.shape[0] == 8 else tall(out.shape[1]) for out in outs],
+        compiler_params=pltpu.CompilerParams(vmem_limit_bytes=48 << 20),
+    )(left, embed, facts)
+
+
 def vocabulary_head(state_low, facts, questions, embed):
     slots, groups = lax.axis_size("slot"), lax.axis_size("pb")
     me = lax.axis_index("slot") * groups + lax.axis_index("pb")
     entries = embed.shape[0]
     tokens = slots * groups * TGT_LEN
-    target_ids = facts[:, 0].astype(jnp.int32).reshape(tokens, 1)
+    target_ids = (facts[:, 0] - (me * entries).astype(jnp.float32)).reshape(1, tokens)
     owners = facts[:, 1, 0].astype(jnp.int32).reshape(slots, groups)
     scores = facts[:, 1, TGT_LEN // 2].reshape(slots, groups)
     states = gather_states(state_low)
-    logits = matmul_nt(states, embed)
-    hit = target_ids - me * entries == lax.broadcasted_iota(jnp.int32, (tokens, entries), 1)
-    top = jnp.max(logits, axis=1)
-    total = jnp.sum(jnp.exp(logits - top[:, None]), axis=1)
-    pick = jnp.sum(jnp.where(hit, logits, 0.0), axis=1)
-    merged = merge_stats(jnp.stack([top, total, pick]).reshape(3, -1, TGT_LEN))
+    logits, stats = token_tiles(
+        logit_kernel,
+        states,
+        embed,
+        jnp.pad(target_ids, ((0, 7), (0, 0))),
+        [
+            jax.ShapeDtypeStruct((tokens, entries), jnp.float32),
+            jax.ShapeDtypeStruct((8, tokens), jnp.float32),
+        ],
+    )
+    merged = merge_stats(stats[:3].reshape(3, -1, TGT_LEN))
     log_total = (merged[0] + jnp.log(merged[1])).reshape(tokens)
     picked = merged[2].reshape(slots, groups, TGT_LEN) - log_total.reshape(slots, groups, TGT_LEN)
     serving = owners[:, :, None] == jnp.arange(questions)
@@ -1069,12 +1110,20 @@
     own_norm = jnp.sum(jnp.where(serving, score_norm[None], 0.0), axis=2)
     posterior = jnp.exp(scores[:, :, None] + picked - own_mix)
     prior = jnp.exp(scores - own_norm)
-    token_grad = (-posterior / count).reshape(tokens, 1)
+    token_grad = (-posterior / count).reshape(1, tokens)
     score_grads = -jnp.sum(posterior - prior[:, :, None], axis=2) / count
-    delta = lax.optimization_barrier(
-        to_low(token_grad * (jnp.where(hit, 1.0, 0.0) - jnp.exp(logits - log_total[:, None])))
-    )
-    grad_state = scatter_states(to_low(matmul(delta, embed)))
+    known = jnp.concatenate([target_ids, token_grad, log_total.reshape(1, tokens)])
+    delta, share = token_tiles(
+        delta_kernel,
+        logits,
+        embed,
+        jnp.pad(known, ((0, 5), (0, 0))),
+        [
+            jax.ShapeDtypeStruct((tokens, entries), jnp.bfloat16),
+            jax.ShapeDtypeStruct((tokens, D), jnp.bfloat16),
+        ],
+    )
+    grad_state = scatter_states(share)
     return (losses[:1], score_grads[:1, :1], grad_state, delta, states)
 
 
@@ -1279,7 +1328,7 @@
     small = jnp.pad(vector_grads, ((0, 0), (0, spare), (0, 0))).reshape(pb_size, -1, D)
     if lax.axis_size("slot") * 16 <= UNIT:
         summed_parts, small_sum, embed_grad = sync_gradients(
-            plan, operands, small, (delta.T, states)
+            plan, operands, small, (delta, states)
         )
     else:
         embed_grad = matmul_tn(delta, states)

time: 940 us -> 920 us (0.979)
  Pallas kernels: 678 us -> 723 us
  matrix products: 138 us -> 101 us
  other arithmetic: 54.5 us -> 30.3 us
    pallas_call x0 -> x2, Pallas kernels: none -> 44.3 us  [token_tiles(): pl.pallas_call(kernel, grid=(tokens // tile,), out_shape=outs, in_specs=[...]
    dot_general x17 -> x16, matrix products: 82.5 us -> 62.1 us  [matmul_nt(): lax.dot_general(left, right, (((1,), (1,)), ((), ())), preferred_element_...]
    dot_general x17 -> x16, matrix products: 55.1 us -> 38.9 us  [matmul(): return jnp.dot(left, right, preferred_element_type=jnp.float32)]
    convert_element_type x11 -> x10, other arithmetic: 13.9 us -> 2.15 us  [to_low(): return value.astype(jnp.bfloat16)]
    reduce_sum x1 -> x0, other arithmetic: 11.6 us -> none  [vocabulary_head(): total = jnp.sum(jnp.exp(logits - top[:, None]), axis=1)]
    unnamed x230 -> x268, local copies, waits for them, and re-layouts: 26.3 us -> 22.7 us
  transfers between devices with their start and end apart: 1 -> 1, of which waited for: 0 -> 0; matrix products, arithmetic and copies ran while one was open for 4% -> 4% of each run, Pallas kernels for 2% -> 3%
where the time goes in v5:
time: 920 us; the launch traced here: 911 us
  Pallas kernels  723 us (79%)
  matrix products  101 us (11%)
  local copies, waits for them, and re-layouts  39.7 us (4%)
  other arithmetic  30.3 us (3%)
  between operations  17.8 us (2%)
    pallas_call x1, Pallas kernels, sync_gradients(): pl.pallas_call(kernel, out_shape=shapes, in_specs=[pl.BlockSpec(memory_sp...  375 us
    pallas_call x1, Pallas kernels, gather_weights(): pl.pallas_call(kernel, out_shape=[widened(shard) for shard in shards] + [...  120 us
    dot_general x16, matrix products, matmul_nt(): lax.dot_general(left, right, (((1,), (1,)), ((), ())), preferred_element_...  62.1 us
    pallas_call x1, Pallas kernels, gather_states(): pl.pallas_call(functools.partial(gather_kernel, bits, parts), out_shape=j...  55.6 us
    pallas_call x1, Pallas kernels, scatter_states(): pl.pallas_call(functools.partial(scatter_kernel, bits, parts), out_shape=...  53.6 us
    pallas_call x2, Pallas kernels, token_tiles(): pl.pallas_call(kernel, grid=(tokens // tile,), out_shape=outs, in_specs=[...  44.3 us
    dot_general x16, matrix products, matmul(): return jnp.dot(left, right, preferred_element_type=jnp.float32)  38.9 us
    pallas_call x3, Pallas kernels, attend_backward(): pl.pallas_call(functools.partial(attend_grad_kernel, causal), grid=(HEADS...  34.5 us
  transfers between devices with their start and end apart: 1, of which 0 were waited for; matrix products, arithmetic and copies ran while one was open for 4% of the time, Pallas kernels for 3%

profile of v5, /device:TPU:0, one launch (start us, length us, event | category | flops | bytes accessed | tf_op | source)
XLA Modules:
  0.0 911.4 jit_solution(7557599847645937775)
XLA Ops:
  10.8 2.9 concatenate.28
  13.7 1.6 copy-done.7
  15.3 1.6 copy-done.8
  16.9 1.6 copy-done.9
  18.5 1.6 copy-done.10
  20.1 1.6 copy-done.11
  21.6 1.6 copy-done.12
  23.2 120.3 %shard_map.322 = (bf16[4,1024,1024]{2,1,0:T(8,128)(2,1)S(1)}, bf16[1024,4096]{1,0:T(8,128)(2,1)}, bf16[4096,1024]{1,0:T(8,128)(2,1)}, bf16[4,1024,1024]{2,1,0:T(...) custom-call(bf16[4,256,1024]{2,1,0:T(8,128)(2,1)S(1)} %copy-done.7, ...), custom_call_target="tpu_custom_call" | custom-call | tf_op jit(solution)/shard_map/pallas_call | solution.py:1004
  143.6 3.3 copy-done.34
  150.4 2.5 fusion.174.keys
  152.9 3.6 fusion.171.values
  156.4 2.3 fusion.168.queries
  158.8 6.6 shard_map.323.refs_14_
  165.5 1.0 fusion.110.keys
  166.5 1.0 fusion.107.values
  167.5 1.0 fusion.104.queries
  168.5 9.3 %shard_map.324.refs_4_ = bf16[384,1024]{1,0:T(8,128)(2,1)S(1)} custom-call(bf16[384,1024]{1,0:T(8,128)(2,1)S(1)} %fusion.104.queries, bf16[384,1024]{1,0:T(8,128)(2,1)S(1)} %fusion.110.keys, bf16[384,1024]{1,0:T(8,128)(2,1)S(1)} %fusion.107.values), custom_call_target="tpu_custom_call" | custom-call | flops 603979776 | bytes 6291456 | tf_op jit(solution)/shard_map/pallas_call | solution.py:137
  177.9 2.4 fusion.206
  180.5 1.1 fusion.207
  183.1 5.9 multiply_convert_fusion
  189.1 3.6 fusion.208
  194.3 1.0 fusion.100.keys
  195.3 1.0 add_convert_fusion.values
  196.4 7.3 shard_map.325.refs_21_
  205.4 6.4 multiply_convert_fusion.1
  211.8 5.2 fusion.210
  218.8 55.6 %shard_map.326 = bf16[2,2,2,2,2,128,1024]{6,5,4,3,2,1,0:T(8,128)(2,1)} custom-call(bf16[128,1024]{1,0:T(8,128)(2,1)} %add_convert_fusion.4.own), custom_call_target="tpu_custom_call" | custom-call | tf_op jit(solution)/shard_map/pallas_call | solution.py:659
  274.4 22.9 %shard_map.327 = (f32[4096,1536]{1,0:T(8,128)}, f32[8,4096]{1,0:T(8,128)S(1)}) custom-call(bf16[4096,1024]{1,0:T(8,128)(2,1)} %bitcast.323, bf16[1536,1024]{1,0:T(8,128)(2,1)S(1)} %copy-done, f32[8,4096]{1,0:T(8,128)S(1)} %pad.22.facts), custom_call_target="tpu_custom_call" | custom-call | tf_op jit(solution)/shard_map/pallas_call | solution.py:1066
  297.9 15.8 %shard_map.328 = f32[3,32,128]{2,1,0:T(8,128)} custom-call(f32[3,32,128]{2,1,0:T(8,128)} %bitcast.331), custom_call_target="tpu_custom_call" | custom-call | tf_op jit(solution)/shard_map/pallas_call | solution.py:822
  315.3 21.5 %shard_map.329 = (bf16[4096,1536]{1,0:T(8,128)(2,1)}, bf16[4096,1024]{1,0:T(8,128)(2,1)}) custom-call(f32[4096,1536]{1,0:T(8,128)} %get-tuple-element.61.logits, bf16[1536,1024]{1,0:T(8,128)(2,1)S(1)} %copy-done, f32[8,4096]{1,0:T(8,128)S(1)} %select_maximum_fusion.facts), custom_call_target="tpu_custom_call" | custom-call | tf_op jit(solution)/shard_map/pallas_call | solution.py:1066
  336.7 53.6 %shard_map.330 = f32[128,1024]{1,0:T(8,128)} custom-call(bf16[2,2,2,2,2,128,1024]{6,5,4,3,2,1,0:T(8,128)(2,1)} %bitcast.325), custom_call_target="tpu_custom_call" | custom-call | tf_op jit(solution)/shard_map/pallas_call | solution.py:765
  390.4 1.5 multiply_reduce_fusion.8
  391.8 1.2 fusion.193
  393.2 6.6 fusion.200
  399.9 6.8 multiply_reduce_fusion.9
  407.0 2.6 fusion.156.upstream
  409.7 11.0 %shard_map.331 = (bf16[128,1024]{1,0:T(8,128)(2,1)S(1)}, bf16[384,1024]{1,0:T(8,128)(2,1)S(1)}, bf16[384,1024]{1,0:T(8,128)(2,1)S(1)}, f32[8,1024]{1,0:T(8,128)S(1)}, f32[8,1024]{1,0:T(8,128)S(1)}) custom-call(bf16[128,1024]{1,0:T(8,128)(2,1)S(1)} %copy-done.26, bf16[384,1024]{1,0:T(8,128)(2,1)S(1)} %copy-done.2, bf16[384,1024]{1,0:T(8,128)(2,1)S(1)} %copy-done.4, ...), custom_call_target="tpu_custom_call" | custom-call | flops 503316480 | bytes 10485760 | tf_op jit(solution)/shard_map/pallas_call | solution.py:156
  420.8 3.2 multiply_reduce_fusion.10
  425.0 2.5 fusion.153.upstream
  427.6 8.9 shard_map.333
  436.5 3.5 fusion.45
  440.1 1.0 fusion.13
  441.4 1.5 multiply_reduce_fusion
  443.7 8.2 fusion.199
  452.0 5.0 multiply_reduce_fusion.1
  457.0 1.9 fusion.197
  459.1 2.9 fusion.97.upstream
  462.0 14.6 %shard_map.332 = (bf16[384,1024]{1,0:T(8,128)(2,1)S(1)}, bf16[384,1024]{1,0:T(8,128)(2,1)S(1)}, bf16[384,1024]{1,0:T(8,128)(2,1)S(1)}, f32[8,1024]{1,0:T(8,128)S(1)}, f32[8,1024]{1,0:T(8,128)S(1)}) custom-call(bf16[384,1024]{1,0:T(8,128)(2,1)S(1)} %copy-done.43, bf16[384,1024]{1,0:T(8,128)(2,1)S(1)} %copy-done.39, bf16[384,1024]{1,0:T(8,128)(2,1)S(1)} %copy-done.41, ...), custom_call_target="tpu_custom_call" | custom-call | flops 1509949440 | bytes 15728640 | tf_op jit(solution)/shard_map/pallas_call | solution.py:156
  477.5 0.9 copy-done.30
  478.4 0.9 copy-done.32
  480.4 375.3 %shard_map.334 = (bf16[28,256,1024]{2,1,0:T(8,128)(2,1)}, f32[8,1024]{1,0:T(8,128)}, f32[1536,1024]{1,0:T(8,128)}) custom-call(bf16[384,1024]{1,0:T(8,128)(2,1)} %bitcast.328, bf16[384,1024]{1,0:T(8,128)(2,1)} %copy-done.5, bf16[384,1024]{1,0:T(8,128)(2,1)} %copy-done.30, bf16[384,1024]{1,0:T(8,128)(2,1)} %copy-done.32, bf16[384,1024]{1,0:T(8,128)(2,1)} %copy-done.27, ...), custom_call_target="tpu_custom_call" | custom-call | tf_op jit(solution)/shard_map/pallas_call | solution.py:544
  855.7 1.4 fusion.202
  860.3 3.9 fusion.25
  864.1 4.5 fusion.29
  868.7 4.0 slice_bitcast_fusion.3
  872.7 6.4 fusion.198
  880.4 2.5 fusion.125
  882.9 3.4 fusion.122
  886.3 2.6 bitcast_convert_fusion
  888.9 2.7 bitcast_convert_fusion.1
  892.5 4.0 add_bitcast_fusion
  896.6 2.6 maximum_convert_fusion.1
  899.1 2.5 maximum_convert_fusion
  901.7 2.7 copy.97
  (379 shorter events, 24.1 us)
Async XLA Ops:
  7.2 198.2 %all-gather.2.cloned.1.call-start = ((), (), s32[]{:S(2)}) async-start(), calls=%async_computation | async-start | bytes 10485760 | tf_op jit(solution)/shard_map/all_gather | solution.py:1177
  147.4 57.2 %copy-start.110 = (f32[32]{0:T(128)}, f32[32]{0:T(128)S(1)}, u32[]{:S(2)}) copy-start(f32[32]{0:T(128)S(1)} %slice_reduce_fusion) | copy-start | bytes 388
  148.3 8.1 copy-start.88
  150.4 15.1 %copy-start.35 = (bf16[4,1024,1024]{2,1,0:T(8,128)(2,1)S(1)}, bf16[4,1024,1024]{2,1,0:T(8,128)(2,1)}, u32[]{:S(2)}) copy-start(bf16[4,1024,1024]{2,1,0:T(8,128)(2,1)} %copy-done.34) | copy-start | bytes 25165828
  152.8 5.9 copy-start.19
  156.4 9.0 copy-start.21
  156.4 9.0 copy-start.82
  158.8 7.6 copy-start.23
  165.4 12.5 %copy-start.13 = (bf16[128,1024]{1,0:T(8,128)(2,1)}, bf16[128,1024]{1,0:T(8,128)(2,1)S(1)}, u32[]{:S(2)}) copy-start(bf16[128,1024]{1,0:T(8,128)(2,1)S(1)} %shard_map.323.refs_14_) | copy-start | bytes 786436
  168.5 9.3 %copy-start.42 = (bf16[384,1024]{1,0:T(8,128)(2,1)}, bf16[384,1024]{1,0:T(8,128)(2,1)S(1)}, u32[]{:S(2)}) copy-start(bf16[384,1024]{1,0:T(8,128)(2,1)S(1)} %fusion.104.queries) | copy-start | bytes 2359300
  180.3 23.4 %copy-start.58 = (f32[128,1024]{1,0:T(8,128)}, f32[128,1024]{1,0:T(8,128)S(1)}, u32[]{:S(2)}) copy-start(f32[128,1024]{1,0:T(8,128)S(1)} %get-tuple-element.162) | copy-start | bytes 1572868
  180.3 23.4 %copy-start.112 = (f32[128]{0:T(128)}, f32[128]{0:T(128)S(1)}, u32[]{:S(2)}) copy-start(f32[128]{0:T(128)S(1)} %broadcast_multiply_fusion.14) | copy-start | bytes 1540
  181.6 7.4 copy-start.46
  181.7 7.4 copy-start.96
  182.0 7.1 copy-start.101
  182.0 7.0 copy-start.90
  182.0 11.3 %copy-start.92 = (f32[1,4,256]{2,0,1:T(1,128)}, f32[1,4,256]{2,0,1:T(1,128)S(1)}, u32[]{:S(2)}) copy-start(f32[1,4,256]{2,0,1:T(1,128)S(1)} %get-tuple-element.159) | copy-start | bytes 12292
  182.0 7.0 slice-start.6
  182.4 6.6 copy-start.64
  183.1 6.0 slice-start.7
  193.0 10.7 %copy-start.114 = (f32[128]{0:T(128)}, f32[128]{0:T(128)S(1)}, u32[]{:S(2)}) copy-start(f32[128]{0:T(128)S(1)} %add_rsqrt_fusion.4) | copy-start | bytes 1540
  193.1 10.6 %copy-start.94 = (f32[1,4,256]{2,0,1:T(1,128)}, f32[1,4,256]{2,0,1:T(1,128)S(1)}, u32[]{:S(2)}) copy-start(f32[1,4,256]{2,0,1:T(1,128)S(1)} %get-tuple-element.158) | copy-start | bytes 12292
  193.1 18.7 %copy-start.84 = (f32[1,4,256]{2,0,1:T(1,128)}, f32[1,4,256]{2,0,1:T(1,128)S(1)}, u32[]{:S(2)}) copy-start(f32[1,4,256]{2,0,1:T(1,128)S(1)} %get-tuple-element.157) | copy-start | bytes 12292
  193.1 24.2 %copy-start.86 = (f32[1,4,256]{2,0,1:T(1,128)}, f32[1,4,256]{2,0,1:T(1,128)S(1)}, u32[]{:S(2)}) copy-start(f32[1,4,256]{2,0,1:T(1,128)S(1)} %get-tuple-element.156) | copy-start | bytes 12292
  196.4 8.0 copy-start.3
  204.3 7.5 copy-start.50
  204.4 7.5 copy-start.105
  204.6 7.2 copy-start.107
  205.4 6.4 copy-start.61
  218.7 55.6 %copy-start = (bf16[1536,1024]{1,0:T(8,128)(2,1)S(1)}, bf16[1536,1024]{1,0:T(8,128)(2,1)}, u32[]{:S(2)}) copy-start(bf16[1536,1024]{1,0:T(8,128)(2,1)} %embed.3) | copy-start | bytes 9437188
  274.4 40.1 %copy-start.89 = (f32[8,4]{1,0:T(8,128)S(1)}, f32[8,4]{1,0:T(8,128)}, u32[]{:S(2)}) copy-start(f32[8,4]{1,0:T(8,128)} %copy-done.88) | copy-start | bytes 388
  274.4 40.2 %copy-start.100 = (pred[8,4,2]{0,2,1:T(4,128)(4,1)S(1)}, pred[8,4,2]{0,2,1:T(4,128)(4,1)}, u32[]{:S(2)}) copy-start(pred[8,4,2]{0,2,1:T(4,128)(4,1)} %copy.62) | copy-start | bytes 196
  274.4 40.4 %copy-start.109 = (f32[4,2]{1,0:T(4,128)S(1)}, f32[4,2]{1,0:T(4,128)}, u32[]{:S(2)}) copy-start(f32[4,2]{1,0:T(4,128)} %copy.71) | copy-start | bytes 100
  336.7 53.6 %copy-start.53 = (f32[128,1024]{1,0:T(8,128)S(1)}, f32[128,1024]{1,0:T(8,128)}, u32[]{:S(2)}) copy-start(f32[128,1024]{1,0:T(8,128)} %copy-done.52) | copy-start | bytes 1572868
  336.7 53.6 %copy-start.87 = (f32[1,4,256]{2,0,1:T(1,128)S(1)}, f32[1,4,256]{2,0,1:T(1,128)}, u32[]{:S(2)}) copy-start(f32[1,4,256]{2,0,1:T(1,128)} %copy-done.86) | copy-start | bytes 12292
  393.1 6.7 copy-start.78
  393.1 6.7 copy-start.51
  393.1 6.7 copy-start.85
  393.2 6.7 copy-start.106
  393.2 6.7 copy-start.108
  399.8 6.9 copy-start.60
  399.9 40.1 %slice-start.10 = ((s8[8388608]{0:T(1024)(128)(4,1)}), s8[4194304]{0:T(1024)(128)(4,1)S(1)}, s32[]{:S(2)}) async-start(s8[8388608]{0:T(1024)(128)(4,1)} %bitcast.410), calls=%async_computation.11 | async-start | bytes 8388608
  407.0 13.7 %copy-start.79 = (bf16[128,1024]{1,0:T(8,128)(2,1)}, bf16[128,1024]{1,0:T(8,128)(2,1)S(1)}, u32[]{:S(2)}) copy-start(bf16[128,1024]{1,0:T(8,128)(2,1)S(1)} %convert_element_type.203.refs_22_) | copy-start | bytes 786436
  407.0 13.7 %copy-start.59 = (f32[128,1024]{1,0:T(8,128)S(1)}, f32[128,1024]{1,0:T(8,128)}, u32[]{:S(2)}) copy-start(f32[128,1024]{1,0:T(8,128)} %copy-done.58) | copy-start | bytes 1572868
  407.0 13.7 %copy-start.95 = (f32[1,4,256]{2,0,1:T(1,128)S(1)}, f32[1,4,256]{2,0,1:T(1,128)}, u32[]{:S(2)}) copy-start(f32[1,4,256]{2,0,1:T(1,128)} %copy-done.94) | copy-start | bytes 12292
  407.0 13.7 %copy-start.113 = (f32[128]{0:T(128)S(1)}, f32[128]{0:T(128)}, u32[]{:S(2)}) copy-start(f32[128]{0:T(128)} %copy-done.112) | copy-start | bytes 1540
  407.0 13.7 %copy-start.115 = (f32[128]{0:T(128)S(1)}, f32[128]{0:T(128)}, u32[]{:S(2)}) copy-start(f32[128]{0:T(128)} %copy-done.114) | copy-start | bytes 1540
  407.0 33.0 %slice-start.11 = ((s8[8388608]{0:T(1024)(128)(4,1)}), s8[4194304]{0:T(1024)(128)(4,1)S(1)}, s32[]{:S(2)}) async-start(s8[8388608]{0:T(1024)(128)(4,1)} %bitcast.410), calls=%async_computation.12 | async-start | bytes 8388608
  420.7 19.3 %copy-start.29 = (bf16[384,1024]{1,0:T(8,128)(2,1)}, bf16[384,1024]{1,0:T(8,128)(2,1)S(1)}, u32[]{:S(2)}) copy-start(bf16[384,1024]{1,0:T(8,128)(2,1)S(1)} %get-tuple-element.64.refs_20_) | copy-start | bytes 2359300
  420.7 20.5 %copy-start.28 = (bf16[384,1024]{1,0:T(8,128)(2,1)}, bf16[384,1024]{1,0:T(8,128)(2,1)S(1)}, u32[]{:S(2)}) copy-start(bf16[384,1024]{1,0:T(8,128)(2,1)S(1)} %get-tuple-element.63.refs_19_) | copy-start | bytes 2359300
  425.0 15.0 %copy-start.80 = (bf16[128,1024]{1,0:T(8,128)(2,1)}, bf16[128,1024]{1,0:T(8,128)(2,1)S(1)}, u32[]{:S(2)}) copy-start(bf16[128,1024]{1,0:T(8,128)(2,1)S(1)} %convert_element_type.209.refs_15_) | copy-start | bytes 786436
  442.9 8.9 slice-start.4
  443.6 8.3 copy-start.66
  443.6 8.3 copy-start.47
  443.6 8.3 copy-start.91
  443.6 8.3 copy-start.97
  443.6 8.3 copy-start.102
  443.7 8.3 slice-start.5
  480.4 379.9 %copy-start.33 = (bf16[384,1024]{1,0:T(8,128)(2,1)S(1)}, bf16[384,1024]{1,0:T(8,128)(2,1)}, u32[]{:S(2)}) copy-start(bf16[384,1024]{1,0:T(8,128)(2,1)} %copy-done.32) | copy-start | bytes 2359300
  860.2 12.4 %copy-start.45 = (bf16[28,256,1024]{2,1,0:T(8,128)(2,1)S(1)}, bf16[28,256,1024]{2,1,0:T(8,128)(2,1)}, u32[]{:S(2)}) copy-start(bf16[28,256,1024]{2,1,0:T(8,128)(2,1)} %get-tuple-element.79) | copy-start | bytes 44040196
  872.7 6.9 copy-start.111
  872.7 6.9 copy-start.116
  872.7 7.7 copy-start.16
  892.5 9.2 %slice-start = ((s8[6291456]{0:T(1024)(128)(4,1)}), s8[4194304]{0:T(1024)(128)(4,1)S(1)}, s32[]{:S(2)}) async-start(s8[6291456]{0:T(1024)(128)(4,1)} %bitcast.326), calls=%async_computation.1 | async-start | bytes 8388608
  (68 other events, 185.1 us)
Sparse Core Ops, SparseCore 0:
  147.0 56.5 all-gather.1

commit v6 on v5

--- a/solution.py
+++ b/solution.py
@@ -1020,7 +1020,7 @@
             pltpu.SemaphoreType.DMA((bits + 3,)),
         ],
         compiler_params=pltpu.CompilerParams(
-            collective_id=5, has_side_effects=True, vmem_limit_bytes=32 << 20
+            collective_id=5, has_side_effects=True, vmem_limit_bytes=58 << 20
         ),
     )(*shards, vector, fact)
 

time: 920 us -> 909 us (0.988)
  local copies, waits for them, and re-layouts: 39.7 us -> 27.8 us
    unnamed x268 -> x190, local copies, waits for them, and re-layouts: 22.7 us -> 9.78 us
where the time goes in v6:
time: 909 us; the launch traced here: 901 us
  Pallas kernels  722 us (79%)
  matrix products  101 us (11%)
  other arithmetic  31.5 us (3%)
  local copies, waits for them, and re-layouts  27.8 us (3%)
  between operations  17.3 us (2%)
    pallas_call x1, Pallas kernels, sync_gradients(): pl.pallas_call(kernel, out_shape=shapes, in_specs=[pl.BlockSpec(memory_sp...  375 us
    pallas_call x1, Pallas kernels, gather_weights(): pl.pallas_call(kernel, out_shape=[widened(shard) for shard in shards] + [...  121 us
    dot_general x16, matrix products, matmul_nt(): lax.dot_general(left, right, (((1,), (1,)), ((), ())), preferred_element_...  62.1 us
    pallas_call x1, Pallas kernels, scatter_states(): pl.pallas_call(functools.partial(scatter_kernel, bits, parts), out_shape=...  53 us
    pallas_call x1, Pallas kernels, gather_states(): pl.pallas_call(functools.partial(gather_kernel, bits, parts), out_shape=j...  52.7 us
    pallas_call x2, Pallas kernels, token_tiles(): pl.pallas_call(kernel, grid=(tokens // tile,), out_shape=outs, in_specs=[...  44.3 us
    dot_general x16, matrix products, matmul(): return jnp.dot(left, right, preferred_element_type=jnp.float32)  39.4 us
    pallas_call x3, Pallas kernels, attend_backward(): pl.pallas_call(functools.partial(attend_grad_kernel, causal), grid=(HEADS...  34.5 us
  transfers between devices with their start and end apart: 1, of which 0 were waited for; matrix products, arithmetic and copies ran while one was open for 4% of the time, Pallas kernels for 3%

profile of v6, /device:TPU:0, one launch (start us, length us, event | category | flops | bytes accessed | tf_op | source)
XLA Modules:
  0.0 900.6 jit_solution(11243965261225697272)
XLA Ops:
  11.4 2.9 concatenate.28
  14.9 121.5 %shard_map.322 = (bf16[4,1024,1024]{2,1,0:T(8,128)(2,1)}, bf16[1024,4096]{1,0:T(8,128)(2,1)}, bf16[4096,1024]{1,0:T(8,128)(2,1)}, bf16[4,1024,1024]{2,1,0:T(8,12...) custom-call(bf16[4,256,1024]{2,1,0:T(8,128)(2,1)} %refs_0_.1, ...), custom_call_target="tpu_custom_call" | custom-call | tf_op jit(solution)/shard_map/pallas_call | solution.py:1004
  136.4 1.4 slice_reduce_fusion
  137.8 1.6 convert_reduce_fusion
  140.4 0.9 subtract_bitcast_fusion
  141.5 2.5 fusion.174.keys
  144.0 3.8 fusion.171.values
  147.9 2.2 fusion.168.queries
  150.0 6.6 shard_map.323.refs_14_
  156.7 1.0 fusion.110.keys
  157.7 1.0 fusion.107.values
  158.7 1.0 fusion.104.queries
  159.8 9.3 %shard_map.324.refs_4_ = bf16[384,1024]{1,0:T(8,128)(2,1)S(1)} custom-call(bf16[384,1024]{1,0:T(8,128)(2,1)S(1)} %fusion.104.queries, bf16[384,1024]{1,0:T(8,128)(2,1)S(1)} %fusion.110.keys, bf16[384,1024]{1,0:T(8,128)(2,1)S(1)} %fusion.107.values), custom_call_target="tpu_custom_call" | custom-call | flops 603979776 | bytes 6291456 | tf_op jit(solution)/shard_map/pallas_call | solution.py:137
  169.1 2.5 fusion.206
  171.9 1.1 fusion.207
  174.4 6.0 multiply_convert_fusion
  180.4 3.7 fusion.208
  185.8 1.0 fusion.100.keys
  186.8 1.0 add_convert_fusion.values
  187.8 7.3 shard_map.325.refs_21_
  196.3 6.4 multiply_convert_fusion.1
  202.7 5.2 fusion.210
  208.7 0.9 add_convert_fusion.4.own
  209.6 52.7 %shard_map.326 = bf16[2,2,2,2,2,128,1024]{6,5,4,3,2,1,0:T(8,128)(2,1)} custom-call(bf16[128,1024]{1,0:T(8,128)(2,1)} %add_convert_fusion.4.own), custom_call_target="tpu_custom_call" | custom-call | tf_op jit(solution)/shard_map/pallas_call | solution.py:659
  262.3 22.8 %shard_map.327 = (f32[4096,1536]{1,0:T(8,128)}, f32[8,4096]{1,0:T(8,128)S(1)}) custom-call(bf16[4096,1024]{1,0:T(8,128)(2,1)} %bitcast.323, bf16[1536,1024]{1,0:T(8,128)(2,1)S(1)} %copy-done, f32[8,4096]{1,0:T(8,128)S(1)} %pad.22.facts), custom_call_target="tpu_custom_call" | custom-call | tf_op jit(solution)/shard_map/pallas_call | solution.py:1066
  285.7 18.7 %shard_map.328 = f32[3,32,128]{2,1,0:T(8,128)} custom-call(f32[3,32,128]{2,1,0:T(8,128)} %bitcast.331), custom_call_target="tpu_custom_call" | custom-call | tf_op jit(solution)/shard_map/pallas_call | solution.py:822
  306.0 21.5 %shard_map.329 = (bf16[4096,1536]{1,0:T(8,128)(2,1)}, bf16[4096,1024]{1,0:T(8,128)(2,1)}) custom-call(f32[4096,1536]{1,0:T(8,128)} %get-tuple-element.61.logits, bf16[1536,1024]{1,0:T(8,128)(2,1)S(1)} %copy-done, f32[8,4096]{1,0:T(8,128)S(1)} %select_maximum_fusion.facts), custom_call_target="tpu_custom_call" | custom-call | tf_op jit(solution)/shard_map/pallas_call | solution.py:1066
  327.4 53.0 %shard_map.330 = f32[128,1024]{1,0:T(8,128)} custom-call(bf16[2,2,2,2,2,128,1024]{6,5,4,3,2,1,0:T(8,128)(2,1)} %bitcast.325), custom_call_target="tpu_custom_call" | custom-call | tf_op jit(solution)/shard_map/pallas_call | solution.py:765
  380.4 1.5 multiply_reduce_fusion.8
  381.9 1.2 fusion.193
  383.2 6.6 fusion.200
  389.8 6.8 multiply_reduce_fusion.9
  397.0 2.6 fusion.156.upstream
  399.6 11.0 %shard_map.331 = (bf16[128,1024]{1,0:T(8,128)(2,1)S(1)}, bf16[384,1024]{1,0:T(8,128)(2,1)S(1)}, bf16[384,1024]{1,0:T(8,128)(2,1)S(1)}, f32[8,1024]{1,0:T(8,128)S(1)}, f32[8,1024]{1,0:T(8,128)S(1)}) custom-call(bf16[128,1024]{1,0:T(8,128)(2,1)S(1)} %copy-done.20, bf16[384,1024]{1,0:T(8,128)(2,1)S(1)} %copy-done.2, bf16[384,1024]{1,0:T(8,128)(2,1)S(1)} %copy-done.4, ...), custom_call_target="tpu_custom_call" | custom-call | flops 503316480 | bytes 10485760 | tf_op jit(solution)/shard_map/pallas_call | solution.py:156
  410.7 3.2 multiply_reduce_fusion.10
  414.9 2.5 fusion.153.upstream
  417.5 8.9 shard_map.333
  426.4 3.5 fusion.45
  429.9 1.0 fusion.13
  431.3 1.5 multiply_reduce_fusion
  433.5 8.2 fusion.199
  441.7 5.0 multiply_reduce_fusion.1
  446.8 1.9 fusion.197
  448.9 2.9 fusion.97.upstream
  451.8 14.6 %shard_map.332 = (bf16[384,1024]{1,0:T(8,128)(2,1)S(1)}, bf16[384,1024]{1,0:T(8,128)(2,1)S(1)}, bf16[384,1024]{1,0:T(8,128)(2,1)S(1)}, f32[8,1024]{1,0:T(8,128)S(1)}, f32[8,1024]{1,0:T(8,128)S(1)}) custom-call(bf16[384,1024]{1,0:T(8,128)(2,1)S(1)} %copy-done.35, bf16[384,1024]{1,0:T(8,128)(2,1)S(1)} %copy-done.31, bf16[384,1024]{1,0:T(8,128)(2,1)S(1)} %copy-done.33, ...), custom_call_target="tpu_custom_call" | custom-call | flops 1509949440 | bytes 15728640 | tf_op jit(solution)/shard_map/pallas_call | solution.py:156
  466.5 0.9 copy-done.5
  467.3 0.9 copy-done.24
  468.2 0.9 copy-done.26
  470.2 374.6 %shard_map.334 = (bf16[28,256,1024]{2,1,0:T(8,128)(2,1)}, f32[8,1024]{1,0:T(8,128)}, f32[1536,1024]{1,0:T(8,128)}) custom-call(bf16[384,1024]{1,0:T(8,128)(2,1)} %bitcast.328, bf16[384,1024]{1,0:T(8,128)(2,1)} %copy-done.5, bf16[384,1024]{1,0:T(8,128)(2,1)} %copy-done.24, bf16[384,1024]{1,0:T(8,128)(2,1)} %copy-done.26, bf16[384,1024]{1,0:T(8,128)(2,1)} %copy-done.21, ...), custom_call_target="tpu_custom_call" | custom-call | tf_op jit(solution)/shard_map/pallas_call | solution.py:544
  844.8 1.4 fusion.202
  846.2 0.8 reshape.470
  849.4 3.9 fusion.25
  853.3 4.5 fusion.29
  857.8 4.0 slice_bitcast_fusion.3
  861.8 6.4 fusion.198
  869.5 2.5 fusion.125
  872.1 3.4 fusion.122
  875.4 2.6 bitcast_convert_fusion
  878.1 2.7 bitcast_convert_fusion.1
  880.8 0.8 copy-done.69
  881.6 4.0 add_bitcast_fusion
  885.7 2.6 maximum_convert_fusion.1
  888.3 2.5 maximum_convert_fusion
  890.8 2.7 copy.97
  (301 shorter events, 19.0 us)
Async XLA Ops:
  7.2 189.1 %all-gather.2.cloned.1.call-start = ((), (), s32[]{:S(2)}) async-start(), calls=%async_computation | async-start | bytes 10485760 | tf_op jit(solution)/shard_map/all_gather | solution.py:1177
  136.4 4.0 copy-start.77
  136.4 5.1 copy-start.76
  141.5 15.2 %copy-start.75 = (bf16[4,1024,1024]{2,1,0:T(8,128)(2,1)S(1)}, bf16[4,1024,1024]{2,1,0:T(8,128)(2,1)}, u32[]{:S(2)}) copy-start(bf16[4,1024,1024]{2,1,0:T(8,128)(2,1)} %get-tuple-element.55) | copy-start | bytes 25165828
  144.0 6.0 copy-start.13
  147.8 8.8 copy-start.15
  147.8 8.8 copy-start.74
  150.0 7.7 copy-start.17
  156.6 12.5 %copy-start.7 = (bf16[128,1024]{1,0:T(8,128)(2,1)}, bf16[128,1024]{1,0:T(8,128)(2,1)S(1)}, u32[]{:S(2)}) copy-start(bf16[128,1024]{1,0:T(8,128)(2,1)S(1)} %shard_map.323.refs_14_) | copy-start | bytes 786436
  159.8 9.3 %copy-start.34 = (bf16[384,1024]{1,0:T(8,128)(2,1)}, bf16[384,1024]{1,0:T(8,128)(2,1)S(1)}, u32[]{:S(2)}) copy-start(bf16[384,1024]{1,0:T(8,128)(2,1)S(1)} %fusion.104.queries) | copy-start | bytes 2359300
  169.1 3.9 copy-start.21
  169.1 4.6 slice-start.2
  171.7 23.5 %copy-start.50 = (f32[128,1024]{1,0:T(8,128)}, f32[128,1024]{1,0:T(8,128)S(1)}, u32[]{:S(2)}) copy-start(f32[128,1024]{1,0:T(8,128)S(1)} %get-tuple-element.162) | copy-start | bytes 1572868
  173.0 7.4 copy-start.38
  173.4 7.0 slice-start.6
  173.7 6.6 copy-start.56
  174.3 6.0 slice-start.7
  180.3 3.7 copy-start.54
  180.3 5.0 slice-start.8
  180.4 4.9 slice-start.9
  187.8 8.0 copy-start.3
  195.8 6.9 copy-start.42
  196.2 6.4 copy-start.53
  202.7 5.3 copy-start.36
  209.6 52.7 %copy-start = (bf16[1536,1024]{1,0:T(8,128)(2,1)S(1)}, bf16[1536,1024]{1,0:T(8,128)(2,1)}, u32[]{:S(2)}) copy-start(bf16[1536,1024]{1,0:T(8,128)(2,1)} %embed.3) | copy-start | bytes 9437188
  327.4 53.0 %copy-start.45 = (f32[128,1024]{1,0:T(8,128)S(1)}, f32[128,1024]{1,0:T(8,128)}, u32[]{:S(2)}) copy-start(f32[128,1024]{1,0:T(8,128)} %copy-done.44) | copy-start | bytes 1572868
  383.2 6.6 copy-start.70
  383.2 6.6 copy-start.43
  389.8 6.9 copy-start.52
  389.8 40.0 %slice-start.10 = ((s8[8388608]{0:T(1024)(128)(4,1)}), s8[4194304]{0:T(1024)(128)(4,1)S(1)}, s32[]{:S(2)}) async-start(s8[8388608]{0:T(1024)(128)(4,1)} %bitcast.410), calls=%async_computation.11 | async-start | bytes 8388608
  397.0 13.6 %copy-start.71 = (bf16[128,1024]{1,0:T(8,128)(2,1)}, bf16[128,1024]{1,0:T(8,128)(2,1)S(1)}, u32[]{:S(2)}) copy-start(bf16[128,1024]{1,0:T(8,128)(2,1)S(1)} %convert_element_type.203.refs_22_) | copy-start | bytes 786436
  397.0 13.7 %copy-start.51 = (f32[128,1024]{1,0:T(8,128)S(1)}, f32[128,1024]{1,0:T(8,128)}, u32[]{:S(2)}) copy-start(f32[128,1024]{1,0:T(8,128)} %copy-done.50) | copy-start | bytes 1572868
  397.0 32.9 %slice-start.11 = ((s8[8388608]{0:T(1024)(128)(4,1)}), s8[4194304]{0:T(1024)(128)(4,1)S(1)}, s32[]{:S(2)}) async-start(s8[8388608]{0:T(1024)(128)(4,1)} %bitcast.410), calls=%async_computation.12 | async-start | bytes 8388608
  410.6 3.3 copy-start.28
  410.6 19.2 %copy-start.23 = (bf16[384,1024]{1,0:T(8,128)(2,1)}, bf16[384,1024]{1,0:T(8,128)(2,1)S(1)}, u32[]{:S(2)}) copy-start(bf16[384,1024]{1,0:T(8,128)(2,1)S(1)} %get-tuple-element.64.refs_20_) | copy-start | bytes 2359300
  410.6 20.3 %copy-start.22 = (bf16[384,1024]{1,0:T(8,128)(2,1)}, bf16[384,1024]{1,0:T(8,128)(2,1)S(1)}, u32[]{:S(2)}) copy-start(bf16[384,1024]{1,0:T(8,128)(2,1)S(1)} %get-tuple-element.63.refs_19_) | copy-start | bytes 2359300
  414.1 3.3 copy-start.14
  414.2 3.3 copy-start.16
  414.2 3.3 copy-start.18
  414.9 15.0 %copy-start.72 = (bf16[128,1024]{1,0:T(8,128)(2,1)}, bf16[128,1024]{1,0:T(8,128)(2,1)S(1)}, u32[]{:S(2)}) copy-start(bf16[128,1024]{1,0:T(8,128)(2,1)S(1)} %convert_element_type.209.refs_15_) | copy-start | bytes 786436
  426.3 4.6 copy-start.9
  426.4 4.6 copy-start.11
  426.4 4.6 copy-start.29
  429.9 3.5 slice-start.12
  432.8 8.9 slice-start.4
  433.4 8.3 copy-start.58
  433.5 8.2 copy-start.39
  433.5 8.2 slice-start.5
  441.7 5.1 copy-start.55
  448.8 3.0 copy-start.59
  470.2 379.2 %copy-start.27 = (bf16[384,1024]{1,0:T(8,128)(2,1)S(1)}, bf16[384,1024]{1,0:T(8,128)(2,1)}, u32[]{:S(2)}) copy-start(bf16[384,1024]{1,0:T(8,128)(2,1)} %copy-done.26) | copy-start | bytes 2359300
  849.4 3.9 copy-start.25
  849.4 12.5 %copy-start.37 = (bf16[28,256,1024]{2,1,0:T(8,128)(2,1)S(1)}, bf16[28,256,1024]{2,1,0:T(8,128)(2,1)}, u32[]{:S(2)}) copy-start(bf16[28,256,1024]{2,1,0:T(8,128)(2,1)} %get-tuple-element.79) | copy-start | bytes 44040196
  861.8 7.7 copy-start.10
  868.2 3.8 copy-start.12
  868.2 3.8 copy-start.49
  872.0 3.4 copy-start.47
  878.1 3.5 copy-start.69
  881.6 4.0 copy-start.64
  881.6 4.0 copy-start.65
  881.6 4.0 copy-start.66
  881.6 4.0 copy-start.67
  881.6 9.2 %slice-start = ((s8[6291456]{0:T(1024)(128)(4,1)}), s8[4194304]{0:T(1024)(128)(4,1)S(1)}, s32[]{:S(2)}) async-start(s8[6291456]{0:T(1024)(128)(4,1)} %bitcast.326), calls=%async_computation.1 | async-start | bytes 8388608
  885.7 5.1 slice-start.1
  (29 other events, 56.2 us)
Sparse Core Ops, SparseCore 0:
  136.5 56.6 all-gather.1
